TPU v7x, 32 devices: a whole 2x2x4 slice. The times are simulated.
32 devices in a mesh: dp: 4 (over y, x), tensor: 8 (over z, core).
Axes of the slice: x: 2, y: 2, z: 4, core: 2. Of those that a mesh axis runs over, the one named last changes fastest.
Arguments:
- tokens: bfloat16 [1024, 2048], P(('dp', 'tensor')), may hold values from -6 to 6
- attn_gain: bfloat16 [2048], replicated, may hold values from 0.099609375 to 1.8984375
- mlp_gain: bfloat16 [2048], replicated, may hold values from 0.099609375 to 1.8984375
- project_in: bfloat16 [3, 2048, 2048], P(None, None, 'tensor'), may hold values from -6 to 6
- project_out: bfloat16 [2048, 2048], P('tensor'), may hold values from -0.125 to 0.125
- gate_up: bfloat16 [2, 2048, 8192], P(None, None, 'tensor'), may hold values from -0.125 to 0.125
- project_down: bfloat16 [8192, 2048], P('tensor'), may hold values from -0.0625 to 0.0625
- kv_cache: bfloat16 [2, 16384, 2048], P(None, 'dp', 'tensor'), may hold values from -10 to 10
- lengths: int32 [1024], replicated, may hold values from 1 to 1024, as said below
- owners: int32 [1024], replicated, may hold values from 0 to 3, as said below
- cache_start: int32 [1024], replicated, may hold values from 0 to 4094, as said below
Outputs:
- hidden_states: bfloat16 [1024, 2048], P(('dp', 'tensor'))
- log_sum_exp: float32 [1024, 32], P('dp', 'tensor')
- kv_updated: bfloat16 [2, 16384, 2048], P(None, 'dp', 'tensor')
Inputs may be any that keep to these rules, and one draw needn't show every extreme that they name: `lengths`: the largest length is exactly 1024 in every draw. `owners`: in each aligned block of 256 requests (those of one dp index) exactly 128 requests name another owner than the block's index and the rest name the block's index; no other owner is named by more than 43 requests of one block, and in every block one owner is named by exactly 43. The requests of one owner occupy disjoint ranges of positions from cache_start to cache_start + length, the last of these (the position for the new token) included, all within that owner's 4096 positions.
All inputs are finite; a program needn't handle non-finite values.
Results may differ from a plain program's by a relative error of at most 0.008.
Values may be sent and summed in bfloat16 or wider, within the bound.
No kernel may reach another device: no remote copies, remote signals or barrier semaphores. Data moves between devices by JAX's collectives and lax.ppermute only.
A program may use at most 64 MiB of HBM per device.

v0:
```python
import math

import jax
import jax.numpy as jnp
from jax import lax
from jax.sharding import PartitionSpec as P

MOST = 4
HD = 64


NORM_EPS = 1e-05
ROPE_BASE = 130000.0
MASK_LOW = -1e30


def scaled_norm(values, scales):
    wide = values.astype(jnp.float32)
    factor = lax.rsqrt(jnp.mean(wide * wide, axis=-1, keepdims=True) + NORM_EPS)
    return (wide * factor * scales.astype(jnp.float32)).astype(jnp.bfloat16)


def rotate(values, positions, head_size):
    half_size = head_size // 2
    freqs = ROPE_BASE ** (-(jnp.arange(half_size, dtype=jnp.float32) * 2.0 / head_size))
    angles = positions.astype(jnp.float32)[:, None] * freqs[None, :]
    cosine = jnp.cos(angles)[:, None, :]
    sine = jnp.sin(angles)[:, None, :]
    first = values[..., :half_size]
    second = values[..., half_size:]
    return jnp.concatenate(
        [first * cosine - second * sine, second * cosine + first * sine], axis=-1
    )


def expand_hidden(normed_rows, gate_up):
    both = jnp.einsum("rd,cdf->rcf", normed_rows, gate_up, preferred_element_type=jnp.float32)
    return (jax.nn.silu(both[:, 0]) * both[:, 1]).astype(jnp.bfloat16)


def partials(kv_cache, queries, starts, seg_spans, head_size):
    query_count = queries.shape[0]
    feat_width = queries.shape[1]
    heads_local = feat_width // head_size
    cache_rows = kv_cache.shape[1]
    block_rows = min(512, cache_rows)
    ends = jnp.where(seg_spans > 0, starts + seg_spans, 0)
    block_count = (jnp.max(ends) + block_rows - 1) // block_rows
    query_heads = queries.reshape(query_count, heads_local, head_size)
    scale = 1.0 / math.sqrt(head_size)
    finish = starts + seg_spans

    def advance(step_index, carry):
        running_top, running_sum, running_out = carry
        first_row = step_index * block_rows
        window = lax.dynamic_slice_in_dim(kv_cache, first_row, block_rows, 1)
        key_block = window[0].reshape(block_rows, heads_local, head_size)
        value_block = window[1].reshape(block_rows, heads_local, head_size).astype(jnp.float32)
        scores = (
            jnp.einsum("qhe,phe->qhp", query_heads, key_block, preferred_element_type=jnp.float32)
            * scale
        )
        position = first_row + jnp.arange(block_rows)
        live = (position[None, :] >= starts[:, None]) & (position[None, :] < finish[:, None])
        live = live[:, None, :]
        masked = jnp.where(live, scores, MASK_LOW)
        new_top = jnp.maximum(running_top, jnp.max(masked, axis=-1))
        weights = jnp.where(live, jnp.exp(masked - new_top[..., None]), 0.0)
        factor = jnp.exp(running_top - new_top)
        running_sum = running_sum * factor + jnp.sum(weights, axis=-1)
        running_out = running_out * factor[..., None] + jnp.einsum(
            "qhp,phe->qhe", weights, value_block, precision=lax.Precision.HIGHEST
        )
        return (new_top, running_sum, running_out)

    initial = (
        jnp.full((query_count, heads_local), MASK_LOW, jnp.float32),
        jnp.zeros((query_count, heads_local), jnp.float32),
        jnp.zeros((query_count, heads_local, head_size), jnp.float32),
    )
    final_top, final_sum, final_out = lax.fori_loop(0, block_count, advance, initial)
    return (final_out.reshape(query_count, feat_width), final_top, final_sum)


def on_device(
    tokens,
    attn_gain,
    mlp_gain,
    project_in,
    project_out,
    gate_up,
    project_down,
    kv_cache,
    lengths,
    owners,
    cache_start,
):
    groups = lax.axis_size("dp")
    my_index = lax.axis_index("dp")
    tok_rows = tokens.shape[0]
    request_count = tok_rows * lax.axis_size("tensor")
    feat_width = project_in.shape[2]
    head_size = HD
    heads_local = feat_width // head_size
    cache_rows = kv_cache.shape[1]
    capacity = max(MOST, (request_count // 2 + groups - 2) // (groups - 1))
    slot_count = groups * capacity
    gathered = lax.all_gather(tokens, "tensor", axis=0, tiled=True)
    normed = scaled_norm(gathered, attn_gain)
    projected = jnp.einsum("rd,cde->rce", normed, project_in, preferred_element_type=jnp.float32)
    my_length = lax.dynamic_slice_in_dim(lengths, my_index * request_count, request_count)
    my_owner = lax.dynamic_slice_in_dim(owners, my_index * request_count, request_count)
    my_start = lax.dynamic_slice_in_dim(cache_start, my_index * request_count, request_count)
    queries = (
        rotate(projected[:, 0].reshape(request_count, heads_local, head_size), my_length, head_size)
        .astype(jnp.bfloat16)
        .reshape(request_count, feat_width)
    )
    keys_new = (
        rotate(projected[:, 1].reshape(request_count, heads_local, head_size), my_length, head_size)
        .astype(jnp.bfloat16)
        .reshape(request_count, feat_width)
    )
    values_new = projected[:, 2].astype(jnp.bfloat16)
    packed = jnp.concatenate([queries, keys_new, values_new], axis=1)
    remote = my_owner != my_index
    target = (my_owner[:, None] == jnp.arange(groups)[None, :]) & remote[:, None]
    target_int = target.astype(jnp.int32)
    send_rank = jnp.sum((jnp.cumsum(target_int, axis=0) - target_int) * target_int, axis=1)
    send_place = jnp.where(remote, my_owner * capacity + send_rank, -1)
    selector = (jnp.arange(slot_count)[:, None] == send_place[None, :]).astype(jnp.bfloat16)
    outgoing = jnp.dot(selector, packed, preferred_element_type=jnp.float32).astype(jnp.bfloat16)
    outgoing = outgoing.reshape(groups, capacity, 3 * feat_width)
    arrived = lax.all_to_all(outgoing, "dp", split_axis=0, concat_axis=0, tiled=True).reshape(
        slot_count, 3 * feat_width
    )
    owner_blocks = owners.reshape(groups, request_count)
    bound_here = (owner_blocks == my_index) & (jnp.arange(groups)[:, None] != my_index)
    here_int = bound_here.astype(jnp.int32)
    in_rank = jnp.cumsum(here_int, axis=1) - here_int
    matched = bound_here[:, None, :] & (in_rank[:, None, :] == jnp.arange(capacity)[None, :, None])
    in_length = jnp.sum(
        jnp.where(matched, lengths.reshape(groups, request_count)[:, None, :], 0), axis=-1
    ).reshape(slot_count)
    in_start = jnp.sum(
        jnp.where(matched, cache_start.reshape(groups, request_count)[:, None, :], 0), axis=-1
    ).reshape(slot_count)
    in_live = jnp.any(matched, axis=-1).reshape(slot_count)
    in_span = jnp.where(in_live, in_length, 0)
    home_span = jnp.where(remote, 0, my_length)
    arrived_queries = arrived[:, :feat_width]
    joint_out, joint_top, joint_sum = partials(
        kv_cache,
        jnp.concatenate([queries, arrived_queries], axis=0),
        jnp.concatenate([my_start, in_start]),
        jnp.concatenate([home_span, in_span]),
        head_size,
    )
    home_out, far_out = (joint_out[:request_count], joint_out[request_count:])
    home_top, far_top = (joint_top[:request_count], joint_top[request_count:])
    home_sum, far_sum = (joint_sum[:request_count], joint_sum[request_count:])
    back_out, back_top, back_sum = (
        lax.all_to_all(
            far_out.reshape(groups, capacity, feat_width),
            "dp",
            split_axis=0,
            concat_axis=0,
            tiled=True,
        ),
        lax.all_to_all(
            far_top.reshape(groups, capacity, heads_local),
            "dp",
            split_axis=0,
            concat_axis=0,
            tiled=True,
        ),
        lax.all_to_all(
            far_sum.reshape(groups, capacity, heads_local),
            "dp",
            split_axis=0,
            concat_axis=0,
            tiled=True,
        ),
    )
    fetch_index = jnp.clip(send_place, 0, slot_count - 1)
    part_out = jnp.where(
        remote[:, None],
        jnp.take(back_out.reshape(slot_count, feat_width), fetch_index, axis=0),
        home_out,
    )
    part_top = jnp.where(
        remote[:, None],
        jnp.take(back_top.reshape(slot_count, heads_local), fetch_index, axis=0),
        home_top,
    )
    part_sum = jnp.where(
        remote[:, None],
        jnp.take(back_sum.reshape(slot_count, heads_local), fetch_index, axis=0),
        home_sum,
    )
    query_heads = queries.reshape(request_count, heads_local, head_size).astype(jnp.float32)
    key_heads = keys_new.reshape(request_count, heads_local, head_size).astype(jnp.float32)
    value_heads = values_new.reshape(request_count, heads_local, head_size).astype(jnp.float32)
    own_score = jnp.sum(query_heads * key_heads, axis=-1) * (1.0 / math.sqrt(head_size))
    top_all = jnp.maximum(part_top, own_score)
    keep_factor = jnp.exp(part_top - top_all)
    own_weight = jnp.exp(own_score - top_all)
    total_all = part_sum * keep_factor + own_weight
    summed = (
        part_out.reshape(request_count, heads_local, head_size) * keep_factor[..., None]
        + own_weight[..., None] * value_heads
    )
    attention = (
        (summed / total_all[..., None]).astype(jnp.bfloat16).reshape(request_count, feat_width)
    )
    log_sum_exp = top_all + jnp.log(total_all)
    write_rows = jnp.concatenate(
        [
            jnp.where(remote, cache_rows, my_start + my_length),
            jnp.where(in_live, in_start + in_length, cache_rows),
        ]
    )
    write_keys = jnp.concatenate([keys_new, arrived[:, feat_width : 2 * feat_width]], axis=0)
    write_values = jnp.concatenate([values_new, arrived[:, 2 * feat_width :]], axis=0)
    kv_updated = kv_cache.at[0, write_rows].set(write_keys, mode="drop")
    kv_updated = kv_updated.at[1, write_rows].set(write_values, mode="drop")
    attn_mine = lax.psum_scatter(
        jnp.dot(attention, project_out, preferred_element_type=jnp.float32),
        "tensor",
        scatter_dimension=0,
        tiled=True,
    )
    resid = (tokens.astype(jnp.float32) + attn_mine).astype(jnp.bfloat16)
    inner = expand_hidden(
        lax.all_gather(scaled_norm(resid, mlp_gain), "tensor", axis=0, tiled=True), gate_up
    )
    down_mine = lax.psum_scatter(
        jnp.dot(inner, project_down, preferred_element_type=jnp.float32),
        "tensor",
        scatter_dimension=0,
        tiled=True,
    )
    hidden_states = (resid.astype(jnp.float32) + down_mine).astype(jnp.bfloat16)
    return (hidden_states, log_sum_exp, kv_updated)


def solution(mesh):
    placed = (
        P(("dp", "tensor"), None),
        P(),
        P(),
        P(None, None, "tensor"),
        P("tensor", None),
        P(None, None, "tensor"),
        P("tensor", None),
        P(None, "dp", "tensor"),
        P(),
        P(),
        P(),
    )
    return jax.shard_map(
        on_device,
        mesh=mesh,
        in_specs=placed,
        out_specs=(P(("dp", "tensor"), None), P("dp", "tensor"), P(None, "dp", "tensor")),
        check_vma=False,
    )
```

profile of v0, /device:TPU:0, one launch (start us, length us, event | category | flops | bytes accessed | tf_op | source)
XLA Modules:
  0.0 412.1 jit_solution(6143601173590737157)
XLA Ops:
  7.3 4.6 %copy.265 = bf16[2,4096,256]{2,1,0:T(8,128)(2,1)} copy(bf16[2,4096,256]{2,1,0:T(8,128)(2,1)} %param.22) | data formatting | bytes 8388608
  20.3 16.5 %all-gather.3.cloned.1.call-done = bf16[256,2048]{1,0:T(8,128)(2,1)} async-done(((bf16[32,2048]{1,0:T(8,128)(2,1)}), bf16[256,2048]{1,0:T(8,128)(2,1)}) %all-gather.3.cloned.1.call-update) | async-done | bytes 1048592 | tf_op jit(solution)/shard_map/all_gather | solution.py:108
  38.4 2.7 fusion.17
  43.7 3.7 all-to-all-start
  49.0 4.5 %all-to-all-done = bf16[4,43,768]{2,1,0:T(8,128)(2,1)S(1)} async-done(((bf16[4,43,768]{2,1,0:T(8,128)(2,1)}), bf16[4,43,768]{2,1,0:T(8,128)(2,1)S(1)}, u32[]{:S(2)}, u32[]{:S(2)}) %all-to-all-start) | async-done | bytes 264224 | tf_op jit(solution)/shard_map/all_to_all | solution.py:134
  58.6 131.9 %while.14 = (s32[]{:T(128)}, f32[428,4]{0,1:T(4,128)S(1)}, f32[428,4]{0,1:T(4,128)S(1)}, f32[428,4,64]{0,2,1:T(8,128)}, s32[]{:T(128)}, /*index=5*/s32[428]{0:T(...) while((s32[]{:T(128)}, f32[428,4]{0,1:T(4,128)S(1)}, ...), condition=%wide.region_13.14_spmd, body=%wide.region_10.13_spmd.sunk | while | flops 796782464 | bytes 29254224 | solution.py:81
  58.8 1.9 constant_dynamic-slice_fusion.3
  60.7 1.8 copy.248
  62.5 1.9 fusion.73
  64.4 1.7 copy-done.1
  67.5 1.8 copy.249
  69.3 5.7 %fusion.75 = f32[428,4,64]{0,2,1:T(8,128)} fusion(bf16[512,4,64]{0,2,1:T(8,128)(2,1)} %bitcast.123, f32[4,512,428]{1,2,0:T(8,128)} %copy-done.1, f32[428,4]{0,1:T(4,128)S(1)} %max.29, pred[428,512]{1,0:T(8,128)(4,1)S(1)} %compare_and_fusion.3, f32[428,4,64]{0,2,1:T(8,128)} %get-tuple-element.299, f32[428,4]{0,1:T(4,128)S(1)} %get-tuple-element.281), kind=kOutput, calls=%fused_computation.16.clone.1 | convolution fusion | flops 676911104 | bytes 4877696 | tf_op jit(solution)/shard_map/while/body/qhp,phe->qhe/dot_general | solution.py:71
  75.3 1.9 constant_dynamic-slice_fusion.3
  77.2 1.8 copy.248
  79.0 1.9 fusion.73
  84.0 1.8 copy.249
  85.8 5.7 %fusion.75 = f32[428,4,64]{0,2,1:T(8,128)} fusion(bf16[512,4,64]{0,2,1:T(8,128)(2,1)} %bitcast.123, f32[4,512,428]{1,2,0:T(8,128)} %copy-done.1, f32[428,4]{0,1:T(4,128)S(1)} %max.29, pred[428,512]{1,0:T(8,128)(4,1)S(1)} %compare_and_fusion.3, f32[428,4,64]{0,2,1:T(8,128)} %get-tuple-element.299, f32[428,4]{0,1:T(4,128)S(1)} %get-tuple-element.281), kind=kOutput, calls=%fused_computation.16.clone.1 | convolution fusion | flops 676911104 | bytes 4877696 | tf_op jit(solution)/shard_map/while/body/qhp,phe->qhe/dot_general | solution.py:71
  91.8 1.9 constant_dynamic-slice_fusion.3
  93.6 1.8 copy.248
  95.4 1.9 fusion.73
  100.5 1.8 copy.249
  102.3 5.7 %fusion.75 = f32[428,4,64]{0,2,1:T(8,128)} fusion(bf16[512,4,64]{0,2,1:T(8,128)(2,1)} %bitcast.123, f32[4,512,428]{1,2,0:T(8,128)} %copy-done.1, f32[428,4]{0,1:T(4,128)S(1)} %max.29, pred[428,512]{1,0:T(8,128)(4,1)S(1)} %compare_and_fusion.3, f32[428,4,64]{0,2,1:T(8,128)} %get-tuple-element.299, f32[428,4]{0,1:T(4,128)S(1)} %get-tuple-element.281), kind=kOutput, calls=%fused_computation.16.clone.1 | convolution fusion | flops 676911104 | bytes 4877696 | tf_op jit(solution)/shard_map/while/body/qhp,phe->qhe/dot_general | solution.py:71
  108.3 1.9 constant_dynamic-slice_fusion.3
  110.1 1.8 copy.248
  111.9 1.9 fusion.73
  113.9 1.7 copy-done.1
  117.0 1.8 copy.249
  118.8 5.7 %fusion.75 = f32[428,4,64]{0,2,1:T(8,128)} fusion(bf16[512,4,64]{0,2,1:T(8,128)(2,1)} %bitcast.123, f32[4,512,428]{1,2,0:T(8,128)} %copy-done.1, f32[428,4]{0,1:T(4,128)S(1)} %max.29, pred[428,512]{1,0:T(8,128)(4,1)S(1)} %compare_and_fusion.3, f32[428,4,64]{0,2,1:T(8,128)} %get-tuple-element.299, f32[428,4]{0,1:T(4,128)S(1)} %get-tuple-element.281), kind=kOutput, calls=%fused_computation.16.clone.1 | convolution fusion | flops 676911104 | bytes 4877696 | tf_op jit(solution)/shard_map/while/body/qhp,phe->qhe/dot_general | solution.py:71
  124.8 1.9 constant_dynamic-slice_fusion.3
  126.6 1.8 copy.248
  128.4 1.9 fusion.73
  130.3 1.7 copy-done.1
  133.5 1.8 copy.249
  135.3 5.7 %fusion.75 = f32[428,4,64]{0,2,1:T(8,128)} fusion(bf16[512,4,64]{0,2,1:T(8,128)(2,1)} %bitcast.123, f32[4,512,428]{1,2,0:T(8,128)} %copy-done.1, f32[428,4]{0,1:T(4,128)S(1)} %max.29, pred[428,512]{1,0:T(8,128)(4,1)S(1)} %compare_and_fusion.3, f32[428,4,64]{0,2,1:T(8,128)} %get-tuple-element.299, f32[428,4]{0,1:T(4,128)S(1)} %get-tuple-element.281), kind=kOutput, calls=%fused_computation.16.clone.1 | convolution fusion | flops 676911104 | bytes 4877696 | tf_op jit(solution)/shard_map/while/body/qhp,phe->qhe/dot_general | solution.py:71
  141.2 1.9 constant_dynamic-slice_fusion.3
  143.1 1.8 copy.248
  144.9 1.9 fusion.73
  146.8 1.7 copy-done.1
  149.9 1.8 copy.249
  151.7 5.7 %fusion.75 = f32[428,4,64]{0,2,1:T(8,128)} fusion(bf16[512,4,64]{0,2,1:T(8,128)(2,1)} %bitcast.123, f32[4,512,428]{1,2,0:T(8,128)} %copy-done.1, f32[428,4]{0,1:T(4,128)S(1)} %max.29, pred[428,512]{1,0:T(8,128)(4,1)S(1)} %compare_and_fusion.3, f32[428,4,64]{0,2,1:T(8,128)} %get-tuple-element.299, f32[428,4]{0,1:T(4,128)S(1)} %get-tuple-element.281), kind=kOutput, calls=%fused_computation.16.clone.1 | convolution fusion | flops 676911104 | bytes 4877696 | tf_op jit(solution)/shard_map/while/body/qhp,phe->qhe/dot_general | solution.py:71
  157.7 1.9 constant_dynamic-slice_fusion.3
  159.6 1.8 copy.248
  161.4 1.9 fusion.73
  163.3 1.7 copy-done.1
  166.4 1.8 copy.249
  168.2 5.7 %fusion.75 = f32[428,4,64]{0,2,1:T(8,128)} fusion(bf16[512,4,64]{0,2,1:T(8,128)(2,1)} %bitcast.123, f32[4,512,428]{1,2,0:T(8,128)} %copy-done.1, f32[428,4]{0,1:T(4,128)S(1)} %max.29, pred[428,512]{1,0:T(8,128)(4,1)S(1)} %compare_and_fusion.3, f32[428,4,64]{0,2,1:T(8,128)} %get-tuple-element.299, f32[428,4]{0,1:T(4,128)S(1)} %get-tuple-element.281), kind=kOutput, calls=%fused_computation.16.clone.1 | convolution fusion | flops 676911104 | bytes 4877696 | tf_op jit(solution)/shard_map/while/body/qhp,phe->qhe/dot_general | solution.py:71
  174.2 1.9 constant_dynamic-slice_fusion.3
  176.1 1.8 copy.248
  177.8 1.9 fusion.73
  179.8 1.7 copy-done.1
  182.9 1.8 copy.249
  184.7 5.7 %fusion.75 = f32[428,4,64]{0,2,1:T(8,128)} fusion(bf16[512,4,64]{0,2,1:T(8,128)(2,1)} %bitcast.123, f32[4,512,428]{1,2,0:T(8,128)} %copy-done.1, f32[428,4]{0,1:T(4,128)S(1)} %max.29, pred[428,512]{1,0:T(8,128)(4,1)S(1)} %compare_and_fusion.3, f32[428,4,64]{0,2,1:T(8,128)} %get-tuple-element.299, f32[428,4]{0,1:T(4,128)S(1)} %get-tuple-element.281), kind=kOutput, calls=%fused_computation.16.clone.1 | convolution fusion | flops 676911104 | bytes 4877696 | tf_op jit(solution)/shard_map/while/body/qhp,phe->qhe/dot_general | solution.py:71
  191.2 3.2 all-to-all-start.3
  195.2 3.8 all-to-all-done.3
  199.1 3.4 all-to-all-start.2
  210.2 4.0 all-to-all-start.1
  216.7 2.8 all-to-all-done.1
  224.3 3.0 fusion.55
  227.4 34.3 %reduce-scatter.3.cloned.1.call-done = f32[32,2048]{1,0:T(8,128)} async-done(((f32[256,2048]{1,0:T(8,128)}), f32[32,2048]{1,0:T(8,128)}) %reduce-scatter.3.cloned.1.call-update) | async-done | bytes 262160 | tf_op jit(solution)/shard_map/reduce_scatter | solution.py:227
  263.6 20.9 %all-gather.5.cloned.1.call-done = bf16[256,2048]{1,0:T(8,128)(2,1)} async-done(((bf16[32,2048]{1,0:T(8,128)(2,1)}), bf16[256,2048]{1,0:T(8,128)(2,1)}) %all-gather.5.cloned.1.call-update) | async-done | bytes 1048592 | tf_op jit(solution)/shard_map/all_gather | solution.py:235
  284.5 6.2 %fusion.21 = f32[256,2,1024]{2,0,1:T(8,128)S(1)} fusion(bf16[2,2048,1024]{2,1,0:T(8,128)(2,1)} %param.20, bf16[256,2048]{1,0:T(8,128)(2,1)} %all-gather.5.cloned.1.call-done), kind=kOutput, calls=%fused_computation.38 | convolution fusion | flops 2147483648 | bytes 11534336 | tf_op jit(solution)/shard_map/rd,cdf->rcf/dot_general | solution.py:37
  290.8 2.7 fusion.25
  299.6 52.3 %scatter_fusion = bf16[2,4096,256]{2,1,0:T(8,128)(2,1)} fusion(bf16[2,4096,256]{2,1,0:T(8,128)(2,1)} %get-tuple-element.328, s32[428]{0:T(512)S(1)} %bitcast.122, bf16[428,256]{1,0:T(8,128)(2,1)} %copy.229), kind=kCustom, calls=%fused_computation.3 | custom fusion | bytes 660832 | tf_op jit(solution)/shard_map/scatter | solution.py:225
  351.9 52.1 %scatter_fusion.1 = bf16[2,4096,256]{2,1,0:T(8,128)(2,1)} fusion(bf16[2,4096,256]{2,1,0:T(8,128)(2,1)} %scatter_fusion, s32[428]{0:T(512)S(1)} %bitcast.121, bf16[428,256]{1,0:T(8,128)(2,1)S(1)} %copy-done.2), kind=kCustom, calls=%fused_computation.4 | custom fusion | bytes 660832 | tf_op jit(solution)/shard_map/scatter | solution.py:226
  (204 shorter events, 61.1 us)
Async XLA Ops:
  7.2 31.2 %copy-start = (bf16[3,2048,256]{2,1,0:T(8,128)(2,1)S(1)}, bf16[3,2048,256]{2,1,0:T(8,128)(2,1)}, u32[]{:S(2)}) copy-start(bf16[3,2048,256]{2,1,0:T(8,128)(2,1)} %param.18) | copy-start | bytes 9437188
  7.2 4.8 %copy-start.13 = (bf16[2048]{0:T(1024)(128)(2,1)S(1)}, bf16[2048]{0:T(1024)(128)(2,1)}, u32[]{:S(2)}) copy-start(bf16[2048]{0:T(1024)(128)(2,1)} %param.16) | copy-start | bytes 12292
  7.2 7.6 %copy-start.9 = (s32[1024]{0:T(1024)S(1)}, s32[1024]{0:T(1024)}, u32[]{:S(2)}) copy-start(s32[1024]{0:T(1024)} %param.23) | copy-start | bytes 12292
  7.2 4.7 %copy-start.10 = (s32[1024]{0:T(1024)S(1)}, s32[1024]{0:T(1024)}, u32[]{:S(2)}) copy-start(s32[1024]{0:T(1024)} %param.24) | copy-start | bytes 12292
  7.2 7.6 %copy-start.11 = (s32[1024]{0:T(1024)S(1)}, s32[1024]{0:T(1024)}, u32[]{:S(2)}) copy-start(s32[1024]{0:T(1024)} %param.25) | copy-start | bytes 12292
  7.2 29.6 %all-gather.3.cloned.1.call-start = ((), (), s32[]{:S(2)}) async-start(), calls=%async_computation.6 | async-start | bytes 1179648 | tf_op jit(solution)/shard_map/all_gather | solution.py:108
  41.0 0.9 copy-start.3
  41.1 0.9 copy-start.5
  42.0 0.7 copy-start.6
  42.0 0.7 copy-start.7
  43.7 9.7 %all-to-all-start = ((bf16[4,43,768]{2,1,0:T(8,128)(2,1)}), bf16[4,43,768]{2,1,0:T(8,128)(2,1)S(1)}, u32[]{:S(2)}, u32[]{:S(2)}) async-start(bf16[4,43,768]{2,1,0:T(8,128)(2,1)} %reshape.405), calls=%async_computation | async-start | bytes 589824 | tf_op jit(solution)/shard_map/all_to_all | solution.py:134
  64.4 1.8 copy-start.1
  80.9 1.8 copy-start.1
  97.4 1.8 copy-start.1
  113.8 1.8 copy-start.1
  130.3 1.8 copy-start.1
  146.8 1.8 copy-start.1
  163.3 1.8 copy-start.1
  179.8 1.8 copy-start.1
  190.4 25.6 %copy-start.12 = (pred[256]{0:T(512)(128)(4,1)S(1)}, pred[256]{0:T(512)(128)(4,1)}, u32[]{:S(2)}) copy-start(pred[256]{0:T(512)(128)(4,1)} %get-tuple-element.183) | copy-start | bytes 772
  191.2 7.9 %all-to-all-start.3 = ((f32[4,1,172]{2,1,0:T(1,128)}), f32[4,1,172]{2,1,0:T(1,128)S(1)}, u32[]{:S(2)}, u32[]{:S(2)}) async-start(f32[4,1,172]{2,1,0:T(1,128)} %reshape.462), calls=%async_computation.3 | async-start | bytes 8192 | tf_op jit(solution)/shard_map/all_to_all | solution.py:177
  199.1 11.1 %all-to-all-start.2 = ((f32[4,1,172]{2,1,0:T(1,128)}), f32[4,1,172]{2,1,0:T(1,128)S(1)}, u32[]{:S(2)}, u32[]{:S(2)}) async-start(f32[4,1,172]{2,1,0:T(1,128)} %reshape.460), calls=%async_computation.2 | async-start | bytes 8192 | tf_op jit(solution)/shard_map/all_to_all | solution.py:170
  210.2 9.3 %all-to-all-start.1 = ((f32[4,43,256]{2,1,0:T(8,128)}), f32[4,43,256]{2,1,0:T(8,128)}, u32[]{:S(2)}, u32[]{:S(2)}) async-start(f32[4,43,256]{2,1,0:T(8,128)} %reshape.407), calls=%async_computation.1 | async-start | bytes 393216 | tf_op jit(solution)/shard_map/all_to_all | solution.py:163
  214.2 47.5 %reduce-scatter.3.cloned.1.call-start = ((), (), s32[]{:S(2)}) async-start(), calls=%async_computation.7 | async-start | bytes 2359296 | tf_op jit(solution)/shard_map/reduce_scatter | solution.py:227
  222.1 39.6 %copy-start.4 = (bf16[32,2048]{1,0:T(8,128)(2,1)S(1)}, bf16[32,2048]{1,0:T(8,128)(2,1)}, u32[]{:S(2)}) copy-start(bf16[32,2048]{1,0:T(8,128)(2,1)} %param.15) | copy-start | bytes 393220
  224.3 3.1 copy-start.14
  227.3 57.2 %all-gather.5.cloned.1.call-start = ((), (), s32[]{:S(2)}) async-start(), calls=%async_computation.8 | async-start | bytes 1179648 | tf_op jit(solution)/shard_map/all_gather | solution.py:235
  263.6 140.4 %reduce-scatter.5.cloned.1.call-start = ((), (), s32[]{:S(2)}) async-start(), calls=%async_computation.9 | async-start | bytes 2359296 | tf_op jit(solution)/shard_map/reduce_scatter | solution.py:237
  284.5 6.2 %copy-start.17 = (bf16[1024,2048]{1,0:T(8,128)(2,1)S(1)}, bf16[1024,2048]{1,0:T(8,128)(2,1)}, u32[]{:S(2)}) copy-start(bf16[1024,2048]{1,0:T(8,128)(2,1)} %param.21) | copy-start | bytes 12582916
  290.7 2.8 copy-start.15
  290.7 2.8 copy-start.16
  290.7 2.8 copy-start.8
  299.6 52.3 %copy-start.2 = (bf16[428,256]{1,0:T(8,128)(2,1)S(1)}, bf16[428,256]{1,0:T(8,128)(2,1)}, u32[]{:S(2)}) copy-start(bf16[428,256]{1,0:T(8,128)(2,1)} %copy.231) | copy-start | bytes 657412
Sparse Core Ops, SparseCore 0:
  12.0 24.7 all-gather.2
  227.5 34.1 reduce-scatter.2
  263.8 20.6 all-gather.4
  293.6 35.3 reduce-scatter.4
where the time goes:
time: 416 us; the launch traced here: 412 us
  local copies, waits for them, and re-layouts  191 us (46%)
  waiting for transfers between devices  82.9 us (20%)
  matrix products  75.8 us (18%)
  other arithmetic  32.8 us (8%)
  between operations  14.9 us (4%)
  starting transfers between devices  14.5 us (3%)
    scatter x1, local copies, waits for them, and re-layouts, on_device(): kv_updated = kv_cache.at[0, write_rows].set(write_keys, mode='drop')  52.3 us
    scatter x1, local copies, waits for them, and re-layouts, on_device(): kv_updated = kv_updated.at[1, write_rows].set(write_values, mode='drop')  52.1 us
    dot_general x8, matrix products, advance(): jnp.einsum('qhp,phe->qhe', weights, value_block, precision=lax.Precision....  45.7 us
    while x40, local copies, waits for them, and re-layouts  42.7 us
    reduce_scatter x1, waiting for transfers between devices, on_device(): lax.psum_scatter(jnp.dot(attention, project_out, preferred_element_type=j...  34.3 us
    all_gather x1, waiting for transfers between devices, on_device(): lax.all_gather(scaled_norm(resid, mlp_gain), 'tensor', axis=0, tiled=True)  20.9 us
    all_gather x1, waiting for transfers between devices, on_device(): gathered = lax.all_gather(tokens, 'tensor', axis=0, tiled=True)  16.5 us
    dot_general x8, matrix products, advance(): jnp.einsum('qhe,phe->qhp', query_heads, key_block, preferred_element_type...  15.2 us
  transfers between devices with their start and end apart: 8, of which 6 were waited for; matrix products, arithmetic and copies ran while one was open for 32% of the time, Pallas kernels for 0%

commit v1 on v0

v1 whole, which is shorter than its diff:
```python
import functools
import math

import jax
import jax.numpy as jnp
from jax import lax
from jax.experimental import pallas as pl
from jax.experimental.pallas import tpu as pltpu
from jax.sharding import PartitionSpec as P

HD = 64
NORM_EPS = 1e-05
ROPE_BASE = 130000.0
MASK_LOW = -1e30
BF = jnp.bfloat16
F32 = jnp.float32
LANES = 128
Q_TILE = 32
P_TILE = 512


def round_up(count, step):
    return (count + step - 1) // step * step


def dot(left, right):
    return jnp.dot(left, right, preferred_element_type=F32)


def dot_nt(left, right):
    return lax.dot_general(left, right, (((1,), (1,)), ((), ())), preferred_element_type=F32)


def dot_tn(left, right):
    return lax.dot_general(left, right, (((0,), (0,)), ((), ())), preferred_element_type=F32)


def one_hot(row_count, slots):
    rows = lax.broadcasted_iota(jnp.int32, (row_count, slots.shape[1]), 0)
    return jnp.where(rows == slots, 1.0, 0.0).astype(BF)


def swap(values, axis_name, offset):
    count = lax.axis_size(axis_name)
    return lax.ppermute(values, axis_name, [(i, i ^ offset) for i in range(count)])


def gather_tensor(block):
    count = lax.axis_size("tensor")
    pieces = [None] * count
    pieces[0] = block
    for k in range(2, count, 2):
        pieces[k] = swap(block, "tensor", k)
    for k in range(0, count, 2):
        pieces[k + 1] = swap(pieces[k], "tensor", 1)
    return pieces


def reduce_tensor(keep, send):
    count = lax.axis_size("tensor")
    came = swap(send, "tensor", 1)
    joined = [(keep[k].astype(F32) + came[k].astype(F32)).astype(BF) for k in range(count // 2)]
    return [joined[0]] + [swap(joined[k], "tensor", 2 * k) for k in range(1, count // 2)]


def relative(values, block_count, me):
    cut = values.reshape(block_count, -1)
    bit = 1
    while bit < block_count:
        split = cut.reshape(block_count // (2 * bit), 2, bit, -1)
        cut = jnp.where((me & bit) != 0, split[:, ::-1], split).reshape(block_count, -1)
        bit *= 2
    return cut.reshape(values.shape)


def scaled_norm(values, scales):
    wide = values.astype(F32)
    factor = lax.rsqrt(jnp.mean(wide * wide, axis=-1, keepdims=True) + NORM_EPS)
    return (wide * factor * scales.astype(F32)).astype(BF)


def qkv_kernel(piece_count, home_count, slot_rows, hop_count, *refs):
    pieces = refs[:piece_count]
    weights, cosine, sine, slots = refs[piece_count : piece_count + 4]
    home_ref = refs[piece_count + 4]
    out_refs = refs[piece_count + 5 :]
    normed = jnp.concatenate([piece[...] for piece in pieces], axis=0)
    width = weights.shape[2]
    lane = lax.broadcasted_iota(jnp.int32, (normed.shape[0], width), 1)
    low_half = (lane % HD) < HD // 2
    parts = []
    for c in range(3):
        projected = dot(normed, weights[c])
        if c < 2:
            ahead = pltpu.roll(projected, width - HD // 2, 1)
            behind = pltpu.roll(projected, HD // 2, 1)
            turned = jnp.where(low_half, -ahead, behind)
            projected = projected * cosine[...] + turned * sine[...]
        parts.append(projected.astype(BF))
    packed = jnp.concatenate(parts, axis=1)
    selector = one_hot(home_count + hop_count * slot_rows, slots[...])
    picked = dot(selector, packed).astype(BF)
    home_ref[...] = picked[:home_count]
    for k in range(hop_count):
        first = home_count + k * slot_rows
        out_refs[k][...] = picked[first : first + slot_rows]


def attend_tile(query, key, value, start, span, low, high, kv_ref, heads):
    rows, width = query.shape
    scale = 1.0 / math.sqrt(HD)
    lane_head = lax.broadcasted_iota(jnp.int32, (rows, width), 1) // HD
    masks = [lane_head == h for h in range(heads)]
    zero = jnp.zeros_like(query)
    stacked = jnp.concatenate([jnp.where(m, query, zero) for m in masks], axis=0)
    product = query.astype(F32) * key.astype(F32)
    own = jnp.concatenate(
        [jnp.sum(jnp.where(m, product, 0.0), axis=1, keepdims=True) for m in masks], axis=0
    ) * scale
    starts = jnp.concatenate([start] * heads, axis=0)
    spans = jnp.concatenate([span] * heads, axis=0)
    first_out = jnp.concatenate([value.astype(F32)] * heads, axis=0)

    def advance(step, carry):
        top, total, out = carry
        first = pl.multiple_of(step * P_TILE, P_TILE)
        keys = kv_ref[0, pl.ds(first, P_TILE), :]
        values = kv_ref[1, pl.ds(first, P_TILE), :]
        offset = lax.broadcasted_iota(jnp.int32, (1, P_TILE), 1) + first
        since = offset - starts
        live = (since >= 0) & (since < spans)
        scores = jnp.where(live, dot_nt(stacked, keys) * scale, MASK_LOW)
        new_top = jnp.maximum(top, jnp.max(scores, axis=1, keepdims=True))
        weights = jnp.exp(scores - new_top)
        factor = jnp.exp(top - new_top)
        total = total * factor + jnp.sum(weights, axis=1, keepdims=True)
        out = out * factor + dot(weights.astype(BF), values)
        return new_top, total, out

    top, total, out = lax.fori_loop(
        low, high, advance, (own, jnp.ones_like(own), first_out)
    )
    out = out / total
    log_sum = top + jnp.log(total)
    attended = jnp.zeros((rows, width), F32)
    lane = lax.broadcasted_iota(jnp.int32, (rows, LANES), 1)
    extra = jnp.zeros((rows, LANES), F32)
    for h in range(heads):
        attended = jnp.where(masks[h], out[h * rows : (h + 1) * rows], attended)
        rest = log_sum[h * rows : (h + 1) * rows]
        for part in range(3):
            piece = rest.astype(BF).astype(F32)
            rest = rest - piece
            extra = jnp.where(lane == part * heads + h, piece, extra)
    return jnp.concatenate([attended.astype(BF), extra.astype(BF)], axis=1)


def attend_all(bounds, packed, starts, spans, kv_ref, result, heads):
    width = heads * HD
    for tile in range(packed.shape[0] // Q_TILE):
        here = slice(tile * Q_TILE, (tile + 1) * Q_TILE)
        rows = packed[here]
        result[here, :] = attend_tile(
            rows[:, :width],
            rows[:, width : 2 * width],
            rows[:, 2 * width :],
            starts[here, :],
            spans[here, :],
            bounds[0, tile],
            bounds[1, tile],
            kv_ref,
            heads,
        )


def home_kernel(heads, bounds, packed, starts, spans, kv_ref, result):
    attend_all(bounds, packed[...], starts, spans, kv_ref, result, heads)


def far_kernel(heads, hop_count, sorted_count, bounds, *refs):
    arrived = jnp.concatenate([ref[...] for ref in refs[:hop_count]], axis=0)
    order, starts, spans, kv_ref = refs[hop_count : hop_count + 4]
    outs = refs[hop_count + 4 : 2 * hop_count + 4]
    scratch = refs[-1]
    mover = one_hot(sorted_count, order[...])
    in_order = dot(mover, arrived).astype(BF)
    attend_all(bounds, in_order, starts, spans, kv_ref, scratch, heads)
    back = dot_tn(mover, scratch[...]).astype(BF)
    slot_rows = arrived.shape[0] // hop_count
    for k in range(hop_count):
        outs[k][...] = back[k * slot_rows : (k + 1) * slot_rows]


def out_kernel(heads, hop_count, rows, slots, home, *refs):
    backs = refs[:hop_count]
    weights, keep_ref, send_ref, log_ref = refs[hop_count:]
    width = heads * HD
    both = jnp.concatenate([home[...]] + [ref[...] for ref in backs], axis=0)
    selector = one_hot(both.shape[0], slots[...])
    placed = dot_tn(selector, both)
    extra = placed[:, width:]
    log_sum = extra + pltpu.roll(extra, LANES - heads, 1) + pltpu.roll(extra, LANES - 2 * heads, 1)
    log_ref[...] = log_sum
    partial = dot(placed[:, :width].astype(BF), weights[...]).astype(BF)
    for k in range(partial.shape[0] // rows):
        ref = keep_ref if k % 2 == 0 else send_ref
        ref[k // 2] = partial[k * rows : (k + 1) * rows]


def mlp_kernel(piece_count, rows, *refs):
    pieces = refs[:piece_count]
    gate_up, down, keep_ref, send_ref, normed, total = refs[piece_count:]
    step = pl.program_id(0)

    @pl.when(step == 0)
    def _():
        for k, piece in enumerate(pieces):
            normed[k * rows : (k + 1) * rows, :] = piece[...]

    gate = dot(normed[...], gate_up[0])
    upward = dot(normed[...], gate_up[1])
    inner = (gate / (1.0 + jnp.exp(-gate)) * upward).astype(BF)
    partial = dot(inner, down[...])

    @pl.when(step == 0)
    def _():
        total[...] = partial

    @pl.when(step > 0)
    def _():
        total[...] += partial

    @pl.when(step == pl.num_programs(0) - 1)
    def _():
        for k in range(piece_count):
            ref = keep_ref if k % 2 == 0 else send_ref
            ref[k // 2] = total[k * rows : (k + 1) * rows, :].astype(BF)


def update_kernel(hop_count, width, home_rows, far_rows, home, *refs):
    far = refs[:hop_count]
    kv_in, kv_out = refs[hop_count:]
    block = kv_in.shape[1]
    position = lax.broadcasted_iota(jnp.int32, (block, 1), 0) + pl.program_id(0) * block
    fresh = jnp.concatenate([home[:, width:]] + [ref[:, width:] for ref in far], axis=0)
    targets = jnp.concatenate([home_rows[...], far_rows[...]], axis=1)
    hit = jnp.where(position == targets, 1.0, 0.0)
    written = jnp.max(hit, axis=1, keepdims=True) > 0.0
    values = dot(hit.astype(BF), fresh).astype(BF)
    kv_out[0] = jnp.where(written, values[:, :width], kv_in[0])
    kv_out[1] = jnp.where(written, values[:, width:], kv_in[1])


def tile_bounds(starts, spans, cache_rows):
    cut_start = starts.reshape(-1, Q_TILE)
    cut_end = jnp.where(spans > 0, starts + spans, 0).reshape(-1, Q_TILE)
    low = jnp.min(cut_start, axis=1) // P_TILE
    high = (jnp.max(cut_end, axis=1) + P_TILE - 1) // P_TILE
    return jnp.stack([jnp.minimum(low, high), high]).astype(jnp.int32)


def vmem(count):
    return [pl.BlockSpec(memory_space=pltpu.VMEM)] * count


def on_device(
    tokens,
    attn_gain,
    mlp_gain,
    project_in,
    project_out,
    gate_up,
    project_down,
    kv_cache,
    lengths,
    owners,
    cache_start,
):
    groups = lax.axis_size("dp")
    my_index = lax.axis_index("dp")
    tensor_count = lax.axis_size("tensor")
    me = lax.axis_index("tensor")
    rows, model_width = tokens.shape
    request_count = rows * tensor_count
    width = project_in.shape[2]
    heads = width // HD
    cache_rows = kv_cache.shape[1]
    home_count = round_up(request_count - request_count // 2, Q_TILE)
    hops = groups - 1
    capacity = (request_count // 2 + groups - 2) // (groups - 1)
    slot_rows = round_up(capacity, 16)
    far_count = hops * slot_rows
    sorted_count = round_up(min(hops * capacity, far_count), Q_TILE)
    params = functools.partial(pltpu.CompilerParams, vmem_limit_bytes=40 * 1024 * 1024)

    normed = scaled_norm(tokens, attn_gain)
    pieces = gather_tensor(normed)

    blocks = lambda values: values.reshape(groups, request_count)
    mine = lambda values: lax.dynamic_slice_in_dim(values, my_index * request_count, request_count)
    my_length, my_owner, my_start = (
        relative(mine(values), tensor_count, me) for values in (lengths, owners, cache_start)
    )
    before = (my_owner[:, None] == my_owner[None, :]) & (my_start[:, None] < my_start[None, :])
    rank = jnp.sum(before.astype(jnp.int32), axis=0)
    hop = my_owner ^ my_index
    slot = jnp.where(hop == 0, rank, home_count + (hop - 1) * slot_rows + rank)
    home_hit = slot[None, :] == jnp.arange(home_count)[:, None]
    pick = lambda hit, values: jnp.sum(jnp.where(hit, values, 0), axis=1)
    home_span = pick(home_hit, my_length[None, :])
    home_live = home_span > 0
    home_start = jnp.where(home_live, pick(home_hit, my_start[None, :]), cache_rows)

    all_here = blocks(owners) == my_index
    start_blocks, length_blocks = blocks(cache_start), blocks(lengths)
    ahead = all_here[:, :, None] & (start_blocks[:, :, None] < start_blocks[:, None, :])
    in_rank = jnp.sum(ahead.astype(jnp.int32), axis=1)
    in_hop = jnp.arange(groups)[:, None] ^ my_index
    in_slot = jnp.where(all_here & (in_hop != 0), (in_hop - 1) * slot_rows + in_rank, -1).reshape(-1)
    far_hit = in_slot[None, :] == jnp.arange(far_count)[:, None]
    far_span = pick(far_hit, lengths[None, :])
    far_start = jnp.where(far_span > 0, pick(far_hit, cache_start[None, :]), cache_rows)
    far_live = far_span > 0
    far_before = far_live[:, None] & (far_start[:, None] < far_start[None, :])
    far_order = jnp.where(far_live, jnp.sum(far_before.astype(jnp.int32), axis=0), -1)
    sort_hit = far_order[None, :] == jnp.arange(sorted_count)[:, None]
    sort_span = pick(sort_hit, far_span[None, :])
    sort_start = jnp.where(sort_span > 0, pick(sort_hit, far_start[None, :]), cache_rows)
    home_bounds = tile_bounds(home_start, home_span, cache_rows)
    far_bounds = tile_bounds(sort_start, sort_span, cache_rows)
    home_write = jnp.where(home_live, home_start + home_span, -1)[None, :]
    far_write = jnp.where(far_live, far_start + far_span, -1)[None, :]

    half = HD // 2
    freqs = ROPE_BASE ** (-(jnp.arange(half, dtype=F32) * 2.0 / HD))
    angles = my_length.astype(F32)[:, None] * freqs[None, :]
    cosine = jnp.tile(jnp.cos(angles), (1, width // half))
    sine = jnp.tile(jnp.sin(angles), (1, width // half))

    slots = slot[None, :]
    shape = jax.ShapeDtypeStruct
    packed_outs = pl.pallas_call(
        functools.partial(qkv_kernel, tensor_count, home_count, slot_rows, hops),
        out_shape=[shape((home_count, 3 * width), BF)] + [shape((slot_rows, 3 * width), BF)] * hops,
        in_specs=vmem(tensor_count + 4),
        out_specs=vmem(1 + hops),
        compiler_params=params(),
        name="qkv",
    )(*pieces, project_in, cosine, sine, slots)
    home_packed = packed_outs[0]
    arrived = [swap(packed_outs[k], "dp", k) for k in range(1, groups)]

    out_width = width + LANES
    smem = pl.BlockSpec(memory_space=pltpu.SMEM)
    home_att = pl.pallas_call(
        functools.partial(home_kernel, heads),
        out_shape=shape((home_count, out_width), BF),
        in_specs=[smem] + vmem(4),
        out_specs=vmem(1)[0],
        compiler_params=params(),
        cost_estimate=pl.CostEstimate(flops=2 * 10**9, bytes_accessed=4 * 2**20, transcendentals=10**6),
        name="home_attention",
    )(home_bounds, home_packed, home_start[:, None], home_span[:, None], kv_cache)
    far_outs = pl.pallas_call(
        functools.partial(far_kernel, heads, hops, sorted_count),
        out_shape=[shape((slot_rows, out_width), BF)] * hops,
        in_specs=[smem] + vmem(hops + 4),
        out_specs=vmem(hops),
        scratch_shapes=[pltpu.VMEM((sorted_count, out_width), BF)],
        compiler_params=params(),
        name="far_attention",
    )(far_bounds, *arrived, far_order[None, :], sort_start[:, None], sort_span[:, None], kv_cache)
    backs = [swap(far_outs[k - 1], "dp", k) for k in range(1, groups)]

    block = 512
    kv_spec = pl.BlockSpec((2, block, width), lambda i: (0, i, 0))
    fixed = lambda array: pl.BlockSpec(array.shape, lambda i: (0,) * array.ndim)
    kv_updated = pl.pallas_call(
        functools.partial(update_kernel, hops, width),
        grid=(cache_rows // block,),
        out_shape=shape(kv_cache.shape, BF),
        in_specs=[fixed(home_write), fixed(far_write), fixed(home_packed)]
        + [fixed(a) for a in arrived]
        + [kv_spec],
        out_specs=kv_spec,
        compiler_params=params(),
        cost_estimate=pl.CostEstimate(flops=2 * 10**9, bytes_accessed=8 * 2**20, transcendentals=0),
        name="cache_update",
    )(home_write, far_write, home_packed, *arrived, kv_cache)

    half_count = tensor_count // 2
    keep, send, log_rel = pl.pallas_call(
        functools.partial(out_kernel, heads, hops, rows),
        out_shape=[shape((half_count, rows, model_width), BF)] * 2
        + [shape((request_count, LANES), F32)],
        in_specs=vmem(3 + hops),
        out_specs=vmem(3),
        compiler_params=params(),
        name="project_out",
    )(slots, home_att, *backs, project_out)
    log_sum_exp = relative(log_rel.reshape(-1), tensor_count, me).reshape(log_rel.shape)[:, :heads]

    sums = reduce_tensor(keep, send)
    attn_mine = sum(piece.astype(F32) for piece in sums)
    resid = (tokens.astype(F32) + attn_mine).astype(BF)
    mlp_pieces = gather_tensor(scaled_norm(resid, mlp_gain))

    hidden = gate_up.shape[2]
    f_block = min(256, hidden)
    keep, send = pl.pallas_call(
        functools.partial(mlp_kernel, tensor_count, rows),
        grid=(hidden // f_block,),
        out_shape=[shape((half_count, rows, model_width), BF)] * 2,
        in_specs=[fixed(normed)] * tensor_count
        + [
            pl.BlockSpec((2, model_width, f_block), lambda i: (0, 0, i)),
            pl.BlockSpec((f_block, model_width), lambda i: (i, 0)),
        ],
        out_specs=[pl.BlockSpec((half_count, rows, model_width), lambda i: (0, 0, 0))] * 2,
        scratch_shapes=[
            pltpu.VMEM((request_count, model_width), BF),
            pltpu.VMEM((request_count, model_width), F32),
        ],
        compiler_params=params(),
        name="mlp",
    )(*mlp_pieces, gate_up, project_down)
    down_mine = sum(piece.astype(F32) for piece in reduce_tensor(keep, send))
    hidden_states = (resid.astype(F32) + down_mine).astype(BF)
    return (hidden_states, log_sum_exp, kv_updated)


def solution(mesh):
    placed = (
        P(("dp", "tensor"), None),
        P(),
        P(),
        P(None, None, "tensor"),
        P("tensor", None),
        P(None, None, "tensor"),
        P("tensor", None),
        P(None, "dp", "tensor"),
        P(),
        P(),
        P(),
    )
    return jax.shard_map(
        on_device,
        mesh=mesh,
        in_specs=placed,
        out_specs=(P(("dp", "tensor"), None), P("dp", "tensor"), P(None, "dp", "tensor")),
        check_vma=False,
    )
```

time: 416 us -> 118 us (0.28)
  local copies, waits for them, and re-layouts: 191 us -> 15.7 us
  matrix products: 75.8 us -> 0 us
  waiting for transfers between devices: 82.9 us -> 33.3 us
  Pallas kernels: 0 us -> 24.6 us
  other arithmetic: 32.8 us -> 13.8 us
  starting transfers between devices: 14.5 us -> 29.2 us
  between operations: 14.9 us -> 1.08 us
    scatter x2 -> x0, local copies, waits for them, and re-layouts: 104 us -> none  [the longest x1 52.3 us: on_device(): kv_updated = kv_cache.at[0, write_rows].set(write_keys, mode='drop')]
    dot_general x21 -> x0, matrix products: 75.8 us -> none  [the longest x8 45.7 us: advance(): jnp.einsum('qhp,phe->qhe', weights, value_block, precision=lax.Precision....]
    while x40 -> x0, local copies, waits for them, and re-layouts: 42.7 us -> none
    all_gather x2 -> x0, waiting for transfers between devices: 37.4 us -> none  [the longest x1 20.9 us: on_device(): lax.all_gather(scaled_norm(resid, mlp_gain), 'tensor', axis=0, tiled=True)]
    reduce_scatter x2 -> x0, waiting for transfers between devices: 34.3 us -> none  [the longest x1 34.3 us: on_device(): lax.psum_scatter(jnp.dot(attention, project_out, preferred_element_type=j...]
    ppermute x0 -> x28, waiting for transfers between devices: none -> 33.3 us  [swap(): lax.ppermute(values, axis_name, [(i, i ^ offset) for i in range(count)])]
    ppermute x0 -> x28, starting transfers between devices: none -> 29.2 us  [swap(): lax.ppermute(values, axis_name, [(i, i ^ offset) for i in range(count)])]
    pallas_call x0 -> x6, Pallas kernels: none -> 24.6 us  [the longest x1 7.27 us: on_device(): pl.pallas_call(functools.partial(mlp_kernel, tensor_count, rows), grid=(h...]
  transfers between devices with their start and end apart: 8 -> 28, of which waited for: 6 -> 14; matrix products, arithmetic and copies ran while one was open for 32% -> 18% of each run, Pallas kernels for 0% -> 8%
where the time goes in v1:
time: 118 us
  waiting for transfers between devices  33.3 us (28%)
  starting transfers between devices  29.2 us (25%)
  Pallas kernels  24.6 us (21%)
  local copies, waits for them, and re-layouts  15.7 us (13%)
  other arithmetic  13.8 us (12%)
    ppermute x28, waiting for transfers between devices, swap(): lax.ppermute(values, axis_name, [(i, i ^ offset) for i in range(count)])  33.3 us
    ppermute x28, starting transfers between devices, swap(): lax.ppermute(values, axis_name, [(i, i ^ offset) for i in range(count)])  29.2 us
    pallas_call x1, Pallas kernels, on_device(): pl.pallas_call(functools.partial(mlp_kernel, tensor_count, rows), grid=(h...  7.27 us
    pallas_call x1, Pallas kernels, on_device(): pl.pallas_call(functools.partial(update_kernel, hops, width), grid=(cache...  5.56 us
    unnamed x38, local copies, waits for them, and re-layouts  4.74 us
    pallas_call x1, Pallas kernels, on_device(): pl.pallas_call(functools.partial(far_kernel, heads, hops, sorted_count),...  4.39 us
    pallas_call x1, Pallas kernels, on_device(): pl.pallas_call(functools.partial(home_kernel, heads), out_shape=shape((ho...  4.07 us
    another operation x2, local copies, waits for them, and re-layouts, on_device(): cosine = jnp.tile(jnp.cos(angles), (1, width // half))  3.27 us
  transfers between devices with their start and end apart: 28, of which 14 were waited for; matrix products, arithmetic and copies ran while one was open for 18% of the time, Pallas kernels for 8%

profile of v1, /device:TPU:0, one launch (start us, length us, event | category | flops | bytes accessed | tf_op | source)
XLA Modules:
  0.0 117.6 jit_solution(8703081144983267063)
XLA Ops:
  0.6 1.2 %fusion = f32[32]{0:T(128)S(1)} fusion(bf16[32,2048]{1,0:T(8,128)(2,1)} %param.11), kind=kLoop, calls=%fused_computation.10 | loop fusion | flops 196576 | bytes 131200 | tf_op jit(solution)/shard_map/reduce_sum | solution.py:78
  1.8 0.7 convert_element_type.182
  2.5 1.7 %fusion.2.refs_0_ = bf16[32,2048]{1,0:T(8,128)(2,1)} fusion(bf16[32,2048]{1,0:T(8,128)(2,1)} %param.11, f32[2048]{0:T(1024)S(1)} %convert_element_type.182, f32[32]{0:T(128)S(1)} %add_rsqrt_fusion.1), kind=kLoop, calls=%fused_computation.12 | loop fusion | flops 262144 | bytes 270464 | tf_op jit(solution)/shard_map/convert_element_type | solution.py:79
  4.2 5.0 %collective-permute-start.5 = (bf16[32,2048]{1,0:T(8,128)(2,1)}, bf16[32,2048]{1,0:T(8,128)(2,1)}, u32[]{:S(2)}, u32[]{:S(2)}) collective-permute-start(bf16[32,2048]{1,0:T(8,128)(2,1)} %fusion.2.refs_0_), channel_id=1, source_target_pairs={{0,6},{1,7},{2,4},{3,5},{4,2},{5,3},{6,0},{7,1},{8,14},{9,15},{10,... | collective-permute-start | bytes 393224 | tf_op jit(solution)/shard_map/ppermute | solution.py:45
  9.2 0.6 collective-permute-start.1
  9.8 0.7 broadcast_compare_fusion.1
  10.5 0.8 dynamic_slice.9
  11.3 0.8 dynamic_slice.10
  12.1 0.7 lt.53
  13.1 0.8 dynamic_slice.11
  14.7 0.7 and_select_fusion
  15.4 0.9 select_reduce_fusion
  17.9 0.8 multiply_sine_fusion
  18.7 0.6 compare_select_fusion.1.starts
  19.3 0.6 compare_select_fusion.refs_4_
  20.0 0.6 add_select_fusion.1
  20.6 0.6 add_select_fusion.refs_11_.slots
  21.1 0.6 fusion.21
  22.0 0.6 collective-permute-start.6
  22.7 0.4 collective-permute-start.2
  23.1 0.6 fusion.23
  23.7 0.7 tile.20
  24.4 1.1 copy.27.refs_10_
  25.5 1.5 %tile.8 = f32[256,8,32]{0,2,1:T(8,128)} broadcast(f32[256,32]{0,1:T(8,128)} %get-tuple-element.56), dimensions={0,2} | broadcast | bytes 294912 | tf_op jit(solution)/shard_map/tile | solution.py:337
  27.0 1.8 %copy.26.refs_9_ = f32[256,256]{1,0:T(8,128)} copy(f32[256,256]{0,1:T(8,128)} %bitcast.102) | data formatting | bytes 524288 | tf_op jit(solution)/shard_map/tile | solution.py:337
  28.8 0.8 pad_add_fusion.1.bounds
  29.6 1.1 copy-done.3
  30.8 0.7 copy-done.7
  31.5 2.6 %qkv.1 = (bf16[128,768]{1,0:T(8,128)(2,1)S(1)}, bf16[48,768]{1,0:T(8,128)(2,1)S(1)}, bf16[48,768]{1,0:T(8,128)(2,1)S(1)}, bf16[48,768]{1,0:T(8,128)(2,1)S(1)}) custom-call(bf16[32,2048]{1,0:T(8,128)(2,1)} %fusion.2.refs_0_, bf16[32,2048]{1,0:T(8,128)(2,1)} %collective-permute-done.refs_1_, bf16[32,2048]{1,0:T(8,128)(2,1)} %collective-permute-done.1.refs_2_, ...), custom_call_target="tpu_custom_call" | custom-call | tf_op jit(solution)/shard_map/qkv/pallas_call | solution.py:342
  34.1 1.8 %collective-permute-start.7 = (bf16[48,768]{1,0:T(8,128)(2,1)S(1)}, bf16[48,768]{1,0:T(8,128)(2,1)S(1)}, u32[]{:S(2)}, u32[]{:S(2)}) collective-permute-start(bf16[48,768]{1,0:T(8,128)(2,1)S(1)} %get-tuple-element.16), channel_id=1, source_target_pairs={{0,8},{8,0},{16,24},{24,16},{1,9},{9,1},{17,25},{25,17},{2,10},{10... | collective-permute-start | bytes 221192 | tf_op jit(solution)/shard_map/ppermute | solution.py:45
  35.9 1.5 %collective-permute-start.8 = (bf16[48,768]{1,0:T(8,128)(2,1)S(1)}, bf16[48,768]{1,0:T(8,128)(2,1)S(1)}, u32[]{:S(2)}, u32[]{:S(2)}) collective-permute-start(bf16[48,768]{1,0:T(8,128)(2,1)S(1)} %get-tuple-element.17), channel_id=1, source_target_pairs={{0,16},{8,24},{16,0},{24,8},{1,17},{9,25},{17,1},{25,9},{2,18},{10... | collective-permute-start | bytes 221192 | tf_op jit(solution)/shard_map/ppermute | solution.py:45
  37.7 0.8 collective-permute-done.7.refs_0_
  38.5 1.7 %collective-permute-done.8.refs_1_ = bf16[48,768]{1,0:T(8,128)(2,1)S(1)} collective-permute-done((bf16[48,768]{1,0:T(8,128)(2,1)S(1)}, bf16[48,768]{1,0:T(8,128)(2,1)S(1)}, u32[]{:S(2)}, u32[]{:S(2)}) %collective-permute-start.8) | collective-permute-done | bytes 73760 | tf_op jit(solution)/shard_map/ppermute | solution.py:45
  40.2 2.4 %collective-permute-done.9.refs_2_ = bf16[48,768]{1,0:T(8,128)(2,1)S(1)} collective-permute-done((bf16[48,768]{1,0:T(8,128)(2,1)S(1)}, bf16[48,768]{1,0:T(8,128)(2,1)S(1)}, u32[]{:S(2)}, u32[]{:S(2)}) %collective-permute-start.9) | collective-permute-done | bytes 73760 | tf_op jit(solution)/shard_map/ppermute | solution.py:45
  42.6 4.4 %far_attention.1 = (bf16[48,384]{1,0:T(8,128)(2,1)S(1)}, bf16[48,384]{1,0:T(8,128)(2,1)S(1)}, bf16[48,384]{1,0:T(8,128)(2,1)S(1)}) custom-call(s32[2,5]{1,0:T(2,128)S(1)} %pad_add_fusion.1.bounds, bf16[48,768]{1,0:T(8,128)(2,1)S(1)} %collective-permute-done.7.refs_0_, bf16[48,768]{1,0:T(8,128)(2,1)S(1)} %collective-permute-done.8.refs_1_, ...), custom_call_target="tpu_custom_call" | custom-call | tf_op jit(solution)/shard_map/far_attention/pallas_call | solution.py:364
  47.0 3.7 %collective-permute-start.10 = (bf16[48,384]{1,0:T(8,128)(2,1)S(1)}, bf16[48,384]{1,0:T(8,128)(2,1)S(1)}, u32[]{:S(2)}, u32[]{:S(2)}) collective-permute-start(bf16[48,384]{1,0:T(8,128)(2,1)S(1)} %get-tuple-element.19), channel_id=1, source_target_pairs={{0,8},{8,0},{16,24},{24,16},{1,9},{9,1},{17,25},{25,17},{2,10},{10... | collective-permute-start | bytes 110600 | tf_op jit(solution)/shard_map/ppermute | solution.py:45
  50.7 1.5 %collective-permute-start.12 = (bf16[48,384]{1,0:T(8,128)(2,1)S(1)}, bf16[48,384]{1,0:T(8,128)(2,1)S(1)}, u32[]{:S(2)}, u32[]{:S(2)}) collective-permute-start(bf16[48,384]{1,0:T(8,128)(2,1)S(1)} %get-tuple-element.21), channel_id=1, source_target_pairs={{0,24},{8,16},{16,8},{24,0},{1,25},{9,17},{17,9},{25,1},{2,26},{10... | collective-permute-start | bytes 110600 | tf_op jit(solution)/shard_map/ppermute | solution.py:45
  52.3 4.1 %home_attention.1.home = bf16[128,384]{1,0:T(8,128)(2,1)S(1)} custom-call(s32[2,4]{1,0:T(2,128)S(1)} %pad_add_fusion.bounds, bf16[128,768]{1,0:T(8,128)(2,1)S(1)} %get-tuple-element.15.packed.home, s32[128,1]{1,0:T(8,128)S(1)} %copy-done.6, s32[128,1]{1,0:T(8,128)S(1)} %copy.28.spans, bf16[2,4096,256]{2,1,0:T(8,128)(2,1)S(1)} %copy-done), custom_call_target="tpu_custom_call" | custom-call | flops 2000000000 | bytes 4194304 | tf_op jit(solution)/shard_map/home_attention/pallas_call | solution.py:355
  56.4 0.6 project_out.1
  57.2 1.9 %collective-permute-done.13 = bf16[4,32,2048]{2,1,0:T(8,128)(2,1)S(1)} collective-permute-done((bf16[4,32,2048]{2,1,0:T(8,128)(2,1)S(1)}, bf16[4,32,2048]{2,1,0:T(8,128)(2,1)S(1)}, u32[]{:S(2)}, u32[]{:S(2)}) %collective-permute-start.13) | collective-permute-done | bytes 524320 | tf_op jit(solution)/shard_map/ppermute | solution.py:45
  59.2 1.3 %collective-permute-start.14 = (bf16[32,2048]{1,0:T(8,128)(2,1)S(1)}, bf16[32,2048]{1,0:T(8,128)(2,1)S(1)}, u32[]{:S(2)}, u32[]{:S(2)}) collective-permute-start(bf16[32,2048]{1,0:T(8,128)(2,1)S(1)} %get-tuple-element.52), channel_id=1, source_target_pairs={{0,2},{1,3},{2,0},{3,1},{4,6},{5,7},{6,4},{7,5},{8,10},{9,11},{10,... | collective-permute-start | bytes 393224 | tf_op jit(solution)/shard_map/ppermute | solution.py:45
  60.5 2.4 %collective-permute-start.16 = (bf16[32,2048]{1,0:T(8,128)(2,1)S(1)}, bf16[32,2048]{1,0:T(8,128)(2,1)S(1)}, u32[]{:S(2)}, u32[]{:S(2)}) collective-permute-start(bf16[32,2048]{1,0:T(8,128)(2,1)S(1)} %get-tuple-element.53), channel_id=1, source_target_pairs={{0,6},{1,7},{2,4},{3,5},{4,2},{5,3},{6,0},{7,1},{8,14},{9,15},{10,... | collective-permute-start | bytes 393224 | tf_op jit(solution)/shard_map/ppermute | solution.py:45
  62.9 0.5 collective-permute-start.15
  63.4 1.4 %collective-permute-done.14 = bf16[32,2048]{1,0:T(8,128)(2,1)S(1)} collective-permute-done((bf16[32,2048]{1,0:T(8,128)(2,1)S(1)}, bf16[32,2048]{1,0:T(8,128)(2,1)S(1)}, u32[]{:S(2)}, u32[]{:S(2)}) %collective-permute-start.14) | collective-permute-done | bytes 131104 | tf_op jit(solution)/shard_map/ppermute | solution.py:45
  64.8 5.3 %collective-permute-done.16 = bf16[32,2048]{1,0:T(8,128)(2,1)S(1)} collective-permute-done((bf16[32,2048]{1,0:T(8,128)(2,1)S(1)}, bf16[32,2048]{1,0:T(8,128)(2,1)S(1)}, u32[]{:S(2)}, u32[]{:S(2)}) %collective-permute-start.16) | collective-permute-done | bytes 131104 | tf_op jit(solution)/shard_map/ppermute | solution.py:45
  70.0 5.3 %collective-permute-done.15 = bf16[32,2048]{1,0:T(8,128)(2,1)S(1)} collective-permute-done((bf16[32,2048]{1,0:T(8,128)(2,1)S(1)}, bf16[32,2048]{1,0:T(8,128)(2,1)S(1)}, u32[]{:S(2)}, u32[]{:S(2)}) %collective-permute-start.15) | collective-permute-done | bytes 131104 | tf_op jit(solution)/shard_map/ppermute | solution.py:45
  75.7 2.7 %collective-permute-start.22 = (bf16[32,2048]{1,0:T(8,128)(2,1)S(1)}, bf16[32,2048]{1,0:T(8,128)(2,1)S(1)}, u32[]{:S(2)}, u32[]{:S(2)}) collective-permute-start(bf16[32,2048]{1,0:T(8,128)(2,1)S(1)} %fusion.6.refs_0_), channel_id=1, source_target_pairs={{0,6},{1,7},{2,4},{3,5},{4,2},{5,3},{6,0},{7,1},{8,14},{9,15},{10,... | collective-permute-start | bytes 393224 | tf_op jit(solution)/shard_map/ppermute | solution.py:45
  78.4 1.7 %collective-permute-start.18 = (bf16[32,2048]{1,0:T(8,128)(2,1)S(1)}, bf16[32,2048]{1,0:T(8,128)(2,1)S(1)}, u32[]{:S(2)}, u32[]{:S(2)}) collective-permute-start(bf16[32,2048]{1,0:T(8,128)(2,1)S(1)} %fusion.6.refs_0_), channel_id=1, source_target_pairs={{0,2},{1,3},{2,0},{3,1},{4,6},{5,7},{6,4},{7,5},{8,10},{9,11},{10,... | collective-permute-start | bytes 393224 | tf_op jit(solution)/shard_map/ppermute | solution.py:45
  80.1 5.6 %cache_update.1 = bf16[2,4096,256]{2,1,0:T(8,128)(2,1)} custom-call(s32[1,128]{1,0:T(1,128)S(1)} %compare_select_fusion.15.home_rows, s32[1,144]{1,0:T(1,128)S(1)} %copy-done.8, bf16[128,768]{1,0:T(8,128)(2,1)S(1)} %get-tuple-element.15.packed.home, bf16[48,768]{1,0:T(8,128)(2,1)S(1)} %collective-permute-done.7.refs_0_, ...), custom_call_target="tpu_custom_call" | custom-call | flops 2000000000 | bytes 8388608 | tf_op jit(solution)/shard_map/cache_update/pallas_call | solution.py:378
  85.8 1.0 rev.45
  86.9 0.5 collective-permute-start.23
  87.4 1.0 collective-permute-done.20.refs_4_
  88.4 0.5 collective-permute-start.19
  89.0 0.8 collective-permute-done.21.refs_5_
  89.9 2.2 %copy-done.1 = bf16[1024,2048]{1,0:T(8,128)(2,1)S(1)} copy-done((bf16[1024,2048]{1,0:T(8,128)(2,1)S(1)}, bf16[1024,2048]{1,0:T(8,128)(2,1)}, u32[]{:S(2)}) %copy-start.1) | copy-done | bytes 4194328
  92.1 7.3 %mlp.1 = (bf16[4,32,2048]{2,1,0:T(8,128)(2,1)S(1)}, bf16[4,32,2048]{2,1,0:T(8,128)(2,1)S(1)}) custom-call(bf16[32,2048]{1,0:T(8,128)(2,1)S(1)} %fusion.6.refs_0_, bf16[32,2048]{1,0:T(8,128)(2,1)S(1)} %collective-permute-done.17.refs_1_, bf16[32,2048]{1,0:T(8,128)(2,1)S(1)} %collective-permute-done.18.refs_2_, ...), custom_call_target="tpu_custom_call" | custom-call | tf_op jit(solution)/shard_map/mlp/pallas_call | solution.py:410
  100.0 1.4 %collective-permute-done.24 = bf16[4,32,2048]{2,1,0:T(8,128)(2,1)S(1)} collective-permute-done((bf16[4,32,2048]{2,1,0:T(8,128)(2,1)S(1)}, bf16[4,32,2048]{2,1,0:T(8,128)(2,1)S(1)}, u32[]{:S(2)}, u32[]{:S(2)}) %collective-permute-start.24) | collective-permute-done | bytes 524320 | tf_op jit(solution)/shard_map/ppermute | solution.py:45
  101.6 2.0 %collective-permute-start.27 = (bf16[32,2048]{1,0:T(8,128)(2,1)S(1)}, bf16[32,2048]{1,0:T(8,128)(2,1)S(1)}, u32[]{:S(2)}, u32[]{:S(2)}) collective-permute-start(bf16[32,2048]{1,0:T(8,128)(2,1)S(1)} %get-tuple-element.50), channel_id=1, source_target_pairs={{0,6},{1,7},{2,4},{3,5},{4,2},{5,3},{6,0},{7,1},{8,14},{9,15},{10,... | collective-permute-start | bytes 393224 | tf_op jit(solution)/shard_map/ppermute | solution.py:45
  103.6 1.5 %collective-permute-start.26 = (bf16[32,2048]{1,0:T(8,128)(2,1)S(1)}, bf16[32,2048]{1,0:T(8,128)(2,1)S(1)}, u32[]{:S(2)}, u32[]{:S(2)}) collective-permute-start(bf16[32,2048]{1,0:T(8,128)(2,1)S(1)} %get-tuple-element.51), channel_id=1, source_target_pairs={{0,4},{1,5},{2,6},{3,7},{4,0},{5,1},{6,2},{7,3},{8,12},{9,13},{10,... | collective-permute-start | bytes 393224 | tf_op jit(solution)/shard_map/ppermute | solution.py:45
  105.2 0.7 copy.34
  105.9 1.5 %collective-permute-done.25 = bf16[32,2048]{1,0:T(8,128)(2,1)S(1)} collective-permute-done((bf16[32,2048]{1,0:T(8,128)(2,1)S(1)}, bf16[32,2048]{1,0:T(8,128)(2,1)S(1)}, u32[]{:S(2)}, u32[]{:S(2)}) %collective-permute-start.25) | collective-permute-done | bytes 131104 | tf_op jit(solution)/shard_map/ppermute | solution.py:45
  107.3 3.4 %collective-permute-done.27 = bf16[32,2048]{1,0:T(8,128)(2,1)S(1)} collective-permute-done((bf16[32,2048]{1,0:T(8,128)(2,1)S(1)}, bf16[32,2048]{1,0:T(8,128)(2,1)S(1)}, u32[]{:S(2)}, u32[]{:S(2)}) %collective-permute-start.27) | collective-permute-done | bytes 131104 | tf_op jit(solution)/shard_map/ppermute | solution.py:45
  110.7 6.2 %collective-permute-done.26 = bf16[32,2048]{1,0:T(8,128)(2,1)S(1)} collective-permute-done((bf16[32,2048]{1,0:T(8,128)(2,1)S(1)}, bf16[32,2048]{1,0:T(8,128)(2,1)S(1)}, u32[]{:S(2)}, u32[]{:S(2)}) %collective-permute-start.26) | collective-permute-done | bytes 131104 | tf_op jit(solution)/shard_map/ppermute | solution.py:45
  116.9 0.8 fusion.7
  (121 shorter events, 5.2 us)
Async XLA Ops:
  0.6 29.0 %copy-start.2 = (bf16[3,2048,256]{2,1,0:T(8,128)(2,1)S(1)}, bf16[3,2048,256]{2,1,0:T(8,128)(2,1)}, u32[]{:S(2)}) copy-start(bf16[3,2048,256]{2,1,0:T(8,128)(2,1)} %refs_8_.2) | copy-start | bytes 9437188
  4.2 17.8 %collective-permute-start.5 = (bf16[32,2048]{1,0:T(8,128)(2,1)}, bf16[32,2048]{1,0:T(8,128)(2,1)}, u32[]{:S(2)}, u32[]{:S(2)}) collective-permute-start(bf16[32,2048]{1,0:T(8,128)(2,1)} %fusion.2.refs_0_), channel_id=1, source_target_pairs={{0,6},{1,7},{2,4},{3,5},{4,2},{5,3},{6,0},{7,1},{8,14},{9,15},{10,... | collective-permute-start | bytes 393224 | tf_op jit(solution)/shard_map/ppermute | solution.py:45
  9.2 13.3 %collective-permute-start.3 = (bf16[32,2048]{1,0:T(8,128)(2,1)}, bf16[32,2048]{1,0:T(8,128)(2,1)}, u32[]{:S(2)}, u32[]{:S(2)}) collective-permute-start(bf16[32,2048]{1,0:T(8,128)(2,1)} %fusion.2.refs_0_), channel_id=1, source_target_pairs={{0,4},{1,5},{2,6},{3,7},{4,0},{5,1},{6,2},{7,3},{8,12},{9,13},{10,... | collective-permute-start | bytes 393224 | tf_op jit(solution)/shard_map/ppermute | solution.py:45
  9.2 13.4 %collective-permute-start.1 = (bf16[32,2048]{1,0:T(8,128)(2,1)}, bf16[32,2048]{1,0:T(8,128)(2,1)}, u32[]{:S(2)}, u32[]{:S(2)}) collective-permute-start(bf16[32,2048]{1,0:T(8,128)(2,1)} %fusion.2.refs_0_), channel_id=1, source_target_pairs={{0,2},{1,3},{2,0},{3,1},{4,6},{5,7},{6,4},{7,5},{8,10},{9,11},{10,... | collective-permute-start | bytes 393224 | tf_op jit(solution)/shard_map/ppermute | solution.py:45
  9.8 19.8 %collective-permute-start = (bf16[32,2048]{1,0:T(8,128)(2,1)}, bf16[32,2048]{1,0:T(8,128)(2,1)}, u32[]{:S(2)}, u32[]{:S(2)}) collective-permute-start(bf16[32,2048]{1,0:T(8,128)(2,1)} %fusion.2.refs_0_), channel_id=1, source_target_pairs={{0,1},{1,0},{2,3},{3,2},{4,5},{5,4},{6,7},{7,6},{8,9},{9,8},{10,11... | collective-permute-start | bytes 393224 | tf_op jit(solution)/shard_map/ppermute | solution.py:45
  17.3 7.1 %copy-start.11 = (s32[128]{0:T(128)}, s32[128]{0:T(128)S(1)}, u32[]{:S(2)}) copy-start(s32[128]{0:T(128)S(1)} %get-tuple-element.41) | copy-start | bytes 1540
  17.3 7.1 %copy-start.13 = (s32[128]{0:T(128)}, s32[128]{0:T(128)S(1)}, u32[]{:S(2)}) copy-start(s32[128]{0:T(128)S(1)} %get-tuple-element.42) | copy-start | bytes 1540
  22.0 7.6 %collective-permute-start.6 = (bf16[32,2048]{1,0:T(8,128)(2,1)}, bf16[32,2048]{1,0:T(8,128)(2,1)}, u32[]{:S(2)}, u32[]{:S(2)}) collective-permute-start(bf16[32,2048]{1,0:T(8,128)(2,1)} %collective-permute-done.5.refs_6_), channel_id=1, source_target_pairs={{0,1},{1,0},{2,3},{3,2},{4,5},{5,4},{6,7},{7,6},{8,9},{9,8},{10,11... | collective-permute-start | bytes 393224 | tf_op jit(solution)/shard_map/ppermute | solution.py:45
  22.6 7.0 %collective-permute-start.4 = (bf16[32,2048]{1,0:T(8,128)(2,1)}, bf16[32,2048]{1,0:T(8,128)(2,1)}, u32[]{:S(2)}, u32[]{:S(2)}) collective-permute-start(bf16[32,2048]{1,0:T(8,128)(2,1)} %collective-permute-done.3.refs_4_), channel_id=1, source_target_pairs={{0,1},{1,0},{2,3},{3,2},{4,5},{5,4},{6,7},{7,6},{8,9},{9,8},{10,11... | collective-permute-start | bytes 393224 | tf_op jit(solution)/shard_map/ppermute | solution.py:45
  22.7 6.9 %collective-permute-start.2 = (bf16[32,2048]{1,0:T(8,128)(2,1)}, bf16[32,2048]{1,0:T(8,128)(2,1)}, u32[]{:S(2)}, u32[]{:S(2)}) collective-permute-start(bf16[32,2048]{1,0:T(8,128)(2,1)} %collective-permute-done.1.refs_2_), channel_id=1, source_target_pairs={{0,1},{1,0},{2,3},{3,2},{4,5},{5,4},{6,7},{7,6},{8,9},{9,8},{10,11... | collective-permute-start | bytes 393224 | tf_op jit(solution)/shard_map/ppermute | solution.py:45
  28.8 13.9 %copy-start = (bf16[2,4096,256]{2,1,0:T(8,128)(2,1)S(1)}, bf16[2,4096,256]{2,1,0:T(8,128)(2,1)}, u32[]{:S(2)}) copy-start(bf16[2,4096,256]{2,1,0:T(8,128)(2,1)} %refs_3_.3) | copy-start | bytes 12582916
  29.6 1.1 copy-start.3
  30.8 0.7 copy-start.7
  31.4 6.2 %copy-start.16 = (s32[1,4]{1,0:T(1,128)S(1)}, s32[1,4]{1,0:T(1,128)}, u32[]{:S(2)}) copy-start(s32[1,4]{1,0:T(1,128)} %get-tuple-element.61) | copy-start | bytes 52
  31.4 6.2 %copy-start.17 = (s32[1,4]{1,0:T(1,128)S(1)}, s32[1,4]{1,0:T(1,128)}, u32[]{:S(2)}) copy-start(s32[1,4]{1,0:T(1,128)} %get-tuple-element.62) | copy-start | bytes 52
  31.4 11.2 %copy-start.5 = (s32[160,1]{1,0:T(8,128)S(1)}, s32[160,1]{1,0:T(8,128)}, u32[]{:S(2)}) copy-start(s32[160,1]{1,0:T(8,128)} %compare_select_fusion.refs_4_) | copy-start | bytes 1924
  31.4 11.2 %copy-start.9 = (s32[1,144]{1,0:T(1,128)S(1)}, s32[1,144]{1,0:T(1,128)}, u32[]{:S(2)}) copy-start(s32[1,144]{1,0:T(1,128)} %get-tuple-element.58.refs_3_) | copy-start | bytes 1732
  31.4 20.8 %copy-start.6 = (s32[128,1]{1,0:T(8,128)S(1)}, s32[128,1]{1,0:T(8,128)}, u32[]{:S(2)}) copy-start(s32[128,1]{1,0:T(8,128)} %compare_select_fusion.1.starts) | copy-start | bytes 1540
  34.1 4.4 %collective-permute-start.7 = (bf16[48,768]{1,0:T(8,128)(2,1)S(1)}, bf16[48,768]{1,0:T(8,128)(2,1)S(1)}, u32[]{:S(2)}, u32[]{:S(2)}) collective-permute-start(bf16[48,768]{1,0:T(8,128)(2,1)S(1)} %get-tuple-element.16), channel_id=1, source_target_pairs={{0,8},{8,0},{16,24},{24,16},{1,9},{9,1},{17,25},{25,17},{2,10},{10... | collective-permute-start | bytes 221192 | tf_op jit(solution)/shard_map/ppermute | solution.py:45
  35.9 4.4 %collective-permute-start.8 = (bf16[48,768]{1,0:T(8,128)(2,1)S(1)}, bf16[48,768]{1,0:T(8,128)(2,1)S(1)}, u32[]{:S(2)}, u32[]{:S(2)}) collective-permute-start(bf16[48,768]{1,0:T(8,128)(2,1)S(1)} %get-tuple-element.17), channel_id=1, source_target_pairs={{0,16},{8,24},{16,0},{24,8},{1,17},{9,25},{17,1},{25,9},{2,18},{10... | collective-permute-start | bytes 221192 | tf_op jit(solution)/shard_map/ppermute | solution.py:45
  37.4 5.3 %collective-permute-start.9 = (bf16[48,768]{1,0:T(8,128)(2,1)S(1)}, bf16[48,768]{1,0:T(8,128)(2,1)S(1)}, u32[]{:S(2)}, u32[]{:S(2)}) collective-permute-start(bf16[48,768]{1,0:T(8,128)(2,1)S(1)} %get-tuple-element.18), channel_id=1, source_target_pairs={{0,24},{8,16},{16,8},{24,0},{1,25},{9,17},{17,9},{25,1},{2,26},{10... | collective-permute-start | bytes 221192 | tf_op jit(solution)/shard_map/ppermute | solution.py:45
  47.0 9.4 %copy-start.4 = (bf16[256,2048]{1,0:T(8,128)(2,1)S(1)}, bf16[256,2048]{1,0:T(8,128)(2,1)}, u32[]{:S(2)}) copy-start(bf16[256,2048]{1,0:T(8,128)(2,1)} %refs_3_.2) | copy-start | bytes 3145732
  47.0 9.4 %collective-permute-start.10 = (bf16[48,384]{1,0:T(8,128)(2,1)S(1)}, bf16[48,384]{1,0:T(8,128)(2,1)S(1)}, u32[]{:S(2)}, u32[]{:S(2)}) collective-permute-start(bf16[48,384]{1,0:T(8,128)(2,1)S(1)} %get-tuple-element.19), channel_id=1, source_target_pairs={{0,8},{8,0},{16,24},{24,16},{1,9},{9,1},{17,25},{25,17},{2,10},{10... | collective-permute-start | bytes 110600 | tf_op jit(solution)/shard_map/ppermute | solution.py:45
  50.7 5.7 %collective-permute-start.11 = (bf16[48,384]{1,0:T(8,128)(2,1)S(1)}, bf16[48,384]{1,0:T(8,128)(2,1)S(1)}, u32[]{:S(2)}, u32[]{:S(2)}) collective-permute-start(bf16[48,384]{1,0:T(8,128)(2,1)S(1)} %get-tuple-element.20), channel_id=1, source_target_pairs={{0,16},{8,24},{16,0},{24,8},{1,17},{9,25},{17,1},{25,9},{2,18},{10... | collective-permute-start | bytes 110600 | tf_op jit(solution)/shard_map/ppermute | solution.py:45
  50.7 5.7 %collective-permute-start.12 = (bf16[48,384]{1,0:T(8,128)(2,1)S(1)}, bf16[48,384]{1,0:T(8,128)(2,1)S(1)}, u32[]{:S(2)}, u32[]{:S(2)}) collective-permute-start(bf16[48,384]{1,0:T(8,128)(2,1)S(1)} %get-tuple-element.21), channel_id=1, source_target_pairs={{0,24},{8,16},{16,8},{24,0},{1,25},{9,17},{17,9},{25,1},{2,26},{10... | collective-permute-start | bytes 110600 | tf_op jit(solution)/shard_map/ppermute | solution.py:45
  52.3 4.9 %copy-start.15 = (bf16[2048]{0:T(1024)(128)(2,1)S(1)}, bf16[2048]{0:T(1024)(128)(2,1)}, u32[]{:S(2)}) copy-start(bf16[2048]{0:T(1024)(128)(2,1)} %param.13) | copy-start | bytes 12292
  52.3 11.1 %copy-start.12 = (s32[128]{0:T(128)S(1)}, s32[128]{0:T(128)}, u32[]{:S(2)}) copy-start(s32[128]{0:T(128)} %copy-done.11) | copy-start | bytes 1540
  52.3 11.1 %copy-start.14 = (s32[128]{0:T(128)S(1)}, s32[128]{0:T(128)}, u32[]{:S(2)}) copy-start(s32[128]{0:T(128)} %copy-done.13) | copy-start | bytes 1540
  52.3 23.0 %copy-start.10 = (bf16[32,2048]{1,0:T(8,128)(2,1)S(1)}, bf16[32,2048]{1,0:T(8,128)(2,1)}, u32[]{:S(2)}) copy-start(bf16[32,2048]{1,0:T(8,128)(2,1)} %param.11) | copy-start | bytes 393220
  52.3 27.8 %copy-start.8 = (s32[1,144]{1,0:T(1,128)S(1)}, s32[1,144]{1,0:T(1,128)}, u32[]{:S(2)}) copy-start(s32[1,144]{1,0:T(1,128)} %get-tuple-element.57.far_rows) | copy-start | bytes 1732
  57.1 2.0 %collective-permute-start.13 = (bf16[4,32,2048]{2,1,0:T(8,128)(2,1)S(1)}, bf16[4,32,2048]{2,1,0:T(8,128)(2,1)S(1)}, u32[]{:S(2)}, u32[]{:S(2)}) collective-permute-start(bf16[4,32,2048]{2,1,0:T(8,128)(2,1)S(1)} %get-tuple-element.23), channel_id=1, source_target_pairs={{0,1},{1,0},{2,3},{3,2},{4,5},{5,4},{6,7},{7,6},{8,9},{9,8},{10,11... | collective-permute-start | bytes 1572872 | tf_op jit(solution)/shard_map/ppermute | solution.py:45
  59.2 5.6 %collective-permute-start.14 = (bf16[32,2048]{1,0:T(8,128)(2,1)S(1)}, bf16[32,2048]{1,0:T(8,128)(2,1)S(1)}, u32[]{:S(2)}, u32[]{:S(2)}) collective-permute-start(bf16[32,2048]{1,0:T(8,128)(2,1)S(1)} %get-tuple-element.52), channel_id=1, source_target_pairs={{0,2},{1,3},{2,0},{3,1},{4,6},{5,7},{6,4},{7,5},{8,10},{9,11},{10,... | collective-permute-start | bytes 393224 | tf_op jit(solution)/shard_map/ppermute | solution.py:45
  60.5 9.5 %collective-permute-start.16 = (bf16[32,2048]{1,0:T(8,128)(2,1)S(1)}, bf16[32,2048]{1,0:T(8,128)(2,1)S(1)}, u32[]{:S(2)}, u32[]{:S(2)}) collective-permute-start(bf16[32,2048]{1,0:T(8,128)(2,1)S(1)} %get-tuple-element.53), channel_id=1, source_target_pairs={{0,6},{1,7},{2,4},{3,5},{4,2},{5,3},{6,0},{7,1},{8,14},{9,15},{10,... | collective-permute-start | bytes 393224 | tf_op jit(solution)/shard_map/ppermute | solution.py:45
  62.9 12.4 %collective-permute-start.15 = (bf16[32,2048]{1,0:T(8,128)(2,1)S(1)}, bf16[32,2048]{1,0:T(8,128)(2,1)S(1)}, u32[]{:S(2)}, u32[]{:S(2)}) collective-permute-start(bf16[32,2048]{1,0:T(8,128)(2,1)S(1)} %get-tuple-element.54), channel_id=1, source_target_pairs={{0,4},{1,5},{2,6},{3,7},{4,0},{5,1},{6,2},{7,3},{8,12},{9,13},{10,... | collective-permute-start | bytes 393224 | tf_op jit(solution)/shard_map/ppermute | solution.py:45
  75.7 11.2 %collective-permute-start.22 = (bf16[32,2048]{1,0:T(8,128)(2,1)S(1)}, bf16[32,2048]{1,0:T(8,128)(2,1)S(1)}, u32[]{:S(2)}, u32[]{:S(2)}) collective-permute-start(bf16[32,2048]{1,0:T(8,128)(2,1)S(1)} %fusion.6.refs_0_), channel_id=1, source_target_pairs={{0,6},{1,7},{2,4},{3,5},{4,2},{5,3},{6,0},{7,1},{8,14},{9,15},{10,... | collective-permute-start | bytes 393224 | tf_op jit(solution)/shard_map/ppermute | solution.py:45
  78.4 10.0 %collective-permute-start.20 = (bf16[32,2048]{1,0:T(8,128)(2,1)S(1)}, bf16[32,2048]{1,0:T(8,128)(2,1)S(1)}, u32[]{:S(2)}, u32[]{:S(2)}) collective-permute-start(bf16[32,2048]{1,0:T(8,128)(2,1)S(1)} %fusion.6.refs_0_), channel_id=1, source_target_pairs={{0,4},{1,5},{2,6},{3,7},{4,0},{5,1},{6,2},{7,3},{8,12},{9,13},{10,... | collective-permute-start | bytes 393224 | tf_op jit(solution)/shard_map/ppermute | solution.py:45
  78.4 10.0 %collective-permute-start.18 = (bf16[32,2048]{1,0:T(8,128)(2,1)S(1)}, bf16[32,2048]{1,0:T(8,128)(2,1)S(1)}, u32[]{:S(2)}, u32[]{:S(2)}) collective-permute-start(bf16[32,2048]{1,0:T(8,128)(2,1)S(1)} %fusion.6.refs_0_), channel_id=1, source_target_pairs={{0,2},{1,3},{2,0},{3,1},{4,6},{5,7},{6,4},{7,5},{8,10},{9,11},{10,... | collective-permute-start | bytes 393224 | tf_op jit(solution)/shard_map/ppermute | solution.py:45
  86.8 2.1 %collective-permute-start.17 = (bf16[32,2048]{1,0:T(8,128)(2,1)S(1)}, bf16[32,2048]{1,0:T(8,128)(2,1)S(1)}, u32[]{:S(2)}, u32[]{:S(2)}) collective-permute-start(bf16[32,2048]{1,0:T(8,128)(2,1)S(1)} %fusion.6.refs_0_), channel_id=1, source_target_pairs={{0,1},{1,0},{2,3},{3,2},{4,5},{5,4},{6,7},{7,6},{8,9},{9,8},{10,11... | collective-permute-start | bytes 393224 | tf_op jit(solution)/shard_map/ppermute | solution.py:45
  86.9 2.0 %collective-permute-start.23 = (bf16[32,2048]{1,0:T(8,128)(2,1)S(1)}, bf16[32,2048]{1,0:T(8,128)(2,1)S(1)}, u32[]{:S(2)}, u32[]{:S(2)}) collective-permute-start(bf16[32,2048]{1,0:T(8,128)(2,1)S(1)} %collective-permute-done.22.refs_6_), channel_id=1, source_target_pairs={{0,1},{1,0},{2,3},{3,2},{4,5},{5,4},{6,7},{7,6},{8,9},{9,8},{10,11... | collective-permute-start | bytes 393224 | tf_op jit(solution)/shard_map/ppermute | solution.py:45
  88.4 1.3 %collective-permute-start.21 = (bf16[32,2048]{1,0:T(8,128)(2,1)S(1)}, bf16[32,2048]{1,0:T(8,128)(2,1)S(1)}, u32[]{:S(2)}, u32[]{:S(2)}) collective-permute-start(bf16[32,2048]{1,0:T(8,128)(2,1)S(1)} %collective-permute-done.20.refs_4_), channel_id=1, source_target_pairs={{0,1},{1,0},{2,3},{3,2},{4,5},{5,4},{6,7},{7,6},{8,9},{9,8},{10,11... | collective-permute-start | bytes 393224 | tf_op jit(solution)/shard_map/ppermute | solution.py:45
  88.4 1.5 %collective-permute-start.19 = (bf16[32,2048]{1,0:T(8,128)(2,1)S(1)}, bf16[32,2048]{1,0:T(8,128)(2,1)S(1)}, u32[]{:S(2)}, u32[]{:S(2)}) collective-permute-start(bf16[32,2048]{1,0:T(8,128)(2,1)S(1)} %collective-permute-done.18.refs_2_), channel_id=1, source_target_pairs={{0,1},{1,0},{2,3},{3,2},{4,5},{5,4},{6,7},{7,6},{8,9},{9,8},{10,11... | collective-permute-start | bytes 393224 | tf_op jit(solution)/shard_map/ppermute | solution.py:45
  89.9 2.2 %copy-start.1 = (bf16[1024,2048]{1,0:T(8,128)(2,1)S(1)}, bf16[1024,2048]{1,0:T(8,128)(2,1)}, u32[]{:S(2)}) copy-start(bf16[1024,2048]{1,0:T(8,128)(2,1)} %refs_9_.1) | copy-start | bytes 12582916
  99.4 2.0 %collective-permute-start.24 = (bf16[4,32,2048]{2,1,0:T(8,128)(2,1)S(1)}, bf16[4,32,2048]{2,1,0:T(8,128)(2,1)S(1)}, u32[]{:S(2)}, u32[]{:S(2)}) collective-permute-start(bf16[4,32,2048]{2,1,0:T(8,128)(2,1)S(1)} %get-tuple-element.25), channel_id=1, source_target_pairs={{0,1},{1,0},{2,3},{3,2},{4,5},{5,4},{6,7},{7,6},{8,9},{9,8},{10,11... | collective-permute-start | bytes 1572872 | tf_op jit(solution)/shard_map/ppermute | solution.py:45
  101.5 5.8 %collective-permute-start.25 = (bf16[32,2048]{1,0:T(8,128)(2,1)S(1)}, bf16[32,2048]{1,0:T(8,128)(2,1)S(1)}, u32[]{:S(2)}, u32[]{:S(2)}) collective-permute-start(bf16[32,2048]{1,0:T(8,128)(2,1)S(1)} %get-tuple-element.49), channel_id=1, source_target_pairs={{0,2},{1,3},{2,0},{3,1},{4,6},{5,7},{6,4},{7,5},{8,10},{9,11},{10,... | collective-permute-start | bytes 393224 | tf_op jit(solution)/shard_map/ppermute | solution.py:45
  101.6 9.1 %collective-permute-start.27 = (bf16[32,2048]{1,0:T(8,128)(2,1)S(1)}, bf16[32,2048]{1,0:T(8,128)(2,1)S(1)}, u32[]{:S(2)}, u32[]{:S(2)}) collective-permute-start(bf16[32,2048]{1,0:T(8,128)(2,1)S(1)} %get-tuple-element.50), channel_id=1, source_target_pairs={{0,6},{1,7},{2,4},{3,5},{4,2},{5,3},{6,0},{7,1},{8,14},{9,15},{10,... | collective-permute-start | bytes 393224 | tf_op jit(solution)/shard_map/ppermute | solution.py:45
  103.6 13.3 %collective-permute-start.26 = (bf16[32,2048]{1,0:T(8,128)(2,1)S(1)}, bf16[32,2048]{1,0:T(8,128)(2,1)S(1)}, u32[]{:S(2)}, u32[]{:S(2)}) collective-permute-start(bf16[32,2048]{1,0:T(8,128)(2,1)S(1)} %get-tuple-element.51), channel_id=1, source_target_pairs={{0,4},{1,5},{2,6},{3,7},{4,0},{5,1},{6,2},{7,3},{8,12},{9,13},{10,... | collective-permute-start | bytes 393224 | tf_op jit(solution)/shard_map/ppermute | solution.py:45

commit v2 on v1

v2 whole, which is shorter than its diff:
```python
import functools
import math

import jax
import jax.numpy as jnp
from jax import lax
from jax.experimental import pallas as pl
from jax.experimental.pallas import tpu as pltpu
from jax.sharding import PartitionSpec as P

HD = 64
NORM_EPS = 1e-05
ROPE_BASE = 130000.0
MASK_LOW = -1e30
BF = jnp.bfloat16
F32 = jnp.float32
LANES = 128
Q_TILE = 32
P_TILE = 512


def round_up(count, step):
    return (count + step - 1) // step * step


def dot(left, right):
    return jnp.dot(left, right, preferred_element_type=F32)


def dot_nt(left, right):
    return lax.dot_general(left, right, (((1,), (1,)), ((), ())), preferred_element_type=F32)


def dot_tn(left, right):
    return lax.dot_general(left, right, (((0,), (0,)), ((), ())), preferred_element_type=F32)


def one_hot(row_count, slots):
    rows = lax.broadcasted_iota(jnp.int32, (row_count, slots.shape[1]), 0)
    return jnp.where(rows == slots, 1.0, 0.0).astype(BF)


def swap(values, axis_name, offset):
    count = lax.axis_size(axis_name)
    return lax.ppermute(values, axis_name, [(i, i ^ offset) for i in range(count)])


def gather_tensor(block, beside=None):
    count = lax.axis_size("tensor")
    pieces = [None] * count
    pieces[0] = block
    for k in range(2, count, 2):
        pieces[k] = swap(block, "tensor", k)
    if beside is not None:
        pieces[::2], done = lax.optimization_barrier((pieces[::2], beside()))
    for k in range(0, count, 2):
        pieces[k + 1] = swap(pieces[k], "tensor", 1)
    return pieces if beside is None else (pieces, done)


def reduce_tensor(keep, send):
    count = lax.axis_size("tensor")
    came = swap(send, "tensor", 1)
    joined = [(keep[k].astype(F32) + came[k].astype(F32)).astype(BF) for k in range(count // 2)]
    return [joined[0]] + [swap(joined[k], "tensor", 2 * k) for k in range(1, count // 2)]


def norm_kernel(tokens, gain, result):
    wide = tokens[...].astype(F32)
    factor = lax.rsqrt(jnp.mean(wide * wide, axis=-1, keepdims=True) + NORM_EPS)
    result[...] = (wide * factor * gain[...].astype(F32)).astype(BF)


def column_of(row):
    count = row.shape[1]
    shape = (count, count)
    same = lax.broadcasted_iota(jnp.int32, shape, 0) == lax.broadcasted_iota(jnp.int32, shape, 1)
    return jnp.sum(jnp.where(same, row, 0.0), axis=1, keepdims=True)


def row_of(column):
    count = column.shape[0]
    shape = (count, count)
    same = lax.broadcasted_iota(jnp.int32, shape, 0) == lax.broadcasted_iota(jnp.int32, shape, 1)
    return jnp.sum(jnp.where(same, column, 0.0), axis=0, keepdims=True)


def picked(row_count, ranks, values):
    rows = lax.broadcasted_iota(jnp.int32, (row_count, ranks.shape[1]), 0).astype(F32)
    return [
        jnp.sum(jnp.where(rows == ranks, value, 0.0), axis=1, keepdims=True) for value in values
    ]


def plan_kernel(sizes, lengths, owners, starts, freqs, *outs):
    groups, count, home_count, slot_rows, sorted_count, cache_rows = sizes
    (
        slots_ref,
        cos_ref,
        sin_ref,
        home_start,
        home_span,
        home_write,
        home_bounds,
        far_order,
        sort_start,
        sort_span,
        far_write,
        far_bounds,
    ) = outs
    here = lax.axis_index("dp")

    def block(ref, index):
        return ref[:, pl.ds(pl.multiple_of(index * count, LANES), count)]

    def ranks_of(owner, start):
        owner_column, start_column = column_of(owner), column_of(start)
        before = (owner_column == owner) & (start_column < start)
        return jnp.sum(jnp.where(before, 1.0, 0.0), axis=0, keepdims=True)

    def put_ranges(start_ref, span_ref, bounds_ref, start, span):
        start_ref[...] = start.astype(jnp.int32)
        span_ref[...] = span.astype(jnp.int32)
        for tile in range(start.shape[0] // Q_TILE):
            cut = slice(tile * Q_TILE, (tile + 1) * Q_TILE)
            live = span[cut] > 0.0
            low = jnp.min(start[cut]).astype(jnp.int32) // P_TILE
            last = jnp.max(jnp.where(live, start[cut] + span[cut], 0.0)).astype(jnp.int32)
            high = (last + (P_TILE - 1)) // P_TILE
            bounds_ref[0, tile] = jnp.minimum(low, high)
            bounds_ref[1, tile] = high

    my_owner = block(owners, here)
    my_start = block(starts, here).astype(F32)
    my_length = block(lengths, here).astype(F32)
    rank = ranks_of(my_owner.astype(F32), my_start)
    hop = my_owner ^ here
    slot = jnp.where(hop == 0, rank, (hop - 1).astype(F32) * slot_rows + (rank + home_count))
    slots_ref[...] = slot.astype(jnp.int32)
    angles = column_of(my_length) * freqs[...]
    cos_ref[...] = jnp.cos(angles)
    sin_ref[...] = jnp.sin(angles)
    start, span = picked(home_count, slot, [my_start, my_length])
    live = span > 0.0
    start = jnp.where(live, start, float(cache_rows))
    put_ranges(home_start, home_span, home_bounds, start, span)
    home_write[...] = row_of(jnp.where(live, start + span, -1.0)).astype(jnp.int32)

    far = []
    for k in range(1, groups):
        source = here ^ k
        owner = block(owners, source)
        start = block(starts, source).astype(F32)
        rank = ranks_of(owner.astype(F32), start)
        rank = jnp.where(owner == here, rank, -1.0)
        far.append(picked(slot_rows, rank, [start, block(lengths, source).astype(F32)]))
    start = jnp.concatenate([pair[0] for pair in far], axis=0)
    span = jnp.concatenate([pair[1] for pair in far], axis=0)
    live = span > 0.0
    start = jnp.where(live, start, float(cache_rows))
    far_write[...] = row_of(jnp.where(live, start + span, -1.0)).astype(jnp.int32)
    start_row, span_row = row_of(start), row_of(span)
    order = jnp.sum(jnp.where(start < start_row, 1.0, 0.0), axis=0, keepdims=True)
    order = jnp.where(span_row > 0.0, order, -1.0)
    far_order[...] = order.astype(jnp.int32)
    start, span = picked(sorted_count, order, [start_row, span_row])
    start = jnp.where(span > 0.0, start, float(cache_rows))
    put_ranges(sort_start, sort_span, far_bounds, start, span)


def qkv_kernel(piece_count, home_count, slot_rows, hop_count, *refs):
    pieces = refs[:piece_count]
    weights, cosine, sine, slots = refs[piece_count : piece_count + 4]
    home_ref = refs[piece_count + 4]
    out_refs = refs[piece_count + 5 : -1]
    normed = refs[-1]
    me = lax.axis_index("tensor")
    rows = pieces[0].shape[0]
    for k, piece in enumerate(pieces):
        normed[pl.ds(pl.multiple_of((me ^ k) * rows, rows), rows), :] = piece[...]
    width = weights.shape[2]
    lane = lax.broadcasted_iota(jnp.int32, (normed.shape[0], width), 1)
    low_half = (lane % HD) < HD // 2
    wide = lambda ref: jnp.concatenate([ref[...]] * (width // LANES), axis=1)
    parts = []
    for c in range(3):
        projected = dot(normed[...], weights[c])
        if c < 2:
            ahead = pltpu.roll(projected, width - HD // 2, 1)
            behind = pltpu.roll(projected, HD // 2, 1)
            turned = jnp.where(low_half, -ahead, behind)
            projected = projected * wide(cosine) + turned * wide(sine)
        parts.append(projected.astype(BF))
    packed = jnp.concatenate(parts, axis=1)
    selector = one_hot(home_count + hop_count * slot_rows, slots[...])
    chosen = dot(selector, packed).astype(BF)
    home_ref[...] = chosen[:home_count]
    for k in range(hop_count):
        first = home_count + k * slot_rows
        out_refs[k][...] = chosen[first : first + slot_rows]


def attend_tile(query, key, value, start, span, low, high, kv_ref, heads):
    rows, width = query.shape
    scale = 1.0 / math.sqrt(HD)
    lane_head = lax.broadcasted_iota(jnp.int32, (rows, width), 1) // HD
    masks = [lane_head == h for h in range(heads)]
    zero = jnp.zeros_like(query)
    stacked = jnp.concatenate([jnp.where(m, query, zero) for m in masks], axis=0)
    product = query.astype(F32) * key.astype(F32)
    own = jnp.concatenate(
        [jnp.sum(jnp.where(m, product, 0.0), axis=1, keepdims=True) for m in masks], axis=0
    ) * scale
    starts = jnp.concatenate([start] * heads, axis=0)
    spans = jnp.concatenate([span] * heads, axis=0)
    first_out = jnp.concatenate([value.astype(F32)] * heads, axis=0)

    def advance(step, carry):
        top, total, out = carry
        first = pl.multiple_of(step * P_TILE, P_TILE)
        keys = kv_ref[0, pl.ds(first, P_TILE), :]
        values = kv_ref[1, pl.ds(first, P_TILE), :]
        offset = lax.broadcasted_iota(jnp.int32, (1, P_TILE), 1) + first
        since = offset - starts
        live = (since >= 0) & (since < spans)
        scores = jnp.where(live, dot_nt(stacked, keys) * scale, MASK_LOW)
        new_top = jnp.maximum(top, jnp.max(scores, axis=1, keepdims=True))
        weights = jnp.exp(scores - new_top)
        factor = jnp.exp(top - new_top)
        total = total * factor + jnp.sum(weights, axis=1, keepdims=True)
        out = out * factor + dot(weights.astype(BF), values)
        return new_top, total, out

    top, total, out = lax.fori_loop(
        low, high, advance, (own, jnp.ones_like(own), first_out)
    )
    out = out / total
    log_sum = top + jnp.log(total)
    attended = jnp.zeros((rows, width), F32)
    lane = lax.broadcasted_iota(jnp.int32, (rows, LANES), 1)
    extra = jnp.zeros((rows, LANES), F32)
    for h in range(heads):
        attended = jnp.where(masks[h], out[h * rows : (h + 1) * rows], attended)
        rest = log_sum[h * rows : (h + 1) * rows]
        for part in range(3):
            piece = rest.astype(BF).astype(F32)
            rest = rest - piece
            extra = jnp.where(lane == part * heads + h, piece, extra)
    return jnp.concatenate([attended.astype(BF), extra.astype(BF)], axis=1)


def attend_all(bounds, packed, starts, spans, kv_ref, result, heads):
    width = heads * HD
    for tile in range(packed.shape[0] // Q_TILE):
        here = slice(tile * Q_TILE, (tile + 1) * Q_TILE)
        rows = packed[here]
        result[here, :] = attend_tile(
            rows[:, :width],
            rows[:, width : 2 * width],
            rows[:, 2 * width :],
            starts[here, :],
            spans[here, :],
            bounds[0, tile],
            bounds[1, tile],
            kv_ref,
            heads,
        )


def home_kernel(heads, bounds, packed, starts, spans, kv_ref, result):
    attend_all(bounds, packed[...], starts, spans, kv_ref, result, heads)


def far_kernel(heads, hop_count, sorted_count, bounds, *refs):
    arrived = jnp.concatenate([ref[...] for ref in refs[:hop_count]], axis=0)
    order, starts, spans, kv_ref, _ = refs[hop_count : hop_count + 5]
    outs = refs[hop_count + 5 : 2 * hop_count + 5]
    scratch = refs[-1]
    mover = one_hot(sorted_count, order[...])
    in_order = dot(mover, arrived).astype(BF)
    attend_all(bounds, in_order, starts, spans, kv_ref, scratch, heads)
    back = dot_tn(mover, scratch[...]).astype(BF)
    slot_rows = arrived.shape[0] // hop_count
    for k in range(hop_count):
        outs[k][...] = back[k * slot_rows : (k + 1) * slot_rows]


def put_chunks(keep_ref, send_ref, partial, rows):
    me = lax.axis_index("tensor")
    for k in range(partial.shape[0] // rows):
        ref = keep_ref if k % 2 == 0 else send_ref
        ref[k // 2] = partial[pl.ds(pl.multiple_of((me ^ k) * rows, rows), rows), :]


def out_first_kernel(heads, hop_count, rows, slots, home, *refs):
    backs = refs[:hop_count]
    weights, keep_ref, send_ref, placed_ref, log_ref, partial = refs[hop_count:]
    width = heads * HD
    half = keep_ref.shape[2]
    both = jnp.concatenate([home[...]] + [ref[...] for ref in backs], axis=0)
    placed = dot_tn(one_hot(both.shape[0], slots[...]), both)
    extra = placed[:, width:]
    log_ref[...] = (
        extra + pltpu.roll(extra, LANES - heads, 1) + pltpu.roll(extra, LANES - 2 * heads, 1)
    )
    attention = placed[:, :width].astype(BF)
    placed_ref[...] = attention
    partial[...] = dot(attention, weights[:, :half]).astype(BF)
    put_chunks(keep_ref, send_ref, partial, rows)


def out_second_kernel(rows, attention, weights, keep_ref, send_ref, partial):
    half = keep_ref.shape[2]
    partial[...] = dot(attention[...], weights[:, half:]).astype(BF)
    put_chunks(keep_ref, send_ref, partial, rows)


def scaled_rows(pieces, gain):
    wide = jnp.concatenate([piece[...] for piece in pieces], axis=0).astype(F32)
    return (wide * gain[...].astype(F32)).astype(BF), jnp.sum(wide * wide, axis=1, keepdims=True)


def gate_kernel(piece_count, *refs):
    pieces = refs[:piece_count]
    gain, gate_up, gate_ref, up_ref, square_ref = refs[piece_count:]
    half = pieces[0].shape[1]
    scaled, square_ref[...] = scaled_rows(pieces, gain)
    gate_ref[...] = dot(scaled, gate_up[0, :half])
    up_ref[...] = dot(scaled, gate_up[1, :half])


def down_first_kernel(piece_count, rows, *refs):
    pieces = refs[:piece_count]
    gain, gate_up, gate_ref, up_ref, square_ref, down = refs[piece_count : piece_count + 6]
    inner_ref, keep_ref, send_ref = refs[piece_count + 6 :]
    half = pieces[0].shape[1]
    scaled, squares = scaled_rows(pieces, gain)
    factor = lax.rsqrt((squares + square_ref[...]) / (2 * half) + NORM_EPS)
    gate = (gate_ref[...] + dot(scaled, gate_up[0, half:])) * factor
    upward = (up_ref[...] + dot(scaled, gate_up[1, half:])) * factor
    inner = (gate / (1.0 + jnp.exp(-gate)) * upward).astype(BF)
    inner_ref[...] = inner
    partial = dot(inner, down[:, :half]).astype(BF)
    put_relative(keep_ref, send_ref, partial, rows)


def down_second_kernel(rows, inner, down, keep_ref, send_ref):
    half = keep_ref.shape[2]
    partial = dot(inner[...], down[:, half:]).astype(BF)
    put_relative(keep_ref, send_ref, partial, rows)


def put_relative(keep_ref, send_ref, partial, rows):
    for k in range(partial.shape[0] // rows):
        ref = keep_ref if k % 2 == 0 else send_ref
        ref[k // 2] = partial[k * rows : (k + 1) * rows]


def update_kernel(hop_count, width, home_rows, far_rows, home, *refs):
    far = refs[:hop_count]
    kv_in, kv_out = refs[hop_count:]
    block = kv_in.shape[1]
    position = lax.broadcasted_iota(jnp.int32, (block, 1), 0) + pl.program_id(0) * block
    fresh = jnp.concatenate([home[:, width:]] + [ref[:, width:] for ref in far], axis=0)
    targets = jnp.concatenate([home_rows[...], far_rows[...]], axis=1)
    hit = jnp.where(position == targets, 1.0, 0.0)
    written = jnp.max(hit, axis=1, keepdims=True) > 0.0
    values = dot(hit.astype(BF), fresh).astype(BF)
    kv_out[0] = jnp.where(written, values[:, :width], kv_in[0])
    kv_out[1] = jnp.where(written, values[:, width:], kv_in[1])


def vmem(count):
    return [pl.BlockSpec(memory_space=pltpu.VMEM)] * count


def on_device(
    tokens,
    attn_gain,
    mlp_gain,
    project_in,
    project_out,
    gate_up,
    project_down,
    kv_cache,
    lengths,
    owners,
    cache_start,
):
    groups = lax.axis_size("dp")
    my_index = lax.axis_index("dp")
    tensor_count = lax.axis_size("tensor")
    me = lax.axis_index("tensor")
    rows, model_width = tokens.shape
    request_count = rows * tensor_count
    width = project_in.shape[2]
    heads = width // HD
    cache_rows = kv_cache.shape[1]
    home_count = round_up(request_count - request_count // 2, Q_TILE)
    hops = groups - 1
    capacity = (request_count // 2 + groups - 2) // (groups - 1)
    slot_rows = round_up(capacity, 16)
    far_count = hops * slot_rows
    sorted_count = round_up(min(hops * capacity, far_count), Q_TILE)
    shape = jax.ShapeDtypeStruct
    smem = pl.BlockSpec(memory_space=pltpu.SMEM)
    anywhere = pl.BlockSpec(memory_space=pl.ANY)

    def params(mebibytes):
        return pltpu.CompilerParams(vmem_limit_bytes=mebibytes * 1024 * 1024)

    def cost(flops, bytes_accessed, transcendentals=0):
        return pl.CostEstimate(
            flops=flops, bytes_accessed=bytes_accessed, transcendentals=transcendentals
        )

    normed = pl.pallas_call(
        norm_kernel,
        out_shape=shape(tokens.shape, BF),
        in_specs=vmem(2),
        out_specs=vmem(1)[0],
        compiler_params=params(16),
        name="attn_norm",
    )(tokens, attn_gain[None, :])

    ints = lambda *dims: shape(dims, jnp.int32)
    freqs = ROPE_BASE ** (-((jnp.arange(LANES) % (HD // 2)).astype(F32) * 2.0 / HD))
    plan = lambda: pl.pallas_call(
        functools.partial(
            plan_kernel,
            (groups, request_count, home_count, slot_rows, sorted_count, cache_rows),
        ),
        out_shape=[
            ints(1, request_count),
            shape((request_count, LANES), F32),
            shape((request_count, LANES), F32),
            ints(home_count, 1),
            ints(home_count, 1),
            ints(1, home_count),
            ints(2, home_count // Q_TILE),
            ints(1, far_count),
            ints(sorted_count, 1),
            ints(sorted_count, 1),
            ints(1, far_count),
            ints(2, sorted_count // Q_TILE),
        ],
        in_specs=vmem(4),
        out_specs=vmem(6) + [smem] + vmem(4) + [smem],
        compiler_params=params(16),
        cost_estimate=cost(4 * 10**9, 10**6, 10**5),
        name="plan",
    )(lengths[None, :], owners[None, :], cache_start[None, :], freqs[None, :])
    pieces, planned = gather_tensor(normed, plan)
    (
        slots,
        cosine,
        sine,
        home_start,
        home_span,
        home_write,
        home_bounds,
        far_order,
        sort_start,
        sort_span,
        far_write,
        far_bounds,
    ) = planned

    packed_outs = pl.pallas_call(
        functools.partial(qkv_kernel, tensor_count, home_count, slot_rows, hops),
        out_shape=[shape((home_count, 3 * width), BF)] + [shape((slot_rows, 3 * width), BF)] * hops,
        in_specs=vmem(tensor_count + 4),
        out_specs=vmem(1 + hops),
        scratch_shapes=[pltpu.VMEM((request_count, model_width), BF)],
        compiler_params=params(24),
        name="qkv",
    )(*pieces, project_in, cosine, sine, slots)
    home_packed = packed_outs[0]
    arrived = [swap(packed_outs[k], "dp", k) for k in range(1, groups)]

    out_width = width + LANES
    home_att = pl.pallas_call(
        functools.partial(home_kernel, heads),
        out_shape=shape((home_count, out_width), BF),
        in_specs=[smem] + vmem(4),
        out_specs=vmem(1)[0],
        compiler_params=params(16),
        cost_estimate=cost(2 * 10**9, 4 * 2**20, 10**6),
        name="home_attention",
    )(home_bounds, home_packed, home_start, home_span, kv_cache)
    far_outs = pl.pallas_call(
        functools.partial(far_kernel, heads, hops, sorted_count),
        out_shape=[shape((slot_rows, out_width), BF)] * hops,
        in_specs=[smem] + vmem(hops + 4) + [anywhere],
        out_specs=vmem(hops),
        scratch_shapes=[pltpu.VMEM((sorted_count, out_width), BF)],
        compiler_params=params(16),
        name="far_attention",
    )(far_bounds, *arrived, far_order, sort_start, sort_span, kv_cache, home_att)
    backs = [swap(far_outs[k - 1], "dp", k) for k in range(1, groups)]

    block = 512
    kv_spec = pl.BlockSpec((2, block, width), lambda i: (0, i, 0))
    fixed = lambda array: pl.BlockSpec(array.shape, lambda i: (0,) * array.ndim)
    kv_updated = pl.pallas_call(
        functools.partial(update_kernel, hops, width),
        grid=(cache_rows // block,),
        out_shape=shape(kv_cache.shape, BF),
        in_specs=[fixed(home_write), fixed(far_write), fixed(home_packed)]
        + [fixed(a) for a in arrived]
        + [kv_spec],
        out_specs=kv_spec,
        compiler_params=params(16),
        cost_estimate=cost(2 * 10**9, 8 * 2**20),
        name="cache_update",
    )(home_write, far_write, home_packed, *arrived, kv_cache)
    home_att, kv_updated = lax.optimization_barrier((home_att, kv_updated))

    half_count = tensor_count // 2
    half = model_width // 2
    halves = [shape((half_count, rows, half), BF)] * 2
    partial_scratch = [pltpu.VMEM((request_count, half), BF)]
    keep, send, attention, log_sum = pl.pallas_call(
        functools.partial(out_first_kernel, heads, hops, rows),
        out_shape=halves + [shape((request_count, width), BF), shape((request_count, LANES), F32)],
        in_specs=vmem(3 + hops),
        out_specs=vmem(4),
        scratch_shapes=partial_scratch,
        compiler_params=params(16),
        name="project_out_first",
    )(slots, home_att, *backs, project_out)
    log_sum_exp = log_sum[:, :heads]
    sums_first = reduce_tensor(keep, send)
    keep, send = pl.pallas_call(
        functools.partial(out_second_kernel, rows),
        out_shape=halves,
        in_specs=vmem(2),
        out_specs=vmem(2),
        scratch_shapes=partial_scratch,
        compiler_params=params(16),
        name="project_out_second",
    )(attention, project_out)
    sums_second = reduce_tensor(keep, send)

    def add_up(base, sums):
        return (base.astype(F32) + sum(piece.astype(F32) for piece in sums)).astype(BF)

    resid_first = add_up(tokens[:, :half], sums_first)
    resid_second = add_up(tokens[:, half:], sums_second)
    pieces_first = gather_tensor(resid_first)
    pieces_second = gather_tensor(resid_second)
    hidden = gate_up.shape[2]
    gate_part, up_part, squares = pl.pallas_call(
        functools.partial(gate_kernel, tensor_count),
        out_shape=[shape((request_count, hidden), F32)] * 2 + [shape((request_count, 1), F32)],
        in_specs=vmem(tensor_count + 2),
        out_specs=vmem(3),
        compiler_params=params(24),
        cost_estimate=cost(2 * 10**9, 4 * 2**20),
        name="gate_up_first",
    )(*pieces_first, mlp_gain[None, :half], gate_up)
    inner, keep, send = pl.pallas_call(
        functools.partial(down_first_kernel, tensor_count, rows),
        out_shape=[shape((request_count, hidden), BF)] + halves,
        in_specs=vmem(tensor_count + 6),
        out_specs=vmem(3),
        compiler_params=params(32),
        name="down_first",
    )(*pieces_second, mlp_gain[None, half:], gate_up, gate_part, up_part, squares, project_down)
    sums_first = reduce_tensor(keep, send)
    keep, send = pl.pallas_call(
        functools.partial(down_second_kernel, rows),
        out_shape=halves,
        in_specs=vmem(2),
        out_specs=vmem(2),
        compiler_params=params(16),
        name="down_second",
    )(inner, project_down)
    sums_second = reduce_tensor(keep, send)
    hidden_states = jnp.concatenate(
        [add_up(resid_first, sums_first), add_up(resid_second, sums_second)], axis=1
    )
    return (hidden_states, log_sum_exp, kv_updated)


def solution(mesh):
    placed = (
        P(("dp", "tensor"), None),
        P(),
        P(),
        P(None, None, "tensor"),
        P("tensor", None),
        P(None, None, "tensor"),
        P("tensor", None),
        P(None, "dp", "tensor"),
        P(),
        P(),
        P(),
    )
    return jax.shard_map(
        on_device,
        mesh=mesh,
        in_specs=placed,
        out_specs=(P(("dp", "tensor"), None), P("dp", "tensor"), P(None, "dp", "tensor")),
        check_vma=False,
    )
```

time: 118 us -> 102 us (0.86)
  other arithmetic: 13.8 us -> 1.11 us
  starting transfers between devices: 29.2 us -> 41 us
  local copies, waits for them, and re-layouts: 15.7 us -> 4.38 us
  waiting for transfers between devices: 33.3 us -> 31 us
  Pallas kernels: 24.6 us -> 22.5 us
    ppermute x28 -> x43, starting transfers between devices: 29.2 us -> 41 us  [swap(): lax.ppermute(values, axis_name, [(i, i ^ offset) for i in range(count)])]
    another operation x10 -> x0, local copies, waits for them, and re-layouts: 5.59 us -> none  [the longest x2 3.27 us: on_device(): cosine = jnp.tile(jnp.cos(angles), (1, width // half))]
    select_n x19 -> x0, other arithmetic: 3.26 us -> none  [the longest x1 0.7 us: on_device(): jnp.where(all_here & (in_hop != 0), (in_hop - 1) * slot_rows + in_rank, -1)]
    reduce_sum x8 -> x0, other arithmetic: 3.23 us -> none  [the longest x2 1.41 us: scaled_norm(): factor = lax.rsqrt(jnp.mean(wide * wide, axis=-1, keepdims=True) + NORM_EPS)]
    convert_element_type x6 -> x3, other arithmetic: 3.23 us -> 0.23 us  [add_up(): (base.astype(F32) + sum((piece.astype(F32) for piece in sums))).astype(BF)]
    ppermute x28 -> x43, waiting for transfers between devices: 33.3 us -> 31 us  [swap(): lax.ppermute(values, axis_name, [(i, i ^ offset) for i in range(count)])]
    dynamic_slice x3 -> x0, local copies, waits for them, and re-layouts: 2.28 us -> none  [on_device(): lax.dynamic_slice_in_dim(values, my_index * request_count, request_count)]
    pallas_call x1, Pallas kernels: 2.62 us -> 1.39 us  [on_device(): pl.pallas_call(functools.partial(qkv_kernel, tensor_count, home_count, sl...]
  transfers between devices with their start and end apart: 28 -> 43, of which waited for: 14 -> 15; matrix products, arithmetic and copies ran while one was open for 18% -> 1% of each run, Pallas kernels for 8% -> 14%
where the time goes in v2:
time: 102 us; the launch traced here: 101 us
  starting transfers between devices  41 us (40%)
  waiting for transfers between devices  31 us (30%)
  Pallas kernels  22.5 us (22%)
  local copies, waits for them, and re-layouts  4.38 us (4%)
  other arithmetic  1.11 us (1%)
    ppermute x43, starting transfers between devices, swap(): lax.ppermute(values, axis_name, [(i, i ^ offset) for i in range(count)])  41 us
    ppermute x43, waiting for transfers between devices, swap(): lax.ppermute(values, axis_name, [(i, i ^ offset) for i in range(count)])  31 us
    pallas_call x1, Pallas kernels, on_device(): pl.pallas_call(functools.partial(update_kernel, hops, width), grid=(cache...  5.56 us
    pallas_call x1, Pallas kernels, on_device(): pl.pallas_call(functools.partial(home_kernel, heads), out_shape=shape((ho...  4.42 us
    pallas_call x1, Pallas kernels, on_device(): pl.pallas_call(functools.partial(far_kernel, heads, hops, sorted_count),...  4.04 us
    unnamed x25, local copies, waits for them, and re-layouts  3.67 us
    pallas_call x1, Pallas kernels, on_device(): pl.pallas_call(functools.partial(plan_kernel, (groups, request_count, hom...  2.07 us
  transfers between devices with their start and end apart: 43, of which 15 were waited for; matrix products, arithmetic and copies ran while one was open for 1% of the time, Pallas kernels for 14%

profile of v2, /device:TPU:0, one launch (start us, length us, event | category | flops | bytes accessed | tf_op | source)
XLA Modules:
  0.0 100.9 jit_solution(10583043646883827382)
XLA Ops:
  0.6 0.7 broadcast_in_dim.19.gain
  1.3 0.9 copy-done.4
  2.2 0.1 attn_norm.1.refs_0_
  2.4 5.1 %collective-permute-start.2 = (bf16[32,2048]{1,0:T(8,128)(2,1)S(1)}, bf16[32,2048]{1,0:T(8,128)(2,1)S(1)}, u32[]{:S(2)}, u32[]{:S(2)}) collective-permute-start(bf16[32,2048]{1,0:T(8,128)(2,1)S(1)} %attn_norm.1.refs_0_), channel_id=1, source_target_pairs={{0,6},{1,7},{2,4},{3,5},{4,2},{5,3},{6,0},{7,1},{8,14},{9,15},{10,... | collective-permute-start | bytes 393224 | tf_op jit(solution)/shard_map/ppermute | solution.py:45
  7.5 0.6 collective-permute-start
  8.1 0.7 copy-done.6
  8.8 0.7 copy-done.7
  9.5 0.7 copy-done.8
  10.2 2.1 %plan.1 = (s32[1,256]{1,0:T(1,128)S(1)}, f32[256,128]{1,0:T(8,128)S(1)}, f32[256,128]{1,0:T(8,128)S(1)}, s32[128,1]{1,0:T(8,128)S(1)}, s32[128,1]{1,0:T(8,128)S(...) custom-call(s32[1,1024]{1,0:T(1,128)S(1)} %bitcast.51, ...), custom_call_target="tpu_custom_call" | custom-call | flops 4000000000 | bytes 1000000 | tf_op jit(solution)/shard_map/plan/pallas_call | solution.py:428
  12.3 6.2 %collective-permute-done.1.refs_4_ = bf16[32,2048]{1,0:T(8,128)(2,1)S(1)} collective-permute-done((bf16[32,2048]{1,0:T(8,128)(2,1)S(1)}, bf16[32,2048]{1,0:T(8,128)(2,1)S(1)}, u32[]{:S(2)}, u32[]{:S(2)}) %collective-permute-start.1) | collective-permute-done | bytes 131104 | tf_op jit(solution)/shard_map/ppermute | solution.py:45
  18.6 0.5 collective-permute-start.4
  19.1 0.5 collective-permute-start.6
  19.6 0.3 collective-permute-done.3.refs_1_
  19.9 0.2 collective-permute-done.4.refs_3_
  20.1 0.3 collective-permute-done.5.refs_5_
  20.4 0.2 collective-permute-done.6.refs_7_
  20.6 1.4 %qkv.1 = (bf16[128,768]{1,0:T(8,128)(2,1)S(1)}, bf16[48,768]{1,0:T(8,128)(2,1)S(1)}, bf16[48,768]{1,0:T(8,128)(2,1)S(1)}, bf16[48,768]{1,0:T(8,128)(2,1)S(1)}) custom-call(bf16[32,2048]{1,0:T(8,128)(2,1)S(1)} %attn_norm.1.refs_0_, bf16[32,2048]{1,0:T(8,128)(2,1)S(1)} %collective-permute-done.3.refs_1_, bf16[32,2048]{1,0:T(8,128)(2,1)S(1)} %collective-permute-done.refs_2_, ...), custom_call_target="tpu_custom_call" | custom-call | tf_op jit(solution)/shard_map/qkv/pallas_call | solution.py:469
  22.0 1.6 %collective-permute-start.7 = (bf16[48,768]{1,0:T(8,128)(2,1)S(1)}, bf16[48,768]{1,0:T(8,128)(2,1)S(1)}, u32[]{:S(2)}, u32[]{:S(2)}) collective-permute-start(bf16[48,768]{1,0:T(8,128)(2,1)S(1)} %get-tuple-element.79), channel_id=1, source_target_pairs={{0,8},{8,0},{16,24},{24,16},{1,9},{9,1},{17,25},{25,17},{2,10},{10... | collective-permute-start | bytes 221192 | tf_op jit(solution)/shard_map/ppermute | solution.py:45
  23.6 1.5 %collective-permute-start.8 = (bf16[48,768]{1,0:T(8,128)(2,1)S(1)}, bf16[48,768]{1,0:T(8,128)(2,1)S(1)}, u32[]{:S(2)}, u32[]{:S(2)}) collective-permute-start(bf16[48,768]{1,0:T(8,128)(2,1)S(1)} %get-tuple-element.80), channel_id=1, source_target_pairs={{0,16},{8,24},{16,0},{24,8},{1,17},{9,25},{17,1},{25,9},{2,18},{10... | collective-permute-start | bytes 221192 | tf_op jit(solution)/shard_map/ppermute | solution.py:45
  25.1 0.5 collective-permute-start.9
  25.6 4.4 %home_attention.1.refs_7_.home = bf16[128,384]{1,0:T(8,128)(2,1)S(1)} custom-call(s32[2,4]{1,0:T(2,128)S(1)} %get-tuple-element.67.bounds, bf16[128,768]{1,0:T(8,128)(2,1)S(1)} %get-tuple-element.74.packed.home, s32[128,1]{1,0:T(8,128)S(1)} %get-tuple-element.75.starts, s32[128,1]{1,0:T(8,128)S(1)} %get-tuple-element.76.spans, bf16[2,4096,256]{2,1,0:T(8,128)(2,1)S(1)} %copy-done), custom_call_target="tpu_custom_call" | custom-call | flops 2000000000 | bytes 4194304 | tf_op jit(solution)/shard_map/home_attention/pallas_call | solution.py:482
  30.0 0.3 collective-permute-done.9.refs_2_
  30.3 4.0 %far_attention.1 = (bf16[48,384]{1,0:T(8,128)(2,1)S(1)}, bf16[48,384]{1,0:T(8,128)(2,1)S(1)}, bf16[48,384]{1,0:T(8,128)(2,1)S(1)}) custom-call(s32[2,5]{1,0:T(2,128)S(1)} %get-tuple-element.83.bounds, bf16[48,768]{1,0:T(8,128)(2,1)S(1)} %collective-permute-done.7.refs_0_, bf16[48,768]{1,0:T(8,128)(2,1)S(1)} %collective-permute-done.8.refs_1_, ...), custom_call_target="tpu_custom_call" | custom-call | tf_op jit(solution)/shard_map/far_attention/pallas_call | solution.py:491
  34.4 1.8 %collective-permute-start.10 = (bf16[48,384]{1,0:T(8,128)(2,1)S(1)}, bf16[48,384]{1,0:T(8,128)(2,1)S(1)}, u32[]{:S(2)}, u32[]{:S(2)}) collective-permute-start(bf16[48,384]{1,0:T(8,128)(2,1)S(1)} %get-tuple-element.87), channel_id=1, source_target_pairs={{0,8},{8,0},{16,24},{24,16},{1,9},{9,1},{17,25},{25,17},{2,10},{10... | collective-permute-start | bytes 110600 | tf_op jit(solution)/shard_map/ppermute | solution.py:45
  36.2 4.1 %collective-permute-start.11 = (bf16[48,384]{1,0:T(8,128)(2,1)S(1)}, bf16[48,384]{1,0:T(8,128)(2,1)S(1)}, u32[]{:S(2)}, u32[]{:S(2)}) collective-permute-start(bf16[48,384]{1,0:T(8,128)(2,1)S(1)} %get-tuple-element.88), channel_id=1, source_target_pairs={{0,16},{8,24},{16,0},{24,8},{1,17},{9,25},{17,1},{25,9},{2,18},{10... | collective-permute-start | bytes 110600 | tf_op jit(solution)/shard_map/ppermute | solution.py:45
  40.3 0.6 collective-permute-start.12
  40.8 5.6 %cache_update.1 = bf16[2,4096,256]{2,1,0:T(8,128)(2,1)} custom-call(s32[1,128]{1,0:T(1,128)S(1)} %get-tuple-element.77.home_rows, s32[1,144]{1,0:T(1,128)S(1)} %get-tuple-element.78.far_rows, bf16[128,768]{1,0:T(8,128)(2,1)S(1)} %get-tuple-element.74.packed.home, bf16[48,768]{1,0:T(8,128)(2,1)S(1)} %collective-permute-done.7.refs_0_, ...), custom_call_target="tpu_custom_call" | custom-call | flops 2000000000 | bytes 8388608 | tf_op jit(solution)/shard_map/cache_update/pallas_call | solution.py:505
  46.4 0.6 project_out_first.1
  47.0 0.1 collective-permute-start.13
  47.1 0.3 project_out_second.1
  47.4 0.6 collective-permute-start.17
  48.0 0.6 collective-permute-done.13
  48.7 0.1 collective-permute-start.14
  48.8 2.5 %collective-permute-start.16 = (bf16[32,1024]{1,0:T(8,128)(2,1)S(1)}, bf16[32,1024]{1,0:T(8,128)(2,1)S(1)}, u32[]{:S(2)}, u32[]{:S(2)}) collective-permute-start(bf16[32,1024]{1,0:T(8,128)(2,1)S(1)} %get-tuple-element.115), channel_id=1, source_target_pairs={{0,6},{1,7},{2,4},{3,5},{4,2},{5,3},{6,0},{7,1},{8,14},{9,15},{10,... | collective-permute-start | bytes 196616 | tf_op jit(solution)/shard_map/ppermute | solution.py:45
  51.3 0.9 collective-permute-start.15
  52.3 1.0 %collective-permute-start.18 = (bf16[32,1024]{1,0:T(8,128)(2,1)S(1)}, bf16[32,1024]{1,0:T(8,128)(2,1)S(1)}, u32[]{:S(2)}, u32[]{:S(2)}) collective-permute-start(bf16[32,1024]{1,0:T(8,128)(2,1)S(1)} %get-tuple-element.117), channel_id=1, source_target_pairs={{0,2},{1,3},{2,0},{3,1},{4,6},{5,7},{6,4},{7,5},{8,10},{9,11},{10,... | collective-permute-start | bytes 196616 | tf_op jit(solution)/shard_map/ppermute | solution.py:45
  53.3 2.5 %collective-permute-start.20 = (bf16[32,1024]{1,0:T(8,128)(2,1)S(1)}, bf16[32,1024]{1,0:T(8,128)(2,1)S(1)}, u32[]{:S(2)}, u32[]{:S(2)}) collective-permute-start(bf16[32,1024]{1,0:T(8,128)(2,1)S(1)} %get-tuple-element.118), channel_id=1, source_target_pairs={{0,6},{1,7},{2,4},{3,5},{4,2},{5,3},{6,0},{7,1},{8,14},{9,15},{10,... | collective-permute-start | bytes 196616 | tf_op jit(solution)/shard_map/ppermute | solution.py:45
  55.8 6.0 %collective-permute-done.15 = bf16[32,1024]{1,0:T(8,128)(2,1)S(1)} collective-permute-done((bf16[32,1024]{1,0:T(8,128)(2,1)S(1)}, bf16[32,1024]{1,0:T(8,128)(2,1)S(1)}, u32[]{:S(2)}, u32[]{:S(2)}) %collective-permute-start.15) | collective-permute-done | bytes 65568 | tf_op jit(solution)/shard_map/ppermute | solution.py:45
  61.8 2.2 %collective-permute-done.19 = bf16[32,1024]{1,0:T(8,128)(2,1)S(1)} collective-permute-done((bf16[32,1024]{1,0:T(8,128)(2,1)S(1)}, bf16[32,1024]{1,0:T(8,128)(2,1)S(1)}, u32[]{:S(2)}, u32[]{:S(2)}) %collective-permute-start.19) | collective-permute-done | bytes 65568 | tf_op jit(solution)/shard_map/ppermute | solution.py:45
  64.1 0.1 fusion.15
  64.2 2.4 %collective-permute-start.33 = (bf16[32,1024]{1,0:T(8,128)(2,1)S(1)}, bf16[32,1024]{1,0:T(8,128)(2,1)S(1)}, u32[]{:S(2)}, u32[]{:S(2)}) collective-permute-start(bf16[32,1024]{1,0:T(8,128)(2,1)S(1)} %get-tuple-element.120.refs_0_), channel_id=1, source_target_pairs={{0,6},{1,7},{2,4},{3,5},{4,2},{5,3},{6,0},{7,1},{8,14},{9,15},{10,... | collective-permute-start | bytes 196616 | tf_op jit(solution)/shard_map/ppermute | solution.py:45
  66.6 2.1 %collective-permute-start.29 = (bf16[32,1024]{1,0:T(8,128)(2,1)S(1)}, bf16[32,1024]{1,0:T(8,128)(2,1)S(1)}, u32[]{:S(2)}, u32[]{:S(2)}) collective-permute-start(bf16[32,1024]{1,0:T(8,128)(2,1)S(1)} %get-tuple-element.120.refs_0_), channel_id=1, source_target_pairs={{0,2},{1,3},{2,0},{3,1},{4,6},{5,7},{6,4},{7,5},{8,10},{9,11},{10,... | collective-permute-start | bytes 196616 | tf_op jit(solution)/shard_map/ppermute | solution.py:45
  68.6 2.3 %collective-permute-start.26 = (bf16[32,1024]{1,0:T(8,128)(2,1)S(1)}, bf16[32,1024]{1,0:T(8,128)(2,1)S(1)}, u32[]{:S(2)}, u32[]{:S(2)}) collective-permute-start(bf16[32,1024]{1,0:T(8,128)(2,1)S(1)} %get-tuple-element.121.refs_0_), channel_id=1, source_target_pairs={{0,6},{1,7},{2,4},{3,5},{4,2},{5,3},{6,0},{7,1},{8,14},{9,15},{10,... | collective-permute-start | bytes 196616 | tf_op jit(solution)/shard_map/ppermute | solution.py:45
  71.0 2.1 %collective-permute-done.31.refs_4_ = bf16[32,1024]{1,0:T(8,128)(2,1)S(1)} collective-permute-done((bf16[32,1024]{1,0:T(8,128)(2,1)S(1)}, bf16[32,1024]{1,0:T(8,128)(2,1)S(1)}, u32[]{:S(2)}, u32[]{:S(2)}) %collective-permute-start.31) | collective-permute-done | bytes 65568 | tf_op jit(solution)/shard_map/ppermute | solution.py:45
  73.0 0.9 collective-permute-start.22
  73.9 0.5 collective-permute-start.32
  74.4 1.0 %collective-permute-done.26.refs_6_ = bf16[32,1024]{1,0:T(8,128)(2,1)S(1)} collective-permute-done((bf16[32,1024]{1,0:T(8,128)(2,1)S(1)}, bf16[32,1024]{1,0:T(8,128)(2,1)S(1)}, u32[]{:S(2)}, u32[]{:S(2)}) %collective-permute-start.26) | collective-permute-done | bytes 65568 | tf_op jit(solution)/shard_map/ppermute | solution.py:45
  75.5 2.6 %collective-permute-done.24.refs_4_ = bf16[32,1024]{1,0:T(8,128)(2,1)S(1)} collective-permute-done((bf16[32,1024]{1,0:T(8,128)(2,1)S(1)}, bf16[32,1024]{1,0:T(8,128)(2,1)S(1)}, u32[]{:S(2)}, u32[]{:S(2)}) %collective-permute-start.24) | collective-permute-done | bytes 65568 | tf_op jit(solution)/shard_map/ppermute | solution.py:45
  78.1 0.5 collective-permute-done.22.refs_2_
  78.6 0.5 collective-permute-start.25
  79.2 1.3 %gate_up_first.1 = (f32[256,1024]{1,0:T(8,128)S(1)}, f32[256,1024]{1,0:T(8,128)S(1)}, f32[256,1]{1,0:T(8,128)S(1)}) custom-call(bf16[32,1024]{1,0:T(8,128)(2,1)S(1)} %get-tuple-element.120.refs_0_, bf16[32,1024]{1,0:T(8,128)(2,1)S(1)} %collective-permute-done.28.refs_1_, bf16[32,1024]{1,0:T(8,128)(2,1)S(1)} %collective-permute-done.29.refs_2_, ...), custom_call_target="tpu_custom_call" | custom-call | flops 2000000000 | bytes 4194304 | tf_op jit(solution)/shard_map/gate_up_first/pallas_call | solution.py:553
  80.5 2.0 %down_first.1 = (bf16[256,1024]{1,0:T(8,128)(2,1)S(1)}, bf16[4,32,1024]{2,1,0:T(8,128)(2,1)S(1)}, bf16[4,32,1024]{2,1,0:T(8,128)(2,1)S(1)}) custom-call(bf16[32,1024]{1,0:T(8,128)(2,1)S(1)} %get-tuple-element.121.refs_0_, bf16[32,1024]{1,0:T(8,128)(2,1)S(1)} %collective-permute-done.21.refs_1_, bf16[32,1024]{1,0:T(8,128)(2,1)S(1)} %collective-permute-done.22.refs_2_, ...), custom_call_target="tpu_custom_call" | custom-call | tf_op jit(solution)/shard_map/down_first/pallas_call | solution.py:562
  82.6 0.5 collective-permute-start.35
  83.1 0.7 down_second.1
  83.8 0.1 collective-permute-start.39
  83.9 0.7 copy.14
  84.7 2.1 %collective-permute-start.38 = (bf16[32,1024]{1,0:T(8,128)(2,1)S(1)}, bf16[32,1024]{1,0:T(8,128)(2,1)S(1)}, u32[]{:S(2)}, u32[]{:S(2)}) collective-permute-start(bf16[32,1024]{1,0:T(8,128)(2,1)S(1)} %get-tuple-element.109), channel_id=1, source_target_pairs={{0,6},{1,7},{2,4},{3,5},{4,2},{5,3},{6,0},{7,1},{8,14},{9,15},{10,... | collective-permute-start | bytes 196616 | tf_op jit(solution)/shard_map/ppermute | solution.py:45
  86.8 1.4 %collective-permute-start.37 = (bf16[32,1024]{1,0:T(8,128)(2,1)S(1)}, bf16[32,1024]{1,0:T(8,128)(2,1)S(1)}, u32[]{:S(2)}, u32[]{:S(2)}) collective-permute-start(bf16[32,1024]{1,0:T(8,128)(2,1)S(1)} %get-tuple-element.110), channel_id=1, source_target_pairs={{0,4},{1,5},{2,6},{3,7},{4,0},{5,1},{6,2},{7,3},{8,12},{9,13},{10,... | collective-permute-start | bytes 196616 | tf_op jit(solution)/shard_map/ppermute | solution.py:45
  88.3 1.0 %collective-permute-start.40 = (bf16[32,1024]{1,0:T(8,128)(2,1)S(1)}, bf16[32,1024]{1,0:T(8,128)(2,1)S(1)}, u32[]{:S(2)}, u32[]{:S(2)}) collective-permute-start(bf16[32,1024]{1,0:T(8,128)(2,1)S(1)} %get-tuple-element.111), channel_id=1, source_target_pairs={{0,2},{1,3},{2,0},{3,1},{4,6},{5,7},{6,4},{7,5},{8,10},{9,11},{10,... | collective-permute-start | bytes 196616 | tf_op jit(solution)/shard_map/ppermute | solution.py:45
  89.3 2.0 %collective-permute-start.42 = (bf16[32,1024]{1,0:T(8,128)(2,1)S(1)}, bf16[32,1024]{1,0:T(8,128)(2,1)S(1)}, u32[]{:S(2)}, u32[]{:S(2)}) collective-permute-start(bf16[32,1024]{1,0:T(8,128)(2,1)S(1)} %get-tuple-element.112), channel_id=1, source_target_pairs={{0,6},{1,7},{2,4},{3,5},{4,2},{5,3},{6,0},{7,1},{8,14},{9,15},{10,... | collective-permute-start | bytes 196616 | tf_op jit(solution)/shard_map/ppermute | solution.py:45
  91.3 0.5 collective-permute-start.41
  91.8 6.2 %collective-permute-done.37 = bf16[32,1024]{1,0:T(8,128)(2,1)S(1)} collective-permute-done((bf16[32,1024]{1,0:T(8,128)(2,1)S(1)}, bf16[32,1024]{1,0:T(8,128)(2,1)S(1)}, u32[]{:S(2)}, u32[]{:S(2)}) %collective-permute-start.37) | collective-permute-done | bytes 65568 | tf_op jit(solution)/shard_map/ppermute | solution.py:45
  98.1 2.1 %collective-permute-done.41 = bf16[32,1024]{1,0:T(8,128)(2,1)S(1)} collective-permute-done((bf16[32,1024]{1,0:T(8,128)(2,1)S(1)}, bf16[32,1024]{1,0:T(8,128)(2,1)S(1)}, u32[]{:S(2)}, u32[]{:S(2)}) %collective-permute-start.41) | collective-permute-done | bytes 65568 | tf_op jit(solution)/shard_map/ppermute | solution.py:45
  100.2 0.7 pad_maximum_fusion
  (72 shorter events, 0.7 us)
Async XLA Ops:
  1.3 0.9 copy-start.4
  2.4 9.9 %collective-permute-start.2 = (bf16[32,2048]{1,0:T(8,128)(2,1)S(1)}, bf16[32,2048]{1,0:T(8,128)(2,1)S(1)}, u32[]{:S(2)}, u32[]{:S(2)}) collective-permute-start(bf16[32,2048]{1,0:T(8,128)(2,1)S(1)} %attn_norm.1.refs_0_), channel_id=1, source_target_pairs={{0,6},{1,7},{2,4},{3,5},{4,2},{5,3},{6,0},{7,1},{8,14},{9,15},{10,... | collective-permute-start | bytes 393224 | tf_op jit(solution)/shard_map/ppermute | solution.py:45
  7.5 11.1 %collective-permute-start.1 = (bf16[32,2048]{1,0:T(8,128)(2,1)S(1)}, bf16[32,2048]{1,0:T(8,128)(2,1)S(1)}, u32[]{:S(2)}, u32[]{:S(2)}) collective-permute-start(bf16[32,2048]{1,0:T(8,128)(2,1)S(1)} %attn_norm.1.refs_0_), channel_id=1, source_target_pairs={{0,4},{1,5},{2,6},{3,7},{4,0},{5,1},{6,2},{7,3},{8,12},{9,13},{10,... | collective-permute-start | bytes 393224 | tf_op jit(solution)/shard_map/ppermute | solution.py:45
  7.5 11.1 %collective-permute-start = (bf16[32,2048]{1,0:T(8,128)(2,1)S(1)}, bf16[32,2048]{1,0:T(8,128)(2,1)S(1)}, u32[]{:S(2)}, u32[]{:S(2)}) collective-permute-start(bf16[32,2048]{1,0:T(8,128)(2,1)S(1)} %attn_norm.1.refs_0_), channel_id=1, source_target_pairs={{0,2},{1,3},{2,0},{3,1},{4,6},{5,7},{6,4},{7,5},{8,10},{9,11},{10,... | collective-permute-start | bytes 393224 | tf_op jit(solution)/shard_map/ppermute | solution.py:45
  8.1 0.7 copy-start.6
  8.8 0.7 copy-start.7
  9.5 0.7 copy-start.8
  10.2 10.4 %copy-start.3 = (bf16[3,2048,256]{2,1,0:T(8,128)(2,1)S(1)}, bf16[3,2048,256]{2,1,0:T(8,128)(2,1)}, u32[]{:S(2)}) copy-start(bf16[3,2048,256]{2,1,0:T(8,128)(2,1)} %refs_8_.1) | copy-start | bytes 9437188
  12.3 13.3 %copy-start = (bf16[2,4096,256]{2,1,0:T(8,128)(2,1)S(1)}, bf16[2,4096,256]{2,1,0:T(8,128)(2,1)}, u32[]{:S(2)}) copy-start(bf16[2,4096,256]{2,1,0:T(8,128)(2,1)} %refs_6_.1) | copy-start | bytes 12582916
  18.6 1.3 %collective-permute-start.3 = (bf16[32,2048]{1,0:T(8,128)(2,1)S(1)}, bf16[32,2048]{1,0:T(8,128)(2,1)S(1)}, u32[]{:S(2)}, u32[]{:S(2)}) collective-permute-start(bf16[32,2048]{1,0:T(8,128)(2,1)S(1)} %attn_norm.1.refs_0_), channel_id=1, source_target_pairs={{0,1},{1,0},{2,3},{3,2},{4,5},{5,4},{6,7},{7,6},{8,9},{9,8},{10,11... | collective-permute-start | bytes 393224 | tf_op jit(solution)/shard_map/ppermute | solution.py:45
  18.6 1.5 %collective-permute-start.4 = (bf16[32,2048]{1,0:T(8,128)(2,1)S(1)}, bf16[32,2048]{1,0:T(8,128)(2,1)S(1)}, u32[]{:S(2)}, u32[]{:S(2)}) collective-permute-start(bf16[32,2048]{1,0:T(8,128)(2,1)S(1)} %collective-permute-done.refs_2_), channel_id=1, source_target_pairs={{0,1},{1,0},{2,3},{3,2},{4,5},{5,4},{6,7},{7,6},{8,9},{9,8},{10,11... | collective-permute-start | bytes 393224 | tf_op jit(solution)/shard_map/ppermute | solution.py:45
  19.1 1.3 %collective-permute-start.5 = (bf16[32,2048]{1,0:T(8,128)(2,1)S(1)}, bf16[32,2048]{1,0:T(8,128)(2,1)S(1)}, u32[]{:S(2)}, u32[]{:S(2)}) collective-permute-start(bf16[32,2048]{1,0:T(8,128)(2,1)S(1)} %collective-permute-done.1.refs_4_), channel_id=1, source_target_pairs={{0,1},{1,0},{2,3},{3,2},{4,5},{5,4},{6,7},{7,6},{8,9},{9,8},{10,11... | collective-permute-start | bytes 393224 | tf_op jit(solution)/shard_map/ppermute | solution.py:45
  19.1 1.5 %collective-permute-start.6 = (bf16[32,2048]{1,0:T(8,128)(2,1)S(1)}, bf16[32,2048]{1,0:T(8,128)(2,1)S(1)}, u32[]{:S(2)}, u32[]{:S(2)}) collective-permute-start(bf16[32,2048]{1,0:T(8,128)(2,1)S(1)} %collective-permute-done.2.refs_6_), channel_id=1, source_target_pairs={{0,1},{1,0},{2,3},{3,2},{4,5},{5,4},{6,7},{7,6},{8,9},{9,8},{10,11... | collective-permute-start | bytes 393224 | tf_op jit(solution)/shard_map/ppermute | solution.py:45
  22.0 8.0 %collective-permute-start.7 = (bf16[48,768]{1,0:T(8,128)(2,1)S(1)}, bf16[48,768]{1,0:T(8,128)(2,1)S(1)}, u32[]{:S(2)}, u32[]{:S(2)}) collective-permute-start(bf16[48,768]{1,0:T(8,128)(2,1)S(1)} %get-tuple-element.79), channel_id=1, source_target_pairs={{0,8},{8,0},{16,24},{24,16},{1,9},{9,1},{17,25},{25,17},{2,10},{10... | collective-permute-start | bytes 221192 | tf_op jit(solution)/shard_map/ppermute | solution.py:45
  23.6 6.4 %collective-permute-start.8 = (bf16[48,768]{1,0:T(8,128)(2,1)S(1)}, bf16[48,768]{1,0:T(8,128)(2,1)S(1)}, u32[]{:S(2)}, u32[]{:S(2)}) collective-permute-start(bf16[48,768]{1,0:T(8,128)(2,1)S(1)} %get-tuple-element.80), channel_id=1, source_target_pairs={{0,16},{8,24},{16,0},{24,8},{1,17},{9,25},{17,1},{25,9},{2,18},{10... | collective-permute-start | bytes 221192 | tf_op jit(solution)/shard_map/ppermute | solution.py:45
  25.1 5.3 %collective-permute-start.9 = (bf16[48,768]{1,0:T(8,128)(2,1)S(1)}, bf16[48,768]{1,0:T(8,128)(2,1)S(1)}, u32[]{:S(2)}, u32[]{:S(2)}) collective-permute-start(bf16[48,768]{1,0:T(8,128)(2,1)S(1)} %get-tuple-element.81), channel_id=1, source_target_pairs={{0,24},{8,16},{16,8},{24,0},{1,25},{9,17},{17,9},{25,1},{2,26},{10... | collective-permute-start | bytes 221192 | tf_op jit(solution)/shard_map/ppermute | solution.py:45
  30.3 48.8 %slice-start = ((s8[8388608]{0:T(1024)(128)(4,1)}), s8[4194304]{0:T(1024)(128)(4,1)S(1)}, s32[]{:S(2)}) async-start(s8[8388608]{0:T(1024)(128)(4,1)} %bitcast.48), calls=%async_computation | async-start | bytes 8388608
  34.4 12.0 %collective-permute-start.10 = (bf16[48,384]{1,0:T(8,128)(2,1)S(1)}, bf16[48,384]{1,0:T(8,128)(2,1)S(1)}, u32[]{:S(2)}, u32[]{:S(2)}) collective-permute-start(bf16[48,384]{1,0:T(8,128)(2,1)S(1)} %get-tuple-element.87), channel_id=1, source_target_pairs={{0,8},{8,0},{16,24},{24,16},{1,9},{9,1},{17,25},{25,17},{2,10},{10... | collective-permute-start | bytes 110600 | tf_op jit(solution)/shard_map/ppermute | solution.py:45
  36.2 10.3 %collective-permute-start.11 = (bf16[48,384]{1,0:T(8,128)(2,1)S(1)}, bf16[48,384]{1,0:T(8,128)(2,1)S(1)}, u32[]{:S(2)}, u32[]{:S(2)}) collective-permute-start(bf16[48,384]{1,0:T(8,128)(2,1)S(1)} %get-tuple-element.88), channel_id=1, source_target_pairs={{0,16},{8,24},{16,0},{24,8},{1,17},{9,25},{17,1},{25,9},{2,18},{10... | collective-permute-start | bytes 110600 | tf_op jit(solution)/shard_map/ppermute | solution.py:45
  40.3 6.1 %copy-start.2 = (bf16[256,2048]{1,0:T(8,128)(2,1)S(1)}, bf16[256,2048]{1,0:T(8,128)(2,1)}, u32[]{:S(2)}) copy-start(bf16[256,2048]{1,0:T(8,128)(2,1)} %weights.1) | copy-start | bytes 3145732
  40.3 23.8 %copy-start.5 = (bf16[32,2048]{1,0:T(8,128)(2,1)S(1)}, bf16[32,2048]{1,0:T(8,128)(2,1)}, u32[]{:S(2)}) copy-start(bf16[32,2048]{1,0:T(8,128)(2,1)} %tokens.1) | copy-start | bytes 393220
  40.3 38.9 %slice-start.1 = ((s8[8388608]{0:T(1024)(128)(4,1)}), s8[4194304]{0:T(1024)(128)(4,1)S(1)}, s32[]{:S(2)}) async-start(s8[8388608]{0:T(1024)(128)(4,1)} %bitcast.48), calls=%async_computation.1 | async-start | bytes 8388608
  40.3 6.1 %collective-permute-start.12 = (bf16[48,384]{1,0:T(8,128)(2,1)S(1)}, bf16[48,384]{1,0:T(8,128)(2,1)S(1)}, u32[]{:S(2)}, u32[]{:S(2)}) collective-permute-start(bf16[48,384]{1,0:T(8,128)(2,1)S(1)} %get-tuple-element.89), channel_id=1, source_target_pairs={{0,24},{8,16},{16,8},{24,0},{1,25},{9,17},{17,9},{25,1},{2,26},{10... | collective-permute-start | bytes 110600 | tf_op jit(solution)/shard_map/ppermute | solution.py:45
  46.4 29.0 %copy-start.9 = (bf16[2048]{0:T(1024)(128)(2,1)S(1)}, bf16[2048]{0:T(1024)(128)(2,1)}, u32[]{:S(2)}) copy-start(bf16[2048]{0:T(1024)(128)(2,1)} %param.13) | copy-start | bytes 12292
  47.0 1.6 %collective-permute-start.13 = (bf16[4,32,1024]{2,1,0:T(8,128)(2,1)S(1)}, bf16[4,32,1024]{2,1,0:T(8,128)(2,1)S(1)}, u32[]{:S(2)}, u32[]{:S(2)}) collective-permute-start(bf16[4,32,1024]{2,1,0:T(8,128)(2,1)S(1)} %get-tuple-element.91), channel_id=1, source_target_pairs={{0,1},{1,0},{2,3},{3,2},{4,5},{5,4},{6,7},{7,6},{8,9},{9,8},{10,11... | collective-permute-start | bytes 786440 | tf_op jit(solution)/shard_map/ppermute | solution.py:45
  47.4 4.8 %collective-permute-start.17 = (bf16[4,32,1024]{2,1,0:T(8,128)(2,1)S(1)}, bf16[4,32,1024]{2,1,0:T(8,128)(2,1)S(1)}, u32[]{:S(2)}, u32[]{:S(2)}) collective-permute-start(bf16[4,32,1024]{2,1,0:T(8,128)(2,1)S(1)} %get-tuple-element.94), channel_id=1, source_target_pairs={{0,1},{1,0},{2,3},{3,2},{4,5},{5,4},{6,7},{7,6},{8,9},{9,8},{10,11... | collective-permute-start | bytes 786440 | tf_op jit(solution)/shard_map/ppermute | solution.py:45
  48.7 7.1 %collective-permute-start.14 = (bf16[32,1024]{1,0:T(8,128)(2,1)S(1)}, bf16[32,1024]{1,0:T(8,128)(2,1)S(1)}, u32[]{:S(2)}, u32[]{:S(2)}) collective-permute-start(bf16[32,1024]{1,0:T(8,128)(2,1)S(1)} %get-tuple-element.114), channel_id=1, source_target_pairs={{0,2},{1,3},{2,0},{3,1},{4,6},{5,7},{6,4},{7,5},{8,10},{9,11},{10,... | collective-permute-start | bytes 196616 | tf_op jit(solution)/shard_map/ppermute | solution.py:45
  48.8 7.1 %collective-permute-start.16 = (bf16[32,1024]{1,0:T(8,128)(2,1)S(1)}, bf16[32,1024]{1,0:T(8,128)(2,1)S(1)}, u32[]{:S(2)}, u32[]{:S(2)}) collective-permute-start(bf16[32,1024]{1,0:T(8,128)(2,1)S(1)} %get-tuple-element.115), channel_id=1, source_target_pairs={{0,6},{1,7},{2,4},{3,5},{4,2},{5,3},{6,0},{7,1},{8,14},{9,15},{10,... | collective-permute-start | bytes 196616 | tf_op jit(solution)/shard_map/ppermute | solution.py:45
  51.3 10.5 %collective-permute-start.15 = (bf16[32,1024]{1,0:T(8,128)(2,1)S(1)}, bf16[32,1024]{1,0:T(8,128)(2,1)S(1)}, u32[]{:S(2)}, u32[]{:S(2)}) collective-permute-start(bf16[32,1024]{1,0:T(8,128)(2,1)S(1)} %get-tuple-element.116), channel_id=1, source_target_pairs={{0,4},{1,5},{2,6},{3,7},{4,0},{5,1},{6,2},{7,3},{8,12},{9,13},{10,... | collective-permute-start | bytes 196616 | tf_op jit(solution)/shard_map/ppermute | solution.py:45
  52.3 9.5 %collective-permute-start.18 = (bf16[32,1024]{1,0:T(8,128)(2,1)S(1)}, bf16[32,1024]{1,0:T(8,128)(2,1)S(1)}, u32[]{:S(2)}, u32[]{:S(2)}) collective-permute-start(bf16[32,1024]{1,0:T(8,128)(2,1)S(1)} %get-tuple-element.117), channel_id=1, source_target_pairs={{0,2},{1,3},{2,0},{3,1},{4,6},{5,7},{6,4},{7,5},{8,10},{9,11},{10,... | collective-permute-start | bytes 196616 | tf_op jit(solution)/shard_map/ppermute | solution.py:45
  53.3 8.5 %collective-permute-start.20 = (bf16[32,1024]{1,0:T(8,128)(2,1)S(1)}, bf16[32,1024]{1,0:T(8,128)(2,1)S(1)}, u32[]{:S(2)}, u32[]{:S(2)}) collective-permute-start(bf16[32,1024]{1,0:T(8,128)(2,1)S(1)} %get-tuple-element.118), channel_id=1, source_target_pairs={{0,6},{1,7},{2,4},{3,5},{4,2},{5,3},{6,0},{7,1},{8,14},{9,15},{10,... | collective-permute-start | bytes 196616 | tf_op jit(solution)/shard_map/ppermute | solution.py:45
  55.8 8.2 %collective-permute-start.19 = (bf16[32,1024]{1,0:T(8,128)(2,1)S(1)}, bf16[32,1024]{1,0:T(8,128)(2,1)S(1)}, u32[]{:S(2)}, u32[]{:S(2)}) collective-permute-start(bf16[32,1024]{1,0:T(8,128)(2,1)S(1)} %get-tuple-element.119), channel_id=1, source_target_pairs={{0,4},{1,5},{2,6},{3,7},{4,0},{5,1},{6,2},{7,3},{8,12},{9,13},{10,... | collective-permute-start | bytes 196616 | tf_op jit(solution)/shard_map/ppermute | solution.py:45
  64.2 6.8 %collective-permute-start.33 = (bf16[32,1024]{1,0:T(8,128)(2,1)S(1)}, bf16[32,1024]{1,0:T(8,128)(2,1)S(1)}, u32[]{:S(2)}, u32[]{:S(2)}) collective-permute-start(bf16[32,1024]{1,0:T(8,128)(2,1)S(1)} %get-tuple-element.120.refs_0_), channel_id=1, source_target_pairs={{0,6},{1,7},{2,4},{3,5},{4,2},{5,3},{6,0},{7,1},{8,14},{9,15},{10,... | collective-permute-start | bytes 196616 | tf_op jit(solution)/shard_map/ppermute | solution.py:45
  66.6 6.5 %collective-permute-start.31 = (bf16[32,1024]{1,0:T(8,128)(2,1)S(1)}, bf16[32,1024]{1,0:T(8,128)(2,1)S(1)}, u32[]{:S(2)}, u32[]{:S(2)}) collective-permute-start(bf16[32,1024]{1,0:T(8,128)(2,1)S(1)} %get-tuple-element.120.refs_0_), channel_id=1, source_target_pairs={{0,4},{1,5},{2,6},{3,7},{4,0},{5,1},{6,2},{7,3},{8,12},{9,13},{10,... | collective-permute-start | bytes 196616 | tf_op jit(solution)/shard_map/ppermute | solution.py:45
  66.6 7.3 %collective-permute-start.29 = (bf16[32,1024]{1,0:T(8,128)(2,1)S(1)}, bf16[32,1024]{1,0:T(8,128)(2,1)S(1)}, u32[]{:S(2)}, u32[]{:S(2)}) collective-permute-start(bf16[32,1024]{1,0:T(8,128)(2,1)S(1)} %get-tuple-element.120.refs_0_), channel_id=1, source_target_pairs={{0,2},{1,3},{2,0},{3,1},{4,6},{5,7},{6,4},{7,5},{8,10},{9,11},{10,... | collective-permute-start | bytes 196616 | tf_op jit(solution)/shard_map/ppermute | solution.py:45
  68.6 5.2 %collective-permute-start.28 = (bf16[32,1024]{1,0:T(8,128)(2,1)S(1)}, bf16[32,1024]{1,0:T(8,128)(2,1)S(1)}, u32[]{:S(2)}, u32[]{:S(2)}) collective-permute-start(bf16[32,1024]{1,0:T(8,128)(2,1)S(1)} %get-tuple-element.120.refs_0_), channel_id=1, source_target_pairs={{0,1},{1,0},{2,3},{3,2},{4,5},{5,4},{6,7},{7,6},{8,9},{9,8},{10,11... | collective-permute-start | bytes 196616 | tf_op jit(solution)/shard_map/ppermute | solution.py:45
  68.6 6.8 %collective-permute-start.26 = (bf16[32,1024]{1,0:T(8,128)(2,1)S(1)}, bf16[32,1024]{1,0:T(8,128)(2,1)S(1)}, u32[]{:S(2)}, u32[]{:S(2)}) collective-permute-start(bf16[32,1024]{1,0:T(8,128)(2,1)S(1)} %get-tuple-element.121.refs_0_), channel_id=1, source_target_pairs={{0,6},{1,7},{2,4},{3,5},{4,2},{5,3},{6,0},{7,1},{8,14},{9,15},{10,... | collective-permute-start | bytes 196616 | tf_op jit(solution)/shard_map/ppermute | solution.py:45
  70.9 7.2 %collective-permute-start.24 = (bf16[32,1024]{1,0:T(8,128)(2,1)S(1)}, bf16[32,1024]{1,0:T(8,128)(2,1)S(1)}, u32[]{:S(2)}, u32[]{:S(2)}) collective-permute-start(bf16[32,1024]{1,0:T(8,128)(2,1)S(1)} %get-tuple-element.121.refs_0_), channel_id=1, source_target_pairs={{0,4},{1,5},{2,6},{3,7},{4,0},{5,1},{6,2},{7,3},{8,12},{9,13},{10,... | collective-permute-start | bytes 196616 | tf_op jit(solution)/shard_map/ppermute | solution.py:45
  73.0 5.6 %collective-permute-start.22 = (bf16[32,1024]{1,0:T(8,128)(2,1)S(1)}, bf16[32,1024]{1,0:T(8,128)(2,1)S(1)}, u32[]{:S(2)}, u32[]{:S(2)}) collective-permute-start(bf16[32,1024]{1,0:T(8,128)(2,1)S(1)} %get-tuple-element.121.refs_0_), channel_id=1, source_target_pairs={{0,2},{1,3},{2,0},{3,1},{4,6},{5,7},{6,4},{7,5},{8,10},{9,11},{10,... | collective-permute-start | bytes 196616 | tf_op jit(solution)/shard_map/ppermute | solution.py:45
  73.9 4.8 %collective-permute-start.34 = (bf16[32,1024]{1,0:T(8,128)(2,1)S(1)}, bf16[32,1024]{1,0:T(8,128)(2,1)S(1)}, u32[]{:S(2)}, u32[]{:S(2)}) collective-permute-start(bf16[32,1024]{1,0:T(8,128)(2,1)S(1)} %collective-permute-done.33.refs_6_), channel_id=1, source_target_pairs={{0,1},{1,0},{2,3},{3,2},{4,5},{5,4},{6,7},{7,6},{8,9},{9,8},{10,11... | collective-permute-start | bytes 196616 | tf_op jit(solution)/shard_map/ppermute | solution.py:45
  73.9 5.2 %collective-permute-start.32 = (bf16[32,1024]{1,0:T(8,128)(2,1)S(1)}, bf16[32,1024]{1,0:T(8,128)(2,1)S(1)}, u32[]{:S(2)}, u32[]{:S(2)}) collective-permute-start(bf16[32,1024]{1,0:T(8,128)(2,1)S(1)} %collective-permute-done.31.refs_4_), channel_id=1, source_target_pairs={{0,1},{1,0},{2,3},{3,2},{4,5},{5,4},{6,7},{7,6},{8,9},{9,8},{10,11... | collective-permute-start | bytes 196616 | tf_op jit(solution)/shard_map/ppermute | solution.py:45
  75.4 3.8 %collective-permute-start.30 = (bf16[32,1024]{1,0:T(8,128)(2,1)S(1)}, bf16[32,1024]{1,0:T(8,128)(2,1)S(1)}, u32[]{:S(2)}, u32[]{:S(2)}) collective-permute-start(bf16[32,1024]{1,0:T(8,128)(2,1)S(1)} %collective-permute-done.29.refs_2_), channel_id=1, source_target_pairs={{0,1},{1,0},{2,3},{3,2},{4,5},{5,4},{6,7},{7,6},{8,9},{9,8},{10,11... | collective-permute-start | bytes 196616 | tf_op jit(solution)/shard_map/ppermute | solution.py:45
  75.5 5.1 %copy-start.1 = (bf16[1024,2048]{1,0:T(8,128)(2,1)S(1)}, bf16[1024,2048]{1,0:T(8,128)(2,1)}, u32[]{:S(2)}) copy-start(bf16[1024,2048]{1,0:T(8,128)(2,1)} %down.1) | copy-start | bytes 12582916
  78.1 2.4 %collective-permute-start.21 = (bf16[32,1024]{1,0:T(8,128)(2,1)S(1)}, bf16[32,1024]{1,0:T(8,128)(2,1)S(1)}, u32[]{:S(2)}, u32[]{:S(2)}) collective-permute-start(bf16[32,1024]{1,0:T(8,128)(2,1)S(1)} %get-tuple-element.121.refs_0_), channel_id=1, source_target_pairs={{0,1},{1,0},{2,3},{3,2},{4,5},{5,4},{6,7},{7,6},{8,9},{9,8},{10,11... | collective-permute-start | bytes 196616 | tf_op jit(solution)/shard_map/ppermute | solution.py:45
  78.6 1.9 %collective-permute-start.27 = (bf16[32,1024]{1,0:T(8,128)(2,1)S(1)}, bf16[32,1024]{1,0:T(8,128)(2,1)S(1)}, u32[]{:S(2)}, u32[]{:S(2)}) collective-permute-start(bf16[32,1024]{1,0:T(8,128)(2,1)S(1)} %collective-permute-done.26.refs_6_), channel_id=1, source_target_pairs={{0,1},{1,0},{2,3},{3,2},{4,5},{5,4},{6,7},{7,6},{8,9},{9,8},{10,11... | collective-permute-start | bytes 196616 | tf_op jit(solution)/shard_map/ppermute | solution.py:45
  78.6 1.9 %collective-permute-start.25 = (bf16[32,1024]{1,0:T(8,128)(2,1)S(1)}, bf16[32,1024]{1,0:T(8,128)(2,1)S(1)}, u32[]{:S(2)}, u32[]{:S(2)}) collective-permute-start(bf16[32,1024]{1,0:T(8,128)(2,1)S(1)} %collective-permute-done.24.refs_4_), channel_id=1, source_target_pairs={{0,1},{1,0},{2,3},{3,2},{4,5},{5,4},{6,7},{7,6},{8,9},{9,8},{10,11... | collective-permute-start | bytes 196616 | tf_op jit(solution)/shard_map/ppermute | solution.py:45
  79.1 1.4 %collective-permute-start.23 = (bf16[32,1024]{1,0:T(8,128)(2,1)S(1)}, bf16[32,1024]{1,0:T(8,128)(2,1)S(1)}, u32[]{:S(2)}, u32[]{:S(2)}) collective-permute-start(bf16[32,1024]{1,0:T(8,128)(2,1)S(1)} %collective-permute-done.22.refs_2_), channel_id=1, source_target_pairs={{0,1},{1,0},{2,3},{3,2},{4,5},{5,4},{6,7},{7,6},{8,9},{9,8},{10,11... | collective-permute-start | bytes 196616 | tf_op jit(solution)/shard_map/ppermute | solution.py:45
  82.6 2.0 %collective-permute-start.35 = (bf16[4,32,1024]{2,1,0:T(8,128)(2,1)S(1)}, bf16[4,32,1024]{2,1,0:T(8,128)(2,1)S(1)}, u32[]{:S(2)}, u32[]{:S(2)}) collective-permute-start(bf16[4,32,1024]{2,1,0:T(8,128)(2,1)S(1)} %get-tuple-element.99), channel_id=1, source_target_pairs={{0,1},{1,0},{2,3},{3,2},{4,5},{5,4},{6,7},{7,6},{8,9},{9,8},{10,11... | collective-permute-start | bytes 786440 | tf_op jit(solution)/shard_map/ppermute | solution.py:45
  83.8 4.4 %collective-permute-start.39 = (bf16[4,32,1024]{2,1,0:T(8,128)(2,1)S(1)}, bf16[4,32,1024]{2,1,0:T(8,128)(2,1)S(1)}, u32[]{:S(2)}, u32[]{:S(2)}) collective-permute-start(bf16[4,32,1024]{2,1,0:T(8,128)(2,1)S(1)} %get-tuple-element.102), channel_id=1, source_target_pairs={{0,1},{1,0},{2,3},{3,2},{4,5},{5,4},{6,7},{7,6},{8,9},{9,8},{10,11... | collective-permute-start | bytes 786440 | tf_op jit(solution)/shard_map/ppermute | solution.py:45
  84.7 6.7 %collective-permute-start.36 = (bf16[32,1024]{1,0:T(8,128)(2,1)S(1)}, bf16[32,1024]{1,0:T(8,128)(2,1)S(1)}, u32[]{:S(2)}, u32[]{:S(2)}) collective-permute-start(bf16[32,1024]{1,0:T(8,128)(2,1)S(1)} %get-tuple-element.108), channel_id=1, source_target_pairs={{0,2},{1,3},{2,0},{3,1},{4,6},{5,7},{6,4},{7,5},{8,10},{9,11},{10,... | collective-permute-start | bytes 196616 | tf_op jit(solution)/shard_map/ppermute | solution.py:45
  84.7 7.1 %collective-permute-start.38 = (bf16[32,1024]{1,0:T(8,128)(2,1)S(1)}, bf16[32,1024]{1,0:T(8,128)(2,1)S(1)}, u32[]{:S(2)}, u32[]{:S(2)}) collective-permute-start(bf16[32,1024]{1,0:T(8,128)(2,1)S(1)} %get-tuple-element.109), channel_id=1, source_target_pairs={{0,6},{1,7},{2,4},{3,5},{4,2},{5,3},{6,0},{7,1},{8,14},{9,15},{10,... | collective-permute-start | bytes 196616 | tf_op jit(solution)/shard_map/ppermute | solution.py:45
  86.8 11.2 %collective-permute-start.37 = (bf16[32,1024]{1,0:T(8,128)(2,1)S(1)}, bf16[32,1024]{1,0:T(8,128)(2,1)S(1)}, u32[]{:S(2)}, u32[]{:S(2)}) collective-permute-start(bf16[32,1024]{1,0:T(8,128)(2,1)S(1)} %get-tuple-element.110), channel_id=1, source_target_pairs={{0,4},{1,5},{2,6},{3,7},{4,0},{5,1},{6,2},{7,3},{8,12},{9,13},{10,... | collective-permute-start | bytes 196616 | tf_op jit(solution)/shard_map/ppermute | solution.py:45
  88.3 9.8 %collective-permute-start.40 = (bf16[32,1024]{1,0:T(8,128)(2,1)S(1)}, bf16[32,1024]{1,0:T(8,128)(2,1)S(1)}, u32[]{:S(2)}, u32[]{:S(2)}) collective-permute-start(bf16[32,1024]{1,0:T(8,128)(2,1)S(1)} %get-tuple-element.111), channel_id=1, source_target_pairs={{0,2},{1,3},{2,0},{3,1},{4,6},{5,7},{6,4},{7,5},{8,10},{9,11},{10,... | collective-permute-start | bytes 196616 | tf_op jit(solution)/shard_map/ppermute | solution.py:45
  89.3 8.8 %collective-permute-start.42 = (bf16[32,1024]{1,0:T(8,128)(2,1)S(1)}, bf16[32,1024]{1,0:T(8,128)(2,1)S(1)}, u32[]{:S(2)}, u32[]{:S(2)}) collective-permute-start(bf16[32,1024]{1,0:T(8,128)(2,1)S(1)} %get-tuple-element.112), channel_id=1, source_target_pairs={{0,6},{1,7},{2,4},{3,5},{4,2},{5,3},{6,0},{7,1},{8,14},{9,15},{10,... | collective-permute-start | bytes 196616 | tf_op jit(solution)/shard_map/ppermute | solution.py:45
  91.3 8.8 %collective-permute-start.41 = (bf16[32,1024]{1,0:T(8,128)(2,1)S(1)}, bf16[32,1024]{1,0:T(8,128)(2,1)S(1)}, u32[]{:S(2)}, u32[]{:S(2)}) collective-permute-start(bf16[32,1024]{1,0:T(8,128)(2,1)S(1)} %get-tuple-element.113), channel_id=1, source_target_pairs={{0,4},{1,5},{2,6},{3,7},{4,0},{5,1},{6,2},{7,3},{8,12},{9,13},{10,... | collective-permute-start | bytes 196616 | tf_op jit(solution)/shard_map/ppermute | solution.py:45

commit v3 on v2

v3 whole, which is shorter than its diff:
```python
import functools
import math

import jax
import jax.numpy as jnp
from jax import lax
from jax.experimental import pallas as pl
from jax.experimental.pallas import tpu as pltpu
from jax.sharding import PartitionSpec as P

HD = 64
NORM_EPS = 1e-05
ROPE_BASE = 130000.0
MASK_LOW = -1e30
BF = jnp.bfloat16
F32 = jnp.float32
LANES = 128
Q_TILE = 32
P_TILE = 512


def round_up(count, step):
    return (count + step - 1) // step * step


def dot(left, right):
    return jnp.dot(left, right, preferred_element_type=F32)


def dot_nt(left, right):
    return lax.dot_general(left, right, (((1,), (1,)), ((), ())), preferred_element_type=F32)


def dot_tn(left, right):
    return lax.dot_general(left, right, (((0,), (0,)), ((), ())), preferred_element_type=F32)


def one_hot(row_count, slots):
    rows = lax.broadcasted_iota(jnp.int32, (row_count, slots.shape[1]), 0)
    return jnp.where(rows == slots, 1.0, 0.0).astype(BF)


def swap(values, axis_name, offset):
    count = lax.axis_size(axis_name)
    return lax.ppermute(values, axis_name, [(i, i ^ offset) for i in range(count)])


def gather_tensor(block, beside=None):
    count = lax.axis_size("tensor")
    pieces = [None] * count
    pieces[0] = block
    for k in range(2, count, 2):
        pieces[k] = swap(block, "tensor", k)
    if beside is not None:
        pieces[::2], done = lax.optimization_barrier((pieces[::2], beside()))
    for k in range(0, count, 2):
        pieces[k + 1] = swap(pieces[k], "tensor", 1)
    return pieces if beside is None else (pieces, done)


def reduce_tensor(keep, send):
    count = lax.axis_size("tensor")
    came = swap(send, "tensor", 1)
    joined = [(keep[k].astype(F32) + came[k].astype(F32)).astype(BF) for k in range(count // 2)]
    return [joined[0]] + [swap(joined[k], "tensor", 2 * k) for k in range(1, count // 2)]


def normalize(values, gain):
    wide = values.astype(F32)
    factor = lax.rsqrt(jnp.mean(wide * wide, axis=-1, keepdims=True) + NORM_EPS)
    return (wide * factor * gain.astype(F32)).astype(BF)


def column_of(row):
    count = row.shape[1]
    shape = (count, count)
    same = lax.broadcasted_iota(jnp.int32, shape, 0) == lax.broadcasted_iota(jnp.int32, shape, 1)
    return jnp.sum(jnp.where(same, row, 0.0), axis=1, keepdims=True)


def row_of(column):
    count = column.shape[0]
    shape = (count, count)
    same = lax.broadcasted_iota(jnp.int32, shape, 0) == lax.broadcasted_iota(jnp.int32, shape, 1)
    return jnp.sum(jnp.where(same, column, 0.0), axis=0, keepdims=True)


def picked(row_count, ranks, values):
    rows = lax.broadcasted_iota(jnp.int32, (row_count, ranks.shape[1]), 0).astype(F32)
    return [
        jnp.sum(jnp.where(rows == ranks, value, 0.0), axis=1, keepdims=True) for value in values
    ]


def plan_kernel(sizes, lengths, owners, starts, freqs, *outs):
    groups, count, home_count, slot_rows, sorted_count, cache_rows, rows = sizes
    (
        slots_ref,
        middle_ref,
        own_middle,
        far_pick,
        cos_ref,
        sin_ref,
        home_start,
        home_span,
        home_write,
        home_bounds,
        far_order,
        sort_start,
        sort_span,
        far_write,
        far_bounds,
    ) = outs
    here = lax.axis_index("dp")

    def block(ref, index):
        return ref[:, pl.ds(pl.multiple_of(index * count, LANES), count)]

    def ranks_of(owner, start):
        owner_column, start_column = column_of(owner), column_of(start)
        before = (owner_column == owner) & (start_column < start)
        return jnp.sum(jnp.where(before, 1.0, 0.0), axis=0, keepdims=True)

    def put_ranges(start_ref, span_ref, bounds_ref, start, span):
        start_ref[...] = start.astype(jnp.int32)
        span_ref[...] = span.astype(jnp.int32)
        for tile in range(start.shape[0] // Q_TILE):
            cut = slice(tile * Q_TILE, (tile + 1) * Q_TILE)
            live = span[cut] > 0.0
            low = jnp.min(start[cut]).astype(jnp.int32) // P_TILE
            last = jnp.max(jnp.where(live, start[cut] + span[cut], 0.0)).astype(jnp.int32)
            high = (last + (P_TILE - 1)) // P_TILE
            bounds_ref[0, tile] = jnp.minimum(low, high)
            bounds_ref[1, tile] = high

    my_owner = block(owners, here)
    my_start = block(starts, here).astype(F32)
    my_length = block(lengths, here).astype(F32)
    rank = ranks_of(my_owner.astype(F32), my_start)
    hop = my_owner ^ here
    slot = jnp.where(hop == 0, rank, (hop - 1).astype(F32) * slot_rows + (rank + home_count))
    slots_ref[...] = slot.astype(jnp.int32)
    earlier = column_of(slot) < slot
    place = jnp.sum(jnp.where(earlier, 1.0, 0.0), axis=0, keepdims=True).astype(jnp.int32)
    part = rows // 2
    me = lax.axis_index("tensor")
    middle = (((place // part) ^ me) * part) + place % part
    middle = jnp.where(
        place < count // 2,
        middle,
        (((place - count // 2) // part) ^ me) * part + place % part + count // 2,
    )
    middle_ref[...] = middle
    lane = lax.broadcasted_iota(jnp.int32, (rows, count), 1)
    wanted = lax.broadcasted_iota(jnp.int32, (rows, count), 0) + me * rows
    own_middle[...] = jnp.sum(
        jnp.where(lane == wanted, middle.astype(F32), 0.0), axis=1, keepdims=True
    ).astype(jnp.int32)
    far_count = far_pick.shape[1]
    is_far = jnp.where(hop == 0, 0.0, 1.0)
    shifted = jnp.where(hop == 0, -1.0, slot - home_count)
    taken, offset = picked(far_count, shifted, [is_far, (place - count // 2).astype(F32)])
    far_pick[...] = row_of(jnp.where(taken > 0.0, offset, -1.0)).astype(jnp.int32)
    angles = column_of(my_length) * freqs[...]
    cos_ref[...] = jnp.cos(angles)
    sin_ref[...] = jnp.sin(angles)
    start, span = picked(home_count, slot, [my_start, my_length])
    live = span > 0.0
    start = jnp.where(live, start, float(cache_rows))
    put_ranges(home_start, home_span, home_bounds, start, span)
    home_write[...] = row_of(jnp.where(live, start + span, -1.0)).astype(jnp.int32)

    far = []
    for k in range(1, groups):
        source = here ^ k
        owner = block(owners, source)
        start = block(starts, source).astype(F32)
        rank = ranks_of(owner.astype(F32), start)
        rank = jnp.where(owner == here, rank, -1.0)
        far.append(picked(slot_rows, rank, [start, block(lengths, source).astype(F32)]))
    start = jnp.concatenate([pair[0] for pair in far], axis=0)
    span = jnp.concatenate([pair[1] for pair in far], axis=0)
    live = span > 0.0
    start = jnp.where(live, start, float(cache_rows))
    far_write[...] = row_of(jnp.where(live, start + span, -1.0)).astype(jnp.int32)
    start_row, span_row = row_of(start), row_of(span)
    order = jnp.sum(jnp.where(start < start_row, 1.0, 0.0), axis=0, keepdims=True)
    order = jnp.where(span_row > 0.0, order, -1.0)
    far_order[...] = order.astype(jnp.int32)
    start, span = picked(sorted_count, order, [start_row, span_row])
    start = jnp.where(span > 0.0, start, float(cache_rows))
    put_ranges(sort_start, sort_span, far_bounds, start, span)


def qkv_kernel(piece_count, home_count, slot_rows, hop_count, *refs):
    pieces = refs[:piece_count]
    gain, weights, cosine, sine, slots, middle = refs[piece_count : piece_count + 6]
    home_ref = refs[piece_count + 6]
    out_refs = refs[piece_count + 7 : piece_count + 7 + hop_count]
    token_home, token_far, raw, normed = refs[piece_count + 7 + hop_count :]
    me = lax.axis_index("tensor")
    rows = pieces[0].shape[0]
    for k, piece in enumerate(pieces):
        place = pl.ds(pl.multiple_of((me ^ k) * rows, rows), rows)
        raw[place, :] = piece[...]
        normed[place, :] = normalize(piece[...], gain[...])
    width = weights.shape[2]
    count = normed.shape[0]
    lane = lax.broadcasted_iota(jnp.int32, (count, width), 1)
    low_half = (lane % HD) < HD // 2
    wide = lambda ref: jnp.concatenate([ref[...]] * (width // LANES), axis=1)
    parts = []
    for c in range(3):
        projected = dot(normed[...], weights[c])
        if c < 2:
            ahead = pltpu.roll(projected, width - HD // 2, 1)
            behind = pltpu.roll(projected, HD // 2, 1)
            turned = jnp.where(low_half, -ahead, behind)
            projected = projected * wide(cosine) + turned * wide(sine)
        parts.append(projected.astype(BF))
    packed = jnp.concatenate(parts, axis=1)
    selector = one_hot(home_count + hop_count * slot_rows, slots[...])
    chosen = dot(selector, packed).astype(BF)
    home_ref[...] = chosen[:home_count]
    for k in range(hop_count):
        first = home_count + k * slot_rows
        out_refs[k][...] = chosen[first : first + slot_rows]
    part = rows // 2
    token_home[...] = dot(one_hot(part, middle[...]), raw[...]).astype(BF)
    token_far[...] = dot(one_hot(part, middle[...] - count // 2), raw[...]).astype(BF)


def attend_all(bounds, packed, starts, spans, kv_ref, result, heads, outs):
    width = heads * HD
    rows = Q_TILE
    tiles = packed.shape[0] // rows
    lane_head = lax.broadcasted_iota(jnp.int32, (packed.shape[0], width), 1) // HD
    masks = [lane_head == h for h in range(heads)]
    stack = lambda parts: jnp.concatenate(parts, axis=0)
    query = (packed[:, :width].astype(F32) * (1.0 / math.sqrt(HD))).astype(BF)
    product = query.astype(F32) * packed[:, width : 2 * width].astype(F32)
    owns = [jnp.sum(jnp.where(m, product, 0.0), axis=1, keepdims=True) for m in masks]
    single = [jnp.where(m, query, jnp.zeros_like(query)) for m in masks]
    value = packed[:, 2 * width :].astype(F32)
    tops, totals = [], []
    for tile in range(tiles):
        cut = slice(tile * rows, (tile + 1) * rows)
        own = stack([part[cut] for part in owns])
        stacked = stack([part[cut] for part in single])
        start, span = starts[cut, :], spans[cut, :]

        def advance(step, carry):
            top, total, out = carry
            first = pl.multiple_of(step * P_TILE, P_TILE)
            keys = kv_ref[0, pl.ds(first, P_TILE), :]
            values = kv_ref[1, pl.ds(first, P_TILE), :]
            since = lax.broadcasted_iota(jnp.int32, (rows, P_TILE), 1) + (first - start)
            bias = jnp.where((since >= 0) & (since < span), 0.0, MASK_LOW)
            scores = dot_nt(stacked, keys) + stack([bias] * heads)
            new_top = jnp.maximum(top, jnp.max(scores, axis=1, keepdims=True))
            weights = jnp.exp(scores - new_top)
            factor = jnp.exp(top - new_top)
            total = total * factor + jnp.sum(weights, axis=1, keepdims=True)
            out = out * factor + dot(weights.astype(BF), values)
            return new_top, total, out

        first_carry = (own, jnp.ones_like(own), stack([value[cut]] * heads))
        top, total, out = lax.fori_loop(bounds[0, tile], bounds[1, tile], advance, first_carry)
        tops.append(top)
        totals.append(total)
        outs[tile * heads * rows : (tile + 1) * heads * rows, :] = out
    total = stack(totals)
    log_sum = stack(tops) + jnp.log(total)
    scaled = outs[...] * (1.0 / total)
    pieces = []
    rest = log_sum
    for part in range(3):
        pieces.append(rest.astype(BF).astype(F32))
        rest = rest - pieces[-1]
    lane = lax.broadcasted_iota(jnp.int32, (rows, LANES), 1)
    for tile in range(tiles):
        attended = jnp.zeros((rows, width), F32)
        extra = jnp.zeros((rows, LANES), F32)
        for h in range(heads):
            cut = slice((tile * heads + h) * rows, (tile * heads + h + 1) * rows)
            attended = jnp.where(masks[h][:rows], scaled[cut], attended)
            for part in range(3):
                extra = jnp.where(lane == part * heads + h, pieces[part][cut], extra)
        result[tile * rows : (tile + 1) * rows, :] = jnp.concatenate(
            [attended.astype(BF), extra.astype(BF)], axis=1
        )


def send_middle(attention, weights, keep_ref, send_ref, partial):
    partial[...] = dot(attention, weights[...])
    me = lax.axis_index("tensor")
    part = keep_ref.shape[1]
    for k in range(2 * keep_ref.shape[0]):
        ref = keep_ref if k % 2 == 0 else send_ref
        place = pl.ds(pl.multiple_of((me ^ k) * part, part), part)
        ref[k // 2] = partial[place, :].astype(BF)


def home_kernel(
    heads, bounds, packed, starts, spans, kv_ref, weights, result, keep_ref, send_ref, partial, outs
):
    attend_all(bounds, packed[...], starts, spans, kv_ref, result, heads, outs)
    send_middle(result[:, : heads * HD], weights, keep_ref, send_ref, partial)


def far_kernel(heads, hop_count, sorted_count, bounds, *refs):
    arrived = jnp.concatenate([ref[...] for ref in refs[:hop_count]], axis=0)
    order, starts, spans, kv_ref, _ = refs[hop_count : hop_count + 5]
    outs = refs[hop_count + 5 : 2 * hop_count + 5]
    scratch, state = refs[-2:]
    mover = one_hot(sorted_count, order[...])
    in_order = dot(mover, arrived).astype(BF)
    attend_all(bounds, in_order, starts, spans, kv_ref, scratch, heads, state)
    back = dot_tn(mover, scratch[...]).astype(BF)
    slot_rows = arrived.shape[0] // hop_count
    for k in range(hop_count):
        outs[k][...] = back[k * slot_rows : (k + 1) * slot_rows]


def put_chunks(keep_ref, send_ref, partial, rows):
    me = lax.axis_index("tensor")
    for k in range(partial.shape[0] // rows):
        ref = keep_ref if k % 2 == 0 else send_ref
        ref[k // 2] = partial[pl.ds(pl.multiple_of((me ^ k) * rows, rows), rows), :]


def far_out_kernel(heads, hop_count, slots, far_pick, home, *refs):
    backs = refs[:hop_count]
    weights, log_ref, keep_ref, send_ref, partial = refs[hop_count:]
    width = heads * HD
    far = jnp.concatenate([ref[...] for ref in backs], axis=0)
    placed = dot(one_hot(partial.shape[0], far_pick[...]), far[:, :width]).astype(BF)
    send_middle(placed, weights, keep_ref, send_ref, partial)
    extras = jnp.concatenate([home[:, width:], far[:, width:]], axis=0)
    extra = dot_tn(one_hot(extras.shape[0], slots[...]), extras)
    log_ref[...] = (
        extra + pltpu.roll(extra, LANES - heads, 1) + pltpu.roll(extra, LANES - 2 * heads, 1)
    )


def gate_kernel(piece_count, *refs):
    pieces = refs[:piece_count]
    gain, gate_up, inner_ref = refs[piece_count:]
    values = jnp.concatenate([piece[...] for piece in pieces], axis=0)
    normed = normalize(values, gain[...])
    gate = dot(normed, gate_up[0])
    upward = dot(normed, gate_up[1])
    inner_ref[...] = (gate / (1.0 + jnp.exp(-gate)) * upward).astype(BF)


def down_first_kernel(rows, home, far, middle, down, inner_ref, keep_ref, send_ref, partial):
    half = keep_ref.shape[2]
    both = jnp.concatenate([home[...], far[...]], axis=0)
    inner = dot_tn(one_hot(both.shape[0], middle[...]), both).astype(BF)
    inner_ref[...] = inner
    partial[...] = dot(inner, down[:, :half]).astype(BF)
    put_chunks(keep_ref, send_ref, partial, rows)


def down_second_kernel(rows, inner, down, keep_ref, send_ref, partial):
    half = keep_ref.shape[2]
    partial[...] = dot(inner[...], down[:, half:]).astype(BF)
    put_chunks(keep_ref, send_ref, partial, rows)


def own_rows_kernel(own_middle, *refs):
    pieces = refs[:-1]
    values = jnp.concatenate([piece[...] for piece in pieces], axis=0)
    shape = (own_middle.shape[0], values.shape[0])
    selector = jnp.where(lax.broadcasted_iota(jnp.int32, shape, 1) == own_middle[...], 1.0, 0.0)
    refs[-1][...] = dot(selector.astype(BF), values).astype(BF)


def update_kernel(hop_count, width, home_rows, far_rows, home, *refs):
    far = refs[:hop_count]
    kv_in, kv_out = refs[hop_count:]
    block = kv_in.shape[1]
    position = lax.broadcasted_iota(jnp.int32, (block, 1), 0) + pl.program_id(0) * block
    fresh = jnp.concatenate([home[:, width:]] + [ref[:, width:] for ref in far], axis=0)
    targets = jnp.concatenate([home_rows[...], far_rows[...]], axis=1)
    hit = jnp.where(position == targets, 1.0, 0.0)
    written = jnp.max(hit, axis=1, keepdims=True) > 0.0
    values = dot(hit.astype(BF), fresh).astype(BF)
    kv_out[0] = jnp.where(written, values[:, :width], kv_in[0])
    kv_out[1] = jnp.where(written, values[:, width:], kv_in[1])


def vmem(count):
    return [pl.BlockSpec(memory_space=pltpu.VMEM)] * count


def on_device(
    tokens,
    attn_gain,
    mlp_gain,
    project_in,
    project_out,
    gate_up,
    project_down,
    kv_cache,
    lengths,
    owners,
    cache_start,
):
    groups = lax.axis_size("dp")
    my_index = lax.axis_index("dp")
    tensor_count = lax.axis_size("tensor")
    me = lax.axis_index("tensor")
    rows, model_width = tokens.shape
    request_count = rows * tensor_count
    width = project_in.shape[2]
    heads = width // HD
    cache_rows = kv_cache.shape[1]
    home_count = round_up(request_count - request_count // 2, Q_TILE)
    hops = groups - 1
    capacity = (request_count // 2 + groups - 2) // (groups - 1)
    slot_rows = round_up(capacity, 16)
    far_count = hops * slot_rows
    sorted_count = round_up(min(hops * capacity, far_count), Q_TILE)
    shape = jax.ShapeDtypeStruct
    smem = pl.BlockSpec(memory_space=pltpu.SMEM)
    anywhere = pl.BlockSpec(memory_space=pl.ANY)

    def params(mebibytes):
        return pltpu.CompilerParams(vmem_limit_bytes=mebibytes * 1024 * 1024)

    def cost(flops, bytes_accessed, transcendentals=0):
        return pl.CostEstimate(
            flops=flops, bytes_accessed=bytes_accessed, transcendentals=transcendentals
        )

    ints = lambda *dims: shape(dims, jnp.int32)
    freqs = ROPE_BASE ** (-((jnp.arange(LANES) % (HD // 2)).astype(F32) * 2.0 / HD))
    plan = lambda: pl.pallas_call(
        functools.partial(
            plan_kernel,
            (groups, request_count, home_count, slot_rows, sorted_count, cache_rows, rows),
        ),
        out_shape=[
            ints(1, request_count),
            ints(1, request_count),
            ints(rows, 1),
            ints(1, far_count),
            shape((request_count, LANES), F32),
            shape((request_count, LANES), F32),
            ints(home_count, 1),
            ints(home_count, 1),
            ints(1, home_count),
            ints(2, home_count // Q_TILE),
            ints(1, far_count),
            ints(sorted_count, 1),
            ints(sorted_count, 1),
            ints(1, far_count),
            ints(2, sorted_count // Q_TILE),
        ],
        in_specs=vmem(4),
        out_specs=vmem(9) + [smem] + vmem(4) + [smem],
        compiler_params=params(16),
        cost_estimate=cost(4 * 10**9, 10**6, 10**5),
        name="plan",
    )(lengths[None, :], owners[None, :], cache_start[None, :], freqs[None, :])
    pieces, planned = gather_tensor(tokens, plan)
    (
        slots,
        middle,
        own_middle,
        far_pick,
        cosine,
        sine,
        home_start,
        home_span,
        home_write,
        home_bounds,
        far_order,
        sort_start,
        sort_span,
        far_write,
        far_bounds,
    ) = planned

    part = rows // 2
    middle_count = request_count // 2
    half_count = tensor_count // 2
    packed_outs = pl.pallas_call(
        functools.partial(qkv_kernel, tensor_count, home_count, slot_rows, hops),
        out_shape=[shape((home_count, 3 * width), BF)]
        + [shape((slot_rows, 3 * width), BF)] * hops
        + [shape((part, model_width), BF)] * 2,
        in_specs=vmem(tensor_count + 6),
        out_specs=vmem(3 + hops),
        scratch_shapes=[pltpu.VMEM((request_count, model_width), BF)] * 2,
        compiler_params=params(24),
        name="qkv",
    )(*pieces, attn_gain[None, :], project_in, cosine, sine, slots, middle)
    home_packed = packed_outs[0]
    token_home, token_far = packed_outs[1 + hops :]
    arrived = [swap(packed_outs[k], "dp", k) for k in range(1, groups)]

    out_width = width + LANES
    sums = [shape((half_count, part, model_width), BF)] * 2
    partial_scratch = pltpu.VMEM((middle_count, model_width), F32)
    home_att, keep, send = pl.pallas_call(
        functools.partial(home_kernel, heads),
        out_shape=[shape((home_count, out_width), BF)] + sums,
        in_specs=[smem] + vmem(5),
        out_specs=vmem(3),
        scratch_shapes=[partial_scratch, pltpu.VMEM((home_count * heads, width), F32)],
        compiler_params=params(16),
        cost_estimate=cost(2 * 10**9, 4 * 2**20, 10**6),
        name="home_attention",
    )(home_bounds, home_packed, home_start, home_span, kv_cache, project_out)
    (keep, send), arrived = lax.optimization_barrier(((keep, send), arrived))
    home_sums = reduce_tensor(keep, send)
    far_outs = pl.pallas_call(
        functools.partial(far_kernel, heads, hops, sorted_count),
        out_shape=[shape((slot_rows, out_width), BF)] * hops,
        in_specs=[smem] + vmem(hops + 4) + [anywhere],
        out_specs=vmem(hops),
        scratch_shapes=[
            pltpu.VMEM((sorted_count, out_width), BF),
            pltpu.VMEM((sorted_count * heads, width), F32),
        ],
        compiler_params=params(16),
        cost_estimate=cost(2 * 10**9, 4 * 2**20, 10**6),
        name="far_attention",
    )(far_bounds, *arrived, far_order, sort_start, sort_span, kv_cache, home_att)
    backs = [swap(far_outs[k - 1], "dp", k) for k in range(1, groups)]

    block = 512
    kv_spec = pl.BlockSpec((2, block, width), lambda i: (0, i, 0))
    fixed = lambda array: pl.BlockSpec(array.shape, lambda i: (0,) * array.ndim)
    kv_updated = pl.pallas_call(
        functools.partial(update_kernel, hops, width),
        grid=(cache_rows // block,),
        out_shape=shape(kv_cache.shape, BF),
        in_specs=[fixed(home_write), fixed(far_write), fixed(home_packed)]
        + [fixed(a) for a in arrived]
        + [kv_spec],
        out_specs=kv_spec,
        compiler_params=params(16),
        cost_estimate=cost(2 * 10**9, 8 * 2**20),
        name="cache_update",
    )(home_write, far_write, home_packed, *arrived, kv_cache)

    def add_up(base, sums):
        return (base.astype(F32) + sum(piece.astype(F32) for piece in sums)).astype(BF)

    hidden = gate_up.shape[2]
    gate = lambda pieces, name: pl.pallas_call(
        functools.partial(gate_kernel, tensor_count),
        out_shape=shape((middle_count, hidden), BF),
        in_specs=vmem(tensor_count + 2),
        out_specs=vmem(1)[0],
        compiler_params=params(24),
        cost_estimate=cost(2 * 10**9, 8 * 2**20),
        name=name,
    )(*pieces, mlp_gain[None, :], gate_up)
    home_pieces = gather_tensor(add_up(token_home, home_sums))
    home_inner = gate(home_pieces, "gate_up_home")

    log_sum, keep, send = pl.pallas_call(
        functools.partial(far_out_kernel, heads, hops),
        out_shape=[shape((request_count, LANES), F32)] + sums,
        in_specs=vmem(4 + hops),
        out_specs=vmem(3),
        scratch_shapes=[partial_scratch],
        compiler_params=params(16),
        name="project_out_far",
    )(slots, far_pick, home_att, *backs, project_out)
    log_sum_exp = log_sum[:, :heads]
    far_pieces = gather_tensor(add_up(token_far, reduce_tensor(keep, send)))
    far_inner = gate(far_pieces, "gate_up_far")

    half = model_width // 2
    halves = [shape((half_count, rows, half), BF)] * 2
    row_scratch = [pltpu.VMEM((request_count, half), BF)]
    inner, keep, send = pl.pallas_call(
        functools.partial(down_first_kernel, rows),
        out_shape=[shape((request_count, hidden), BF)] + halves,
        in_specs=vmem(4),
        out_specs=vmem(3),
        scratch_shapes=row_scratch,
        compiler_params=params(16),
        name="down_first",
    )(home_inner, far_inner, middle, project_down)
    sums_first = reduce_tensor(keep, send)
    keep, send = pl.pallas_call(
        functools.partial(down_second_kernel, rows),
        out_shape=halves,
        in_specs=vmem(2),
        out_specs=vmem(2),
        scratch_shapes=row_scratch,
        compiler_params=params(16),
        name="down_second",
    )(inner, project_down)
    sums_second = reduce_tensor(keep, send)
    resid = pl.pallas_call(
        own_rows_kernel,
        out_shape=shape(tokens.shape, BF),
        in_specs=vmem(1 + 2 * tensor_count),
        out_specs=vmem(1)[0],
        compiler_params=params(16),
        name="own_rows",
    )(own_middle, *home_pieces, *far_pieces)
    hidden_states = jnp.concatenate(
        [add_up(resid[:, :half], sums_first), add_up(resid[:, half:], sums_second)], axis=1
    )
    return (hidden_states, log_sum_exp, kv_updated)


def solution(mesh):
    placed = (
        P(("dp", "tensor"), None),
        P(),
        P(),
        P(None, None, "tensor"),
        P("tensor", None),
        P(None, None, "tensor"),
        P("tensor", None),
        P(None, "dp", "tensor"),
        P(),
        P(),
        P(),
    )
    return jax.shard_map(
        on_device,
        mesh=mesh,
        in_specs=placed,
        out_specs=(P(("dp", "tensor"), None), P("dp", "tensor"), P(None, "dp", "tensor")),
        check_vma=False,
    )
```

time: 102 us -> 94.6 us (0.927); the launches traced: 101 us -> 94.9 us
  waiting for transfers between devices: 31 us -> 20.7 us
  Pallas kernels: 22.5 us -> 25.2 us
  starting transfers between devices: 41 us -> 43.5 us
    ppermute x43, waiting for transfers between devices: 31 us -> 20.7 us  [swap(): lax.ppermute(values, axis_name, [(i, i ^ offset) for i in range(count)])]
    ppermute x43, starting transfers between devices: 41 us -> 43.5 us  [swap(): lax.ppermute(values, axis_name, [(i, i ^ offset) for i in range(count)])]
    pallas_call x1, Pallas kernels: 4.04 us -> 5.3 us  [on_device(): pl.pallas_call(functools.partial(far_kernel, heads, hops, sorted_count),...]
  transfers between devices with their start and end apart: 43 -> 43, of which waited for: 15 -> 16; matrix products, arithmetic and copies ran while one was open for 1% -> 1% of each run, Pallas kernels for 14% -> 22%
where the time goes in v3:
time: 94.6 us; the launch traced here: 94.9 us
  starting transfers between devices  43.5 us (46%)
  Pallas kernels  25.2 us (27%)
  waiting for transfers between devices  20.7 us (22%)
  local copies, waits for them, and re-layouts  3.45 us (4%)
  other arithmetic  1.12 us (1%)
    ppermute x43, starting transfers between devices, swap(): lax.ppermute(values, axis_name, [(i, i ^ offset) for i in range(count)])  43.5 us
    ppermute x43, waiting for transfers between devices, swap(): lax.ppermute(values, axis_name, [(i, i ^ offset) for i in range(count)])  20.7 us
    pallas_call x1, Pallas kernels, on_device(): pl.pallas_call(functools.partial(update_kernel, hops, width), grid=(cache...  5.55 us
    pallas_call x1, Pallas kernels, on_device(): pl.pallas_call(functools.partial(far_kernel, heads, hops, sorted_count),...  5.3 us
    pallas_call x1, Pallas kernels, on_device(): pl.pallas_call(functools.partial(home_kernel, heads), out_shape=[shape((h...  4.42 us
    unnamed x25, local copies, waits for them, and re-layouts  3.44 us
    pallas_call x2, Pallas kernels, on_device(): pl.pallas_call(functools.partial(gate_kernel, tensor_count), out_shape=sh...  2.91 us
    pallas_call x1, Pallas kernels, on_device(): pl.pallas_call(functools.partial(qkv_kernel, tensor_count, home_count, sl...  2.31 us
  transfers between devices with their start and end apart: 43, of which 16 were waited for; matrix products, arithmetic and copies ran while one was open for 1% of the time, Pallas kernels for 22%

profile of v3, /device:TPU:0, one launch (start us, length us, event | category | flops | bytes accessed | tf_op | source)
XLA Modules:
  0.0 94.9 jit_solution(12966611556428392862)
XLA Ops:
  0.6 4.1 %collective-permute-start.1 = (bf16[32,2048]{1,0:T(8,128)(2,1)}, bf16[32,2048]{1,0:T(8,128)(2,1)S(1)}, u32[]{:S(2)}, u32[]{:S(2)}) collective-permute-start(bf16[32,2048]{1,0:T(8,128)(2,1)} %refs_0_), channel_id=1, source_target_pairs={{0,4},{1,5},{2,6},{3,7},{4,0},{5,1},{6,2},{7,3},{8,12},{9,13},{10,... | collective-permute-start | bytes 393224 | tf_op jit(solution)/shard_map/ppermute | solution.py:45
  4.7 1.6 %collective-permute-start = (bf16[32,2048]{1,0:T(8,128)(2,1)}, bf16[32,2048]{1,0:T(8,128)(2,1)S(1)}, u32[]{:S(2)}, u32[]{:S(2)}) collective-permute-start(bf16[32,2048]{1,0:T(8,128)(2,1)} %refs_0_), channel_id=1, source_target_pairs={{0,2},{1,3},{2,0},{3,1},{4,6},{5,7},{6,4},{7,5},{8,10},{9,11},{10,... | collective-permute-start | bytes 393224 | tf_op jit(solution)/shard_map/ppermute | solution.py:45
  6.3 0.7 copy-done.5
  7.0 0.7 copy-done.6
  7.7 0.7 copy-done.7
  8.4 2.2 %plan.1 = (s32[1,256]{1,0:T(1,128)S(1)}, s32[1,256]{1,0:T(1,128)S(1)}, s32[32,1]{1,0:T(8,128)S(1)}, s32[1,144]{1,0:T(1,128)S(1)}, f32[256,128]{1,0:T(8,128)S(1)}...) custom-call(s32[1,1024]{1,0:T(1,128)S(1)} %bitcast.51, ...), custom_call_target="tpu_custom_call" | custom-call | flops 4000000000 | bytes 1000000 | tf_op jit(solution)/shard_map/plan/pallas_call | solution.py:439
  10.6 2.3 %collective-permute-done.1.refs_4_ = bf16[32,2048]{1,0:T(8,128)(2,1)S(1)} collective-permute-done((bf16[32,2048]{1,0:T(8,128)(2,1)}, bf16[32,2048]{1,0:T(8,128)(2,1)S(1)}, u32[]{:S(2)}, u32[]{:S(2)}) %collective-permute-start.1) | collective-permute-done | bytes 131104 | tf_op jit(solution)/shard_map/ppermute | solution.py:45
  12.9 2.4 %collective-permute-done.2.refs_6_ = bf16[32,2048]{1,0:T(8,128)(2,1)S(1)} collective-permute-done((bf16[32,2048]{1,0:T(8,128)(2,1)}, bf16[32,2048]{1,0:T(8,128)(2,1)S(1)}, u32[]{:S(2)}, u32[]{:S(2)}) %collective-permute-start.2) | collective-permute-done | bytes 131104 | tf_op jit(solution)/shard_map/ppermute | solution.py:45
  15.3 0.5 collective-permute-start.4
  15.8 0.5 collective-permute-start.6
  16.3 0.3 collective-permute-done.3.refs_1_
  16.6 0.2 collective-permute-done.4.refs_3_
  16.8 0.3 collective-permute-done.5.refs_5_
  17.1 0.2 collective-permute-done.6.refs_7_
  17.3 2.3 %qkv.1 = (bf16[128,768]{1,0:T(8,128)(2,1)S(1)}, bf16[48,768]{1,0:T(8,128)(2,1)S(1)}, bf16[48,768]{1,0:T(8,128)(2,1)S(1)}, bf16[48,768]{1,0:T(8,128)(2,1)S(1)}, b...) custom-call(bf16[32,2048]{1,0:T(8,128)(2,1)S(1)} %copy-done.4, ...), custom_call_target="tpu_custom_call" | custom-call | tf_op jit(solution)/shard_map/qkv/pallas_call | solution.py:489
  19.6 1.5 %collective-permute-start.7 = (bf16[48,768]{1,0:T(8,128)(2,1)S(1)}, bf16[48,768]{1,0:T(8,128)(2,1)S(1)}, u32[]{:S(2)}, u32[]{:S(2)}) collective-permute-start(bf16[48,768]{1,0:T(8,128)(2,1)S(1)} %get-tuple-element.93), channel_id=1, source_target_pairs={{0,8},{8,0},{16,24},{24,16},{1,9},{9,1},{17,25},{25,17},{2,10},{10... | collective-permute-start | bytes 221192 | tf_op jit(solution)/shard_map/ppermute | solution.py:45
  21.1 1.5 %collective-permute-start.8 = (bf16[48,768]{1,0:T(8,128)(2,1)S(1)}, bf16[48,768]{1,0:T(8,128)(2,1)S(1)}, u32[]{:S(2)}, u32[]{:S(2)}) collective-permute-start(bf16[48,768]{1,0:T(8,128)(2,1)S(1)} %get-tuple-element.94), channel_id=1, source_target_pairs={{0,16},{8,24},{16,0},{24,8},{1,17},{9,25},{17,1},{25,9},{2,18},{10... | collective-permute-start | bytes 221192 | tf_op jit(solution)/shard_map/ppermute | solution.py:45
  22.7 0.5 collective-permute-start.9
  23.2 4.4 %home_attention.1 = (bf16[128,384]{1,0:T(8,128)(2,1)S(1)}, bf16[4,16,2048]{2,1,0:T(8,128)(2,1)S(1)}, bf16[4,16,2048]{2,1,0:T(8,128)(2,1)S(1)}) custom-call(s32[2,4]{1,0:T(2,128)S(1)} %get-tuple-element.87.bounds, bf16[128,768]{1,0:T(8,128)(2,1)S(1)} %get-tuple-element.88.packed.home, s32[128,1]{1,0:T(8,128)S(1)} %get-tuple-element.89.starts, ...), custom_call_target="tpu_custom_call" | custom-call | flops 2000000000 | bytes 4194304 | tf_op jit(solution)/shard_map/home_attention/pallas_call | solution.py:507
  27.6 0.3 collective-permute-done.9.refs_2_
  27.9 5.3 %far_attention.1 = (bf16[48,384]{1,0:T(8,128)(2,1)S(1)}, bf16[48,384]{1,0:T(8,128)(2,1)S(1)}, bf16[48,384]{1,0:T(8,128)(2,1)S(1)}) custom-call(s32[2,5]{1,0:T(2,128)S(1)} %get-tuple-element.101.bounds, bf16[48,768]{1,0:T(8,128)(2,1)S(1)} %collective-permute-done.7.refs_0_, bf16[48,768]{1,0:T(8,128)(2,1)S(1)} %collective-permute-done.8.refs_1_, ...), custom_call_target="tpu_custom_call" | custom-call | flops 2000000000 | bytes 4194304 | tf_op jit(solution)/shard_map/far_attention/pallas_call | solution.py:519
  33.2 3.4 %collective-permute-start.21 = (bf16[48,384]{1,0:T(8,128)(2,1)S(1)}, bf16[48,384]{1,0:T(8,128)(2,1)S(1)}, u32[]{:S(2)}, u32[]{:S(2)}) collective-permute-start(bf16[48,384]{1,0:T(8,128)(2,1)S(1)} %get-tuple-element.108), channel_id=1, source_target_pairs={{0,8},{8,0},{16,24},{24,16},{1,9},{9,1},{17,25},{25,17},{2,10},{10... | collective-permute-start | bytes 110600 | tf_op jit(solution)/shard_map/ppermute | solution.py:45
  36.6 1.5 %collective-permute-start.23 = (bf16[48,384]{1,0:T(8,128)(2,1)S(1)}, bf16[48,384]{1,0:T(8,128)(2,1)S(1)}, u32[]{:S(2)}, u32[]{:S(2)}) collective-permute-start(bf16[48,384]{1,0:T(8,128)(2,1)S(1)} %get-tuple-element.110), channel_id=1, source_target_pairs={{0,24},{8,16},{16,8},{24,0},{1,25},{9,17},{17,9},{25,1},{2,26},{10... | collective-permute-start | bytes 110600 | tf_op jit(solution)/shard_map/ppermute | solution.py:45
  38.2 0.6 collective-permute-done.21.refs_0_
  38.7 2.2 %collective-permute-done.22.refs_1_ = bf16[48,384]{1,0:T(8,128)(2,1)S(1)} collective-permute-done((bf16[48,384]{1,0:T(8,128)(2,1)S(1)}, bf16[48,384]{1,0:T(8,128)(2,1)S(1)}, u32[]{:S(2)}, u32[]{:S(2)}) %collective-permute-start.22) | collective-permute-done | bytes 36896 | tf_op jit(solution)/shard_map/ppermute | solution.py:45
  41.0 0.5 collective-permute-done.23.refs_2_
  41.5 0.6 project_out_far.1
  42.1 0.1 collective-permute-start.24
  42.2 2.5 %collective-permute-start.11 = (bf16[16,2048]{1,0:T(8,128)(2,1)S(1)}, bf16[16,2048]{1,0:T(8,128)(2,1)S(1)}, u32[]{:S(2)}, u32[]{:S(2)}) collective-permute-start(bf16[16,2048]{1,0:T(8,128)(2,1)S(1)} %get-tuple-element.133), channel_id=1, source_target_pairs={{0,2},{1,3},{2,0},{3,1},{4,6},{5,7},{6,4},{7,5},{8,10},{9,11},{10,... | collective-permute-start | bytes 196616 | tf_op jit(solution)/shard_map/ppermute | solution.py:45
  44.7 3.3 %collective-permute-start.13 = (bf16[16,2048]{1,0:T(8,128)(2,1)S(1)}, bf16[16,2048]{1,0:T(8,128)(2,1)S(1)}, u32[]{:S(2)}, u32[]{:S(2)}) collective-permute-start(bf16[16,2048]{1,0:T(8,128)(2,1)S(1)} %get-tuple-element.134), channel_id=1, source_target_pairs={{0,6},{1,7},{2,4},{3,5},{4,2},{5,3},{6,0},{7,1},{8,14},{9,15},{10,... | collective-permute-start | bytes 196616 | tf_op jit(solution)/shard_map/ppermute | solution.py:45
  48.0 1.2 %collective-permute-start.25 = (bf16[16,2048]{1,0:T(8,128)(2,1)S(1)}, bf16[16,2048]{1,0:T(8,128)(2,1)S(1)}, u32[]{:S(2)}, u32[]{:S(2)}) collective-permute-start(bf16[16,2048]{1,0:T(8,128)(2,1)S(1)} %get-tuple-element.130), channel_id=1, source_target_pairs={{0,2},{1,3},{2,0},{3,1},{4,6},{5,7},{6,4},{7,5},{8,10},{9,11},{10,... | collective-permute-start | bytes 196616 | tf_op jit(solution)/shard_map/ppermute | solution.py:45
  49.2 3.3 %collective-permute-start.27 = (bf16[16,2048]{1,0:T(8,128)(2,1)S(1)}, bf16[16,2048]{1,0:T(8,128)(2,1)S(1)}, u32[]{:S(2)}, u32[]{:S(2)}) collective-permute-start(bf16[16,2048]{1,0:T(8,128)(2,1)S(1)} %get-tuple-element.131), channel_id=1, source_target_pairs={{0,6},{1,7},{2,4},{3,5},{4,2},{5,3},{6,0},{7,1},{8,14},{9,15},{10,... | collective-permute-start | bytes 196616 | tf_op jit(solution)/shard_map/ppermute | solution.py:45
  52.5 5.0 %collective-permute-done.12 = bf16[16,2048]{1,0:T(8,128)(2,1)S(1)} collective-permute-done((bf16[16,2048]{1,0:T(8,128)(2,1)S(1)}, bf16[16,2048]{1,0:T(8,128)(2,1)S(1)}, u32[]{:S(2)}, u32[]{:S(2)}) %collective-permute-start.12) | collective-permute-done | bytes 65568 | tf_op jit(solution)/shard_map/ppermute | solution.py:45
  57.6 2.2 %collective-permute-start.19 = (bf16[16,2048]{1,0:T(8,128)(2,1)S(1)}, bf16[16,2048]{1,0:T(8,128)(2,1)S(1)}, u32[]{:S(2)}, u32[]{:S(2)}) collective-permute-start(bf16[16,2048]{1,0:T(8,128)(2,1)S(1)} %fusion.15.refs_0_), channel_id=1, source_target_pairs={{0,6},{1,7},{2,4},{3,5},{4,2},{5,3},{6,0},{7,1},{8,14},{9,15},{10,... | collective-permute-start | bytes 196616 | tf_op jit(solution)/shard_map/ppermute | solution.py:45
  59.8 2.2 %collective-permute-start.15 = (bf16[16,2048]{1,0:T(8,128)(2,1)S(1)}, bf16[16,2048]{1,0:T(8,128)(2,1)S(1)}, u32[]{:S(2)}, u32[]{:S(2)}) collective-permute-start(bf16[16,2048]{1,0:T(8,128)(2,1)S(1)} %fusion.15.refs_0_), channel_id=1, source_target_pairs={{0,2},{1,3},{2,0},{3,1},{4,6},{5,7},{6,4},{7,5},{8,10},{9,11},{10,... | collective-permute-start | bytes 196616 | tf_op jit(solution)/shard_map/ppermute | solution.py:45
  62.2 2.2 %collective-permute-start.33 = (bf16[16,2048]{1,0:T(8,128)(2,1)S(1)}, bf16[16,2048]{1,0:T(8,128)(2,1)S(1)}, u32[]{:S(2)}, u32[]{:S(2)}) collective-permute-start(bf16[16,2048]{1,0:T(8,128)(2,1)S(1)} %fusion.11.refs_8_.refs_0_), channel_id=1, source_target_pairs={{0,6},{1,7},{2,4},{3,5},{4,2},{5,3},{6,0},{7,1},{8,14},{9,15},{10,... | collective-permute-start | bytes 196616 | tf_op jit(solution)/shard_map/ppermute | solution.py:45
  64.4 1.5 %collective-permute-start.31 = (bf16[16,2048]{1,0:T(8,128)(2,1)S(1)}, bf16[16,2048]{1,0:T(8,128)(2,1)S(1)}, u32[]{:S(2)}, u32[]{:S(2)}) collective-permute-start(bf16[16,2048]{1,0:T(8,128)(2,1)S(1)} %fusion.11.refs_8_.refs_0_), channel_id=1, source_target_pairs={{0,4},{1,5},{2,6},{3,7},{4,0},{5,1},{6,2},{7,3},{8,12},{9,13},{10,... | collective-permute-start | bytes 196616 | tf_op jit(solution)/shard_map/ppermute | solution.py:45
  65.8 0.2 collective-permute-done.17.refs_4_
  66.0 0.6 collective-permute-start.29
  66.6 0.5 collective-permute-start.18
  67.1 1.9 %collective-permute-done.33.refs_14_.refs_6_ = bf16[16,2048]{1,0:T(8,128)(2,1)S(1)} collective-permute-done((bf16[16,2048]{1,0:T(8,128)(2,1)S(1)}, bf16[16,2048]{1,0:T(8,128)(2,1)S(1)}, u32[]{:S(2)}, u32[]{:S(2)}) %collective-permute-start.33) | collective-permute-done | bytes 65568 | tf_op jit(solution)/shard_map/ppermute | solution.py:45
  69.0 2.6 %collective-permute-done.31.refs_12_.refs_4_ = bf16[16,2048]{1,0:T(8,128)(2,1)S(1)} collective-permute-done((bf16[16,2048]{1,0:T(8,128)(2,1)S(1)}, bf16[16,2048]{1,0:T(8,128)(2,1)S(1)}, u32[]{:S(2)}, u32[]{:S(2)}) %collective-permute-start.31) | collective-permute-done | bytes 65568 | tf_op jit(solution)/shard_map/ppermute | solution.py:45
  71.7 0.5 collective-permute-start.34
  72.2 0.4 collective-permute-start.30
  72.7 1.5 %gate_up_home.1.home = bf16[128,1024]{1,0:T(8,128)(2,1)S(1)} custom-call(bf16[16,2048]{1,0:T(8,128)(2,1)S(1)} %fusion.15.refs_0_, bf16[16,2048]{1,0:T(8,128)(2,1)S(1)} %collective-permute-done.14.refs_1_, bf16[16,2048]{1,0:T(8,128)(2,1)S(1)} %collective-permute-done.15.refs_2_, bf16[16,2048]{1,0:T(8,128)(2,1)S(1)} %collective-permute-done.16.refs_3_, ...), custom_call_target="tpu_custom_call" | custom-call | flops 2000000000 | bytes 8388608 | tf_op jit(solution)/shard_map/gate_up_home/pallas_call | solution.py:554
  74.2 1.5 %gate_up_far.1.far = bf16[128,1024]{1,0:T(8,128)(2,1)S(1)} custom-call(bf16[16,2048]{1,0:T(8,128)(2,1)S(1)} %fusion.11.refs_8_.refs_0_, bf16[16,2048]{1,0:T(8,128)(2,1)S(1)} %collective-permute-done.28.refs_9_.refs_1_, bf16[16,2048]{1,0:T(8,128)(2,1)S(1)} %collective-permute-done.29.refs_10_.refs_2_, ...), custom_call_target="tpu_custom_call" | custom-call | flops 2000000000 | bytes 8388608 | tf_op jit(solution)/shard_map/gate_up_far/pallas_call | solution.py:554
  75.6 0.7 copy-done
  76.3 0.9 down_first.1
  77.2 0.1 collective-permute-start.35
  77.4 0.8 down_second.1
  78.1 0.5 collective-permute-start.39
  78.6 0.2 collective-permute-done.35
  78.9 0.1 collective-permute-start.36
  79.0 1.9 %collective-permute-start.38 = (bf16[32,1024]{1,0:T(8,128)(2,1)S(1)}, bf16[32,1024]{1,0:T(8,128)(2,1)S(1)}, u32[]{:S(2)}, u32[]{:S(2)}) collective-permute-start(bf16[32,1024]{1,0:T(8,128)(2,1)S(1)} %get-tuple-element.125), channel_id=1, source_target_pairs={{0,6},{1,7},{2,4},{3,5},{4,2},{5,3},{6,0},{7,1},{8,14},{9,15},{10,... | collective-permute-start | bytes 196616 | tf_op jit(solution)/shard_map/ppermute | solution.py:45
  80.9 1.6 %collective-permute-start.37 = (bf16[32,1024]{1,0:T(8,128)(2,1)S(1)}, bf16[32,1024]{1,0:T(8,128)(2,1)S(1)}, u32[]{:S(2)}, u32[]{:S(2)}) collective-permute-start(bf16[32,1024]{1,0:T(8,128)(2,1)S(1)} %get-tuple-element.126), channel_id=1, source_target_pairs={{0,4},{1,5},{2,6},{3,7},{4,0},{5,1},{6,2},{7,3},{8,12},{9,13},{10,... | collective-permute-start | bytes 196616 | tf_op jit(solution)/shard_map/ppermute | solution.py:45
  82.5 1.0 %collective-permute-start.40 = (bf16[32,1024]{1,0:T(8,128)(2,1)S(1)}, bf16[32,1024]{1,0:T(8,128)(2,1)S(1)}, u32[]{:S(2)}, u32[]{:S(2)}) collective-permute-start(bf16[32,1024]{1,0:T(8,128)(2,1)S(1)} %get-tuple-element.127), channel_id=1, source_target_pairs={{0,2},{1,3},{2,0},{3,1},{4,6},{5,7},{6,4},{7,5},{8,10},{9,11},{10,... | collective-permute-start | bytes 196616 | tf_op jit(solution)/shard_map/ppermute | solution.py:45
  83.5 1.9 %collective-permute-start.42 = (bf16[32,1024]{1,0:T(8,128)(2,1)S(1)}, bf16[32,1024]{1,0:T(8,128)(2,1)S(1)}, u32[]{:S(2)}, u32[]{:S(2)}) collective-permute-start(bf16[32,1024]{1,0:T(8,128)(2,1)S(1)} %get-tuple-element.128), channel_id=1, source_target_pairs={{0,6},{1,7},{2,4},{3,5},{4,2},{5,3},{6,0},{7,1},{8,14},{9,15},{10,... | collective-permute-start | bytes 196616 | tf_op jit(solution)/shard_map/ppermute | solution.py:45
  85.4 0.7 collective-permute-start.41
  86.1 5.6 %cache_update.1 = bf16[2,4096,256]{2,1,0:T(8,128)(2,1)} custom-call(s32[1,128]{1,0:T(1,128)S(1)} %get-tuple-element.119.home_rows, s32[1,144]{1,0:T(1,128)S(1)} %get-tuple-element.120.far_rows, bf16[128,768]{1,0:T(8,128)(2,1)S(1)} %get-tuple-element.88.packed.home, bf16[48,768]{1,0:T(8,128)(2,1)S(1)} %collective-permute-done.7.refs_0_, ...), custom_call_target="tpu_custom_call" | custom-call | flops 2000000000 | bytes 8388608 | tf_op jit(solution)/shard_map/cache_update/pallas_call | solution.py:537
  91.6 0.7 copy.14
  92.3 0.3 own_rows.1
  92.7 1.5 %collective-permute-done.41 = bf16[32,1024]{1,0:T(8,128)(2,1)S(1)} collective-permute-done((bf16[32,1024]{1,0:T(8,128)(2,1)S(1)}, bf16[32,1024]{1,0:T(8,128)(2,1)S(1)}, u32[]{:S(2)}, u32[]{:S(2)}) %collective-permute-start.41) | collective-permute-done | bytes 65568 | tf_op jit(solution)/shard_map/ppermute | solution.py:45
  94.1 0.1 fusion.7
  94.2 0.7 pad_maximum_fusion
  (70 shorter events, 0.6 us)
Async XLA Ops:
  0.6 12.3 %collective-permute-start.1 = (bf16[32,2048]{1,0:T(8,128)(2,1)}, bf16[32,2048]{1,0:T(8,128)(2,1)S(1)}, u32[]{:S(2)}, u32[]{:S(2)}) collective-permute-start(bf16[32,2048]{1,0:T(8,128)(2,1)} %refs_0_), channel_id=1, source_target_pairs={{0,4},{1,5},{2,6},{3,7},{4,0},{5,1},{6,2},{7,3},{8,12},{9,13},{10,... | collective-permute-start | bytes 393224 | tf_op jit(solution)/shard_map/ppermute | solution.py:45
  4.7 8.2 %collective-permute-start = (bf16[32,2048]{1,0:T(8,128)(2,1)}, bf16[32,2048]{1,0:T(8,128)(2,1)S(1)}, u32[]{:S(2)}, u32[]{:S(2)}) collective-permute-start(bf16[32,2048]{1,0:T(8,128)(2,1)} %refs_0_), channel_id=1, source_target_pairs={{0,2},{1,3},{2,0},{3,1},{4,6},{5,7},{6,4},{7,5},{8,10},{9,11},{10,... | collective-permute-start | bytes 393224 | tf_op jit(solution)/shard_map/ppermute | solution.py:45
  6.3 9.0 %collective-permute-start.2 = (bf16[32,2048]{1,0:T(8,128)(2,1)}, bf16[32,2048]{1,0:T(8,128)(2,1)S(1)}, u32[]{:S(2)}, u32[]{:S(2)}) collective-permute-start(bf16[32,2048]{1,0:T(8,128)(2,1)} %refs_0_), channel_id=1, source_target_pairs={{0,6},{1,7},{2,4},{3,5},{4,2},{5,3},{6,0},{7,1},{8,14},{9,15},{10,... | collective-permute-start | bytes 393224 | tf_op jit(solution)/shard_map/ppermute | solution.py:45
  6.3 0.7 copy-start.5
  7.0 0.7 copy-start.6
  7.7 0.7 copy-start.7
  8.4 6.9 %copy-start.4 = (bf16[32,2048]{1,0:T(8,128)(2,1)S(1)}, bf16[32,2048]{1,0:T(8,128)(2,1)}, u32[]{:S(2)}) copy-start(bf16[32,2048]{1,0:T(8,128)(2,1)} %refs_0_) | copy-start | bytes 393220
  8.4 7.9 %copy-start.8 = (bf16[2048]{0:T(1024)(128)(2,1)S(1)}, bf16[2048]{0:T(1024)(128)(2,1)}, u32[]{:S(2)}) copy-start(bf16[2048]{0:T(1024)(128)(2,1)} %param.12) | copy-start | bytes 12292
  8.4 8.9 %copy-start.2 = (bf16[3,2048,256]{2,1,0:T(8,128)(2,1)S(1)}, bf16[3,2048,256]{2,1,0:T(8,128)(2,1)}, u32[]{:S(2)}) copy-start(bf16[3,2048,256]{2,1,0:T(8,128)(2,1)} %refs_9_.3) | copy-start | bytes 9437188
  8.4 14.8 %copy-start.3 = (bf16[256,2048]{1,0:T(8,128)(2,1)S(1)}, bf16[256,2048]{1,0:T(8,128)(2,1)}, u32[]{:S(2)}) copy-start(bf16[256,2048]{1,0:T(8,128)(2,1)} %refs_3_.2) | copy-start | bytes 3145732
  10.6 12.6 %copy-start.1 = (bf16[2,4096,256]{2,1,0:T(8,128)(2,1)S(1)}, bf16[2,4096,256]{2,1,0:T(8,128)(2,1)}, u32[]{:S(2)}) copy-start(bf16[2,4096,256]{2,1,0:T(8,128)(2,1)} %refs_3_.3) | copy-start | bytes 12582916
  15.3 1.3 %collective-permute-start.3 = (bf16[32,2048]{1,0:T(8,128)(2,1)S(1)}, bf16[32,2048]{1,0:T(8,128)(2,1)S(1)}, u32[]{:S(2)}, u32[]{:S(2)}) collective-permute-start(bf16[32,2048]{1,0:T(8,128)(2,1)S(1)} %copy-done.4), channel_id=1, source_target_pairs={{0,1},{1,0},{2,3},{3,2},{4,5},{5,4},{6,7},{7,6},{8,9},{9,8},{10,11... | collective-permute-start | bytes 393224 | tf_op jit(solution)/shard_map/ppermute | solution.py:45
  15.3 1.5 %collective-permute-start.4 = (bf16[32,2048]{1,0:T(8,128)(2,1)S(1)}, bf16[32,2048]{1,0:T(8,128)(2,1)S(1)}, u32[]{:S(2)}, u32[]{:S(2)}) collective-permute-start(bf16[32,2048]{1,0:T(8,128)(2,1)S(1)} %collective-permute-done.refs_2_), channel_id=1, source_target_pairs={{0,1},{1,0},{2,3},{3,2},{4,5},{5,4},{6,7},{7,6},{8,9},{9,8},{10,11... | collective-permute-start | bytes 393224 | tf_op jit(solution)/shard_map/ppermute | solution.py:45
  15.8 1.3 %collective-permute-start.5 = (bf16[32,2048]{1,0:T(8,128)(2,1)S(1)}, bf16[32,2048]{1,0:T(8,128)(2,1)S(1)}, u32[]{:S(2)}, u32[]{:S(2)}) collective-permute-start(bf16[32,2048]{1,0:T(8,128)(2,1)S(1)} %collective-permute-done.1.refs_4_), channel_id=1, source_target_pairs={{0,1},{1,0},{2,3},{3,2},{4,5},{5,4},{6,7},{7,6},{8,9},{9,8},{10,11... | collective-permute-start | bytes 393224 | tf_op jit(solution)/shard_map/ppermute | solution.py:45
  15.8 1.5 %collective-permute-start.6 = (bf16[32,2048]{1,0:T(8,128)(2,1)S(1)}, bf16[32,2048]{1,0:T(8,128)(2,1)S(1)}, u32[]{:S(2)}, u32[]{:S(2)}) collective-permute-start(bf16[32,2048]{1,0:T(8,128)(2,1)S(1)} %collective-permute-done.2.refs_6_), channel_id=1, source_target_pairs={{0,1},{1,0},{2,3},{3,2},{4,5},{5,4},{6,7},{7,6},{8,9},{9,8},{10,11... | collective-permute-start | bytes 393224 | tf_op jit(solution)/shard_map/ppermute | solution.py:45
  19.6 7.9 %collective-permute-start.7 = (bf16[48,768]{1,0:T(8,128)(2,1)S(1)}, bf16[48,768]{1,0:T(8,128)(2,1)S(1)}, u32[]{:S(2)}, u32[]{:S(2)}) collective-permute-start(bf16[48,768]{1,0:T(8,128)(2,1)S(1)} %get-tuple-element.93), channel_id=1, source_target_pairs={{0,8},{8,0},{16,24},{24,16},{1,9},{9,1},{17,25},{25,17},{2,10},{10... | collective-permute-start | bytes 221192 | tf_op jit(solution)/shard_map/ppermute | solution.py:45
  21.1 6.5 %collective-permute-start.8 = (bf16[48,768]{1,0:T(8,128)(2,1)S(1)}, bf16[48,768]{1,0:T(8,128)(2,1)S(1)}, u32[]{:S(2)}, u32[]{:S(2)}) collective-permute-start(bf16[48,768]{1,0:T(8,128)(2,1)S(1)} %get-tuple-element.94), channel_id=1, source_target_pairs={{0,16},{8,24},{16,0},{24,8},{1,17},{9,25},{17,1},{25,9},{2,18},{10... | collective-permute-start | bytes 221192 | tf_op jit(solution)/shard_map/ppermute | solution.py:45
  22.7 5.3 %collective-permute-start.9 = (bf16[48,768]{1,0:T(8,128)(2,1)S(1)}, bf16[48,768]{1,0:T(8,128)(2,1)S(1)}, u32[]{:S(2)}, u32[]{:S(2)}) collective-permute-start(bf16[48,768]{1,0:T(8,128)(2,1)S(1)} %get-tuple-element.95), channel_id=1, source_target_pairs={{0,24},{8,16},{16,8},{24,0},{1,25},{9,17},{17,9},{25,1},{2,26},{10... | collective-permute-start | bytes 221192 | tf_op jit(solution)/shard_map/ppermute | solution.py:45
  23.2 49.5 %slice-start = ((s8[8388608]{0:T(1024)(128)(4,1)}), s8[4194304]{0:T(1024)(128)(4,1)S(1)}, s32[]{:S(2)}) async-start(s8[8388608]{0:T(1024)(128)(4,1)} %bitcast.48), calls=%async_computation | async-start | bytes 8388608
  27.9 14.2 %collective-permute-start.10 = (bf16[4,16,2048]{2,1,0:T(8,128)(2,1)S(1)}, bf16[4,16,2048]{2,1,0:T(8,128)(2,1)S(1)}, u32[]{:S(2)}, u32[]{:S(2)}) collective-permute-start(bf16[4,16,2048]{2,1,0:T(8,128)(2,1)S(1)} %get-tuple-element.97), channel_id=1, source_target_pairs={{0,1},{1,0},{2,3},{3,2},{4,5},{5,4},{6,7},{7,6},{8,9},{9,8},{10,11... | collective-permute-start | bytes 786440 | tf_op jit(solution)/shard_map/ppermute | solution.py:45
  27.9 41.1 %copy-start.9 = (bf16[2048]{0:T(1024)(128)(2,1)S(1)}, bf16[2048]{0:T(1024)(128)(2,1)}, u32[]{:S(2)}) copy-start(bf16[2048]{0:T(1024)(128)(2,1)} %param.13) | copy-start | bytes 12292
  27.9 44.7 %slice-start.1 = ((s8[8388608]{0:T(1024)(128)(4,1)}), s8[4194304]{0:T(1024)(128)(4,1)S(1)}, s32[]{:S(2)}) async-start(s8[8388608]{0:T(1024)(128)(4,1)} %bitcast.48), calls=%async_computation.1 | async-start | bytes 8388608
  33.2 5.5 %collective-permute-start.21 = (bf16[48,384]{1,0:T(8,128)(2,1)S(1)}, bf16[48,384]{1,0:T(8,128)(2,1)S(1)}, u32[]{:S(2)}, u32[]{:S(2)}) collective-permute-start(bf16[48,384]{1,0:T(8,128)(2,1)S(1)} %get-tuple-element.108), channel_id=1, source_target_pairs={{0,8},{8,0},{16,24},{24,16},{1,9},{9,1},{17,25},{25,17},{2,10},{10... | collective-permute-start | bytes 110600 | tf_op jit(solution)/shard_map/ppermute | solution.py:45
  36.6 4.4 %collective-permute-start.22 = (bf16[48,384]{1,0:T(8,128)(2,1)S(1)}, bf16[48,384]{1,0:T(8,128)(2,1)S(1)}, u32[]{:S(2)}, u32[]{:S(2)}) collective-permute-start(bf16[48,384]{1,0:T(8,128)(2,1)S(1)} %get-tuple-element.109), channel_id=1, source_target_pairs={{0,16},{8,24},{16,0},{24,8},{1,17},{9,25},{17,1},{25,9},{2,18},{10... | collective-permute-start | bytes 110600 | tf_op jit(solution)/shard_map/ppermute | solution.py:45
  36.6 4.9 %collective-permute-start.23 = (bf16[48,384]{1,0:T(8,128)(2,1)S(1)}, bf16[48,384]{1,0:T(8,128)(2,1)S(1)}, u32[]{:S(2)}, u32[]{:S(2)}) collective-permute-start(bf16[48,384]{1,0:T(8,128)(2,1)S(1)} %get-tuple-element.110), channel_id=1, source_target_pairs={{0,24},{8,16},{16,8},{24,0},{1,25},{9,17},{17,9},{25,1},{2,26},{10... | collective-permute-start | bytes 110600 | tf_op jit(solution)/shard_map/ppermute | solution.py:45
  42.1 5.9 %collective-permute-start.24 = (bf16[4,16,2048]{2,1,0:T(8,128)(2,1)S(1)}, bf16[4,16,2048]{2,1,0:T(8,128)(2,1)S(1)}, u32[]{:S(2)}, u32[]{:S(2)}) collective-permute-start(bf16[4,16,2048]{2,1,0:T(8,128)(2,1)S(1)} %get-tuple-element.112), channel_id=1, source_target_pairs={{0,1},{1,0},{2,3},{3,2},{4,5},{5,4},{6,7},{7,6},{8,9},{9,8},{10,11... | collective-permute-start | bytes 786440 | tf_op jit(solution)/shard_map/ppermute | solution.py:45
  42.2 10.3 %collective-permute-start.11 = (bf16[16,2048]{1,0:T(8,128)(2,1)S(1)}, bf16[16,2048]{1,0:T(8,128)(2,1)S(1)}, u32[]{:S(2)}, u32[]{:S(2)}) collective-permute-start(bf16[16,2048]{1,0:T(8,128)(2,1)S(1)} %get-tuple-element.133), channel_id=1, source_target_pairs={{0,2},{1,3},{2,0},{3,1},{4,6},{5,7},{6,4},{7,5},{8,10},{9,11},{10,... | collective-permute-start | bytes 196616 | tf_op jit(solution)/shard_map/ppermute | solution.py:45
  44.7 7.8 %collective-permute-start.13 = (bf16[16,2048]{1,0:T(8,128)(2,1)S(1)}, bf16[16,2048]{1,0:T(8,128)(2,1)S(1)}, u32[]{:S(2)}, u32[]{:S(2)}) collective-permute-start(bf16[16,2048]{1,0:T(8,128)(2,1)S(1)} %get-tuple-element.134), channel_id=1, source_target_pairs={{0,6},{1,7},{2,4},{3,5},{4,2},{5,3},{6,0},{7,1},{8,14},{9,15},{10,... | collective-permute-start | bytes 196616 | tf_op jit(solution)/shard_map/ppermute | solution.py:45
  48.0 9.6 %collective-permute-start.12 = (bf16[16,2048]{1,0:T(8,128)(2,1)S(1)}, bf16[16,2048]{1,0:T(8,128)(2,1)S(1)}, u32[]{:S(2)}, u32[]{:S(2)}) collective-permute-start(bf16[16,2048]{1,0:T(8,128)(2,1)S(1)} %get-tuple-element.135), channel_id=1, source_target_pairs={{0,4},{1,5},{2,6},{3,7},{4,0},{5,1},{6,2},{7,3},{8,12},{9,13},{10,... | collective-permute-start | bytes 196616 | tf_op jit(solution)/shard_map/ppermute | solution.py:45
  48.0 11.8 %collective-permute-start.25 = (bf16[16,2048]{1,0:T(8,128)(2,1)S(1)}, bf16[16,2048]{1,0:T(8,128)(2,1)S(1)}, u32[]{:S(2)}, u32[]{:S(2)}) collective-permute-start(bf16[16,2048]{1,0:T(8,128)(2,1)S(1)} %get-tuple-element.130), channel_id=1, source_target_pairs={{0,2},{1,3},{2,0},{3,1},{4,6},{5,7},{6,4},{7,5},{8,10},{9,11},{10,... | collective-permute-start | bytes 196616 | tf_op jit(solution)/shard_map/ppermute | solution.py:45
  49.2 12.9 %collective-permute-start.27 = (bf16[16,2048]{1,0:T(8,128)(2,1)S(1)}, bf16[16,2048]{1,0:T(8,128)(2,1)S(1)}, u32[]{:S(2)}, u32[]{:S(2)}) collective-permute-start(bf16[16,2048]{1,0:T(8,128)(2,1)S(1)} %get-tuple-element.131), channel_id=1, source_target_pairs={{0,6},{1,7},{2,4},{3,5},{4,2},{5,3},{6,0},{7,1},{8,14},{9,15},{10,... | collective-permute-start | bytes 196616 | tf_op jit(solution)/shard_map/ppermute | solution.py:45
  52.5 9.6 %collective-permute-start.26 = (bf16[16,2048]{1,0:T(8,128)(2,1)S(1)}, bf16[16,2048]{1,0:T(8,128)(2,1)S(1)}, u32[]{:S(2)}, u32[]{:S(2)}) collective-permute-start(bf16[16,2048]{1,0:T(8,128)(2,1)S(1)} %get-tuple-element.132), channel_id=1, source_target_pairs={{0,4},{1,5},{2,6},{3,7},{4,0},{5,1},{6,2},{7,3},{8,12},{9,13},{10,... | collective-permute-start | bytes 196616 | tf_op jit(solution)/shard_map/ppermute | solution.py:45
  57.6 6.7 %collective-permute-start.19 = (bf16[16,2048]{1,0:T(8,128)(2,1)S(1)}, bf16[16,2048]{1,0:T(8,128)(2,1)S(1)}, u32[]{:S(2)}, u32[]{:S(2)}) collective-permute-start(bf16[16,2048]{1,0:T(8,128)(2,1)S(1)} %fusion.15.refs_0_), channel_id=1, source_target_pairs={{0,6},{1,7},{2,4},{3,5},{4,2},{5,3},{6,0},{7,1},{8,14},{9,15},{10,... | collective-permute-start | bytes 196616 | tf_op jit(solution)/shard_map/ppermute | solution.py:45
  59.8 6.2 %collective-permute-start.17 = (bf16[16,2048]{1,0:T(8,128)(2,1)S(1)}, bf16[16,2048]{1,0:T(8,128)(2,1)S(1)}, u32[]{:S(2)}, u32[]{:S(2)}) collective-permute-start(bf16[16,2048]{1,0:T(8,128)(2,1)S(1)} %fusion.15.refs_0_), channel_id=1, source_target_pairs={{0,4},{1,5},{2,6},{3,7},{4,0},{5,1},{6,2},{7,3},{8,12},{9,13},{10,... | collective-permute-start | bytes 196616 | tf_op jit(solution)/shard_map/ppermute | solution.py:45
  59.8 6.8 %collective-permute-start.15 = (bf16[16,2048]{1,0:T(8,128)(2,1)S(1)}, bf16[16,2048]{1,0:T(8,128)(2,1)S(1)}, u32[]{:S(2)}, u32[]{:S(2)}) collective-permute-start(bf16[16,2048]{1,0:T(8,128)(2,1)S(1)} %fusion.15.refs_0_), channel_id=1, source_target_pairs={{0,2},{1,3},{2,0},{3,1},{4,6},{5,7},{6,4},{7,5},{8,10},{9,11},{10,... | collective-permute-start | bytes 196616 | tf_op jit(solution)/shard_map/ppermute | solution.py:45
  62.1 4.5 %collective-permute-start.14 = (bf16[16,2048]{1,0:T(8,128)(2,1)S(1)}, bf16[16,2048]{1,0:T(8,128)(2,1)S(1)}, u32[]{:S(2)}, u32[]{:S(2)}) collective-permute-start(bf16[16,2048]{1,0:T(8,128)(2,1)S(1)} %fusion.15.refs_0_), channel_id=1, source_target_pairs={{0,1},{1,0},{2,3},{3,2},{4,5},{5,4},{6,7},{7,6},{8,9},{9,8},{10,11... | collective-permute-start | bytes 196616 | tf_op jit(solution)/shard_map/ppermute | solution.py:45
  62.2 6.9 %collective-permute-start.33 = (bf16[16,2048]{1,0:T(8,128)(2,1)S(1)}, bf16[16,2048]{1,0:T(8,128)(2,1)S(1)}, u32[]{:S(2)}, u32[]{:S(2)}) collective-permute-start(bf16[16,2048]{1,0:T(8,128)(2,1)S(1)} %fusion.11.refs_8_.refs_0_), channel_id=1, source_target_pairs={{0,6},{1,7},{2,4},{3,5},{4,2},{5,3},{6,0},{7,1},{8,14},{9,15},{10,... | collective-permute-start | bytes 196616 | tf_op jit(solution)/shard_map/ppermute | solution.py:45
  64.4 7.2 %collective-permute-start.31 = (bf16[16,2048]{1,0:T(8,128)(2,1)S(1)}, bf16[16,2048]{1,0:T(8,128)(2,1)S(1)}, u32[]{:S(2)}, u32[]{:S(2)}) collective-permute-start(bf16[16,2048]{1,0:T(8,128)(2,1)S(1)} %fusion.11.refs_8_.refs_0_), channel_id=1, source_target_pairs={{0,4},{1,5},{2,6},{3,7},{4,0},{5,1},{6,2},{7,3},{8,12},{9,13},{10,... | collective-permute-start | bytes 196616 | tf_op jit(solution)/shard_map/ppermute | solution.py:45
  66.0 5.7 %collective-permute-start.29 = (bf16[16,2048]{1,0:T(8,128)(2,1)S(1)}, bf16[16,2048]{1,0:T(8,128)(2,1)S(1)}, u32[]{:S(2)}, u32[]{:S(2)}) collective-permute-start(bf16[16,2048]{1,0:T(8,128)(2,1)S(1)} %fusion.11.refs_8_.refs_0_), channel_id=1, source_target_pairs={{0,2},{1,3},{2,0},{3,1},{4,6},{5,7},{6,4},{7,5},{8,10},{9,11},{10,... | collective-permute-start | bytes 196616 | tf_op jit(solution)/shard_map/ppermute | solution.py:45
  66.6 5.5 %collective-permute-start.20 = (bf16[16,2048]{1,0:T(8,128)(2,1)S(1)}, bf16[16,2048]{1,0:T(8,128)(2,1)S(1)}, u32[]{:S(2)}, u32[]{:S(2)}) collective-permute-start(bf16[16,2048]{1,0:T(8,128)(2,1)S(1)} %collective-permute-done.19.refs_6_), channel_id=1, source_target_pairs={{0,1},{1,0},{2,3},{3,2},{4,5},{5,4},{6,7},{7,6},{8,9},{9,8},{10,11... | collective-permute-start | bytes 196616 | tf_op jit(solution)/shard_map/ppermute | solution.py:45
  66.6 5.6 %collective-permute-start.18 = (bf16[16,2048]{1,0:T(8,128)(2,1)S(1)}, bf16[16,2048]{1,0:T(8,128)(2,1)S(1)}, u32[]{:S(2)}, u32[]{:S(2)}) collective-permute-start(bf16[16,2048]{1,0:T(8,128)(2,1)S(1)} %collective-permute-done.17.refs_4_), channel_id=1, source_target_pairs={{0,1},{1,0},{2,3},{3,2},{4,5},{5,4},{6,7},{7,6},{8,9},{9,8},{10,11... | collective-permute-start | bytes 196616 | tf_op jit(solution)/shard_map/ppermute | solution.py:45
  69.0 3.6 %collective-permute-start.16 = (bf16[16,2048]{1,0:T(8,128)(2,1)S(1)}, bf16[16,2048]{1,0:T(8,128)(2,1)S(1)}, u32[]{:S(2)}, u32[]{:S(2)}) collective-permute-start(bf16[16,2048]{1,0:T(8,128)(2,1)S(1)} %collective-permute-done.15.refs_2_), channel_id=1, source_target_pairs={{0,1},{1,0},{2,3},{3,2},{4,5},{5,4},{6,7},{7,6},{8,9},{9,8},{10,11... | collective-permute-start | bytes 196616 | tf_op jit(solution)/shard_map/ppermute | solution.py:45
  71.6 2.5 %collective-permute-start.28 = (bf16[16,2048]{1,0:T(8,128)(2,1)S(1)}, bf16[16,2048]{1,0:T(8,128)(2,1)S(1)}, u32[]{:S(2)}, u32[]{:S(2)}) collective-permute-start(bf16[16,2048]{1,0:T(8,128)(2,1)S(1)} %fusion.11.refs_8_.refs_0_), channel_id=1, source_target_pairs={{0,1},{1,0},{2,3},{3,2},{4,5},{5,4},{6,7},{7,6},{8,9},{9,8},{10,11... | collective-permute-start | bytes 196616 | tf_op jit(solution)/shard_map/ppermute | solution.py:45
  71.7 2.5 %collective-permute-start.34 = (bf16[16,2048]{1,0:T(8,128)(2,1)S(1)}, bf16[16,2048]{1,0:T(8,128)(2,1)S(1)}, u32[]{:S(2)}, u32[]{:S(2)}) collective-permute-start(bf16[16,2048]{1,0:T(8,128)(2,1)S(1)} %collective-permute-done.33.refs_14_.refs_6_), channel_id=1, source_target_pairs={{0,1},{1,0},{2,3},{3,2},{4,5},{5,4},{6,7},{7,6},{8,9},{9,8},{10,11... | collective-permute-start | bytes 196616 | tf_op jit(solution)/shard_map/ppermute | solution.py:45
  72.1 2.0 %collective-permute-start.32 = (bf16[16,2048]{1,0:T(8,128)(2,1)S(1)}, bf16[16,2048]{1,0:T(8,128)(2,1)S(1)}, u32[]{:S(2)}, u32[]{:S(2)}) collective-permute-start(bf16[16,2048]{1,0:T(8,128)(2,1)S(1)} %collective-permute-done.31.refs_12_.refs_4_), channel_id=1, source_target_pairs={{0,1},{1,0},{2,3},{3,2},{4,5},{5,4},{6,7},{7,6},{8,9},{9,8},{10,11... | collective-permute-start | bytes 196616 | tf_op jit(solution)/shard_map/ppermute | solution.py:45
  72.2 2.0 %collective-permute-start.30 = (bf16[16,2048]{1,0:T(8,128)(2,1)S(1)}, bf16[16,2048]{1,0:T(8,128)(2,1)S(1)}, u32[]{:S(2)}, u32[]{:S(2)}) collective-permute-start(bf16[16,2048]{1,0:T(8,128)(2,1)S(1)} %collective-permute-done.29.refs_10_.refs_2_), channel_id=1, source_target_pairs={{0,1},{1,0},{2,3},{3,2},{4,5},{5,4},{6,7},{7,6},{8,9},{9,8},{10,11... | collective-permute-start | bytes 196616 | tf_op jit(solution)/shard_map/ppermute | solution.py:45
  74.1 2.2 %copy-start = (bf16[1024,2048]{1,0:T(8,128)(2,1)S(1)}, bf16[1024,2048]{1,0:T(8,128)(2,1)}, u32[]{:S(2)}) copy-start(bf16[1024,2048]{1,0:T(8,128)(2,1)} %down.3) | copy-start | bytes 12582916
  77.2 1.6 %collective-permute-start.35 = (bf16[4,32,1024]{2,1,0:T(8,128)(2,1)S(1)}, bf16[4,32,1024]{2,1,0:T(8,128)(2,1)S(1)}, u32[]{:S(2)}, u32[]{:S(2)}) collective-permute-start(bf16[4,32,1024]{2,1,0:T(8,128)(2,1)S(1)} %get-tuple-element.114), channel_id=1, source_target_pairs={{0,1},{1,0},{2,3},{3,2},{4,5},{5,4},{6,7},{7,6},{8,9},{9,8},{10,11... | collective-permute-start | bytes 786440 | tf_op jit(solution)/shard_map/ppermute | solution.py:45
  78.1 4.3 %collective-permute-start.39 = (bf16[4,32,1024]{2,1,0:T(8,128)(2,1)S(1)}, bf16[4,32,1024]{2,1,0:T(8,128)(2,1)S(1)}, u32[]{:S(2)}, u32[]{:S(2)}) collective-permute-start(bf16[4,32,1024]{2,1,0:T(8,128)(2,1)S(1)} %get-tuple-element.117), channel_id=1, source_target_pairs={{0,1},{1,0},{2,3},{3,2},{4,5},{5,4},{6,7},{7,6},{8,9},{9,8},{10,11... | collective-permute-start | bytes 786440 | tf_op jit(solution)/shard_map/ppermute | solution.py:45
  78.9 6.5 %collective-permute-start.36 = (bf16[32,1024]{1,0:T(8,128)(2,1)S(1)}, bf16[32,1024]{1,0:T(8,128)(2,1)S(1)}, u32[]{:S(2)}, u32[]{:S(2)}) collective-permute-start(bf16[32,1024]{1,0:T(8,128)(2,1)S(1)} %get-tuple-element.124), channel_id=1, source_target_pairs={{0,2},{1,3},{2,0},{3,1},{4,6},{5,7},{6,4},{7,5},{8,10},{9,11},{10,... | collective-permute-start | bytes 196616 | tf_op jit(solution)/shard_map/ppermute | solution.py:45
  79.0 13.6 %collective-permute-start.38 = (bf16[32,1024]{1,0:T(8,128)(2,1)S(1)}, bf16[32,1024]{1,0:T(8,128)(2,1)S(1)}, u32[]{:S(2)}, u32[]{:S(2)}) collective-permute-start(bf16[32,1024]{1,0:T(8,128)(2,1)S(1)} %get-tuple-element.125), channel_id=1, source_target_pairs={{0,6},{1,7},{2,4},{3,5},{4,2},{5,3},{6,0},{7,1},{8,14},{9,15},{10,... | collective-permute-start | bytes 196616 | tf_op jit(solution)/shard_map/ppermute | solution.py:45
  80.9 11.7 %collective-permute-start.37 = (bf16[32,1024]{1,0:T(8,128)(2,1)S(1)}, bf16[32,1024]{1,0:T(8,128)(2,1)S(1)}, u32[]{:S(2)}, u32[]{:S(2)}) collective-permute-start(bf16[32,1024]{1,0:T(8,128)(2,1)S(1)} %get-tuple-element.126), channel_id=1, source_target_pairs={{0,4},{1,5},{2,6},{3,7},{4,0},{5,1},{6,2},{7,3},{8,12},{9,13},{10,... | collective-permute-start | bytes 196616 | tf_op jit(solution)/shard_map/ppermute | solution.py:45
  82.5 10.1 %collective-permute-start.40 = (bf16[32,1024]{1,0:T(8,128)(2,1)S(1)}, bf16[32,1024]{1,0:T(8,128)(2,1)S(1)}, u32[]{:S(2)}, u32[]{:S(2)}) collective-permute-start(bf16[32,1024]{1,0:T(8,128)(2,1)S(1)} %get-tuple-element.127), channel_id=1, source_target_pairs={{0,2},{1,3},{2,0},{3,1},{4,6},{5,7},{6,4},{7,5},{8,10},{9,11},{10,... | collective-permute-start | bytes 196616 | tf_op jit(solution)/shard_map/ppermute | solution.py:45
  83.5 9.1 %collective-permute-start.42 = (bf16[32,1024]{1,0:T(8,128)(2,1)S(1)}, bf16[32,1024]{1,0:T(8,128)(2,1)S(1)}, u32[]{:S(2)}, u32[]{:S(2)}) collective-permute-start(bf16[32,1024]{1,0:T(8,128)(2,1)S(1)} %get-tuple-element.128), channel_id=1, source_target_pairs={{0,6},{1,7},{2,4},{3,5},{4,2},{5,3},{6,0},{7,1},{8,14},{9,15},{10,... | collective-permute-start | bytes 196616 | tf_op jit(solution)/shard_map/ppermute | solution.py:45
  85.4 8.7 %collective-permute-start.41 = (bf16[32,1024]{1,0:T(8,128)(2,1)S(1)}, bf16[32,1024]{1,0:T(8,128)(2,1)S(1)}, u32[]{:S(2)}, u32[]{:S(2)}) collective-permute-start(bf16[32,1024]{1,0:T(8,128)(2,1)S(1)} %get-tuple-element.129), channel_id=1, source_target_pairs={{0,4},{1,5},{2,6},{3,7},{4,0},{5,1},{6,2},{7,3},{8,12},{9,13},{10,... | collective-permute-start | bytes 196616 | tf_op jit(solution)/shard_map/ppermute | solution.py:45

commit v4 on v3

--- a/solution.py
+++ b/solution.py
@@ -15,12 +15,16 @@
 BF = jnp.bfloat16
 F32 = jnp.float32
 LANES = 128
-Q_TILE = 32
+Q_TILE = 64
 P_TILE = 512
 
 
 def round_up(count, step):
     return (count + step - 1) // step * step
+
+
+def row_tiles(count, rows):
+    return [slice(at, at + rows) for at in range(0, count, rows)]
 
 
 def dot(left, right):
@@ -45,24 +49,27 @@
     return lax.ppermute(values, axis_name, [(i, i ^ offset) for i in range(count)])
 
 
-def gather_tensor(block, beside=None):
-    count = lax.axis_size("tensor")
-    pieces = [None] * count
-    pieces[0] = block
-    for k in range(2, count, 2):
-        pieces[k] = swap(block, "tensor", k)
-    if beside is not None:
-        pieces[::2], done = lax.optimization_barrier((pieces[::2], beside()))
-    for k in range(0, count, 2):
-        pieces[k + 1] = swap(pieces[k], "tensor", 1)
-    return pieces if beside is None else (pieces, done)
-
-
-def reduce_tensor(keep, send):
-    count = lax.axis_size("tensor")
+def gather_chips(block):
+    chips = lax.axis_size("tensor") // 2
+    return [block] + [swap(block, "tensor", 2 * k) for k in range(1, chips)]
+
+
+def gather_cores(blocks):
+    return [piece for block in blocks for piece in (block, swap(block, "tensor", 1))]
+
+
+def gather_tensor(block, beside):
+    blocks, done = lax.optimization_barrier((gather_chips(block), beside()))
+    return gather_cores(blocks), done
+
+
+def reduce_chips(keep, send, first):
     came = swap(send, "tensor", 1)
-    joined = [(keep[k].astype(F32) + came[k].astype(F32)).astype(BF) for k in range(count // 2)]
-    return [joined[0]] + [swap(joined[k], "tensor", 2 * k) for k in range(1, count // 2)]
+    sums = []
+    for i in range(keep.shape[0]):
+        joined = (keep[i].astype(F32) + came[i].astype(F32)).astype(BF)
+        sums.append(swap(joined, "tensor", 2 * (first + i)) if first + i else joined)
+    return sums
 
 
 def normalize(values, gain):
@@ -93,11 +100,11 @@
 
 
 def plan_kernel(sizes, lengths, owners, starts, freqs, *outs):
-    groups, count, home_count, slot_rows, sorted_count, cache_rows, rows = sizes
+    groups, count, home_count, slot_rows, cache_rows, rows = sizes
     (
         slots_ref,
         middle_ref,
-        own_middle,
+        own_order,
         far_pick,
         cos_ref,
         sin_ref,
@@ -105,9 +112,8 @@
         home_span,
         home_write,
         home_bounds,
-        far_order,
-        sort_start,
-        sort_span,
+        far_start,
+        far_span,
         far_write,
         far_bounds,
     ) = outs
@@ -121,11 +127,10 @@
         before = (owner_column == owner) & (start_column < start)
         return jnp.sum(jnp.where(before, 1.0, 0.0), axis=0, keepdims=True)
 
-    def put_ranges(start_ref, span_ref, bounds_ref, start, span):
+    def put_ranges(start_ref, span_ref, bounds_ref, start, span, tile_rows):
         start_ref[...] = start.astype(jnp.int32)
         span_ref[...] = span.astype(jnp.int32)
-        for tile in range(start.shape[0] // Q_TILE):
-            cut = slice(tile * Q_TILE, (tile + 1) * Q_TILE)
+        for tile, cut in enumerate(row_tiles(start.shape[0], tile_rows)):
             live = span[cut] > 0.0
             low = jnp.min(start[cut]).astype(jnp.int32) // P_TILE
             last = jnp.max(jnp.where(live, start[cut] + span[cut], 0.0)).astype(jnp.int32)
@@ -151,11 +156,9 @@
         (((place - count // 2) // part) ^ me) * part + place % part + count // 2,
     )
     middle_ref[...] = middle
-    lane = lax.broadcasted_iota(jnp.int32, (rows, count), 1)
-    wanted = lax.broadcasted_iota(jnp.int32, (rows, count), 0) + me * rows
-    own_middle[...] = jnp.sum(
-        jnp.where(lane == wanted, middle.astype(F32), 0.0), axis=1, keepdims=True
-    ).astype(jnp.int32)
+    request = lax.broadcasted_iota(jnp.int32, (1, count), 1)
+    relative = (((request // rows) ^ me) * rows + request % rows).astype(F32)
+    own_order[...] = row_of(picked(count, relative, [middle.astype(F32)])[0]).astype(jnp.int32)
     far_count = far_pick.shape[1]
     is_far = jnp.where(hop == 0, 0.0, 1.0)
     shifted = jnp.where(hop == 0, -1.0, slot - home_count)
@@ -167,7 +170,7 @@
     start, span = picked(home_count, slot, [my_start, my_length])
     live = span > 0.0
     start = jnp.where(live, start, float(cache_rows))
-    put_ranges(home_start, home_span, home_bounds, start, span)
+    put_ranges(home_start, home_span, home_bounds, start, span, Q_TILE)
     home_write[...] = row_of(jnp.where(live, start + span, -1.0)).astype(jnp.int32)
 
     far = []
@@ -183,13 +186,7 @@
     live = span > 0.0
     start = jnp.where(live, start, float(cache_rows))
     far_write[...] = row_of(jnp.where(live, start + span, -1.0)).astype(jnp.int32)
-    start_row, span_row = row_of(start), row_of(span)
-    order = jnp.sum(jnp.where(start < start_row, 1.0, 0.0), axis=0, keepdims=True)
-    order = jnp.where(span_row > 0.0, order, -1.0)
-    far_order[...] = order.astype(jnp.int32)
-    start, span = picked(sorted_count, order, [start_row, span_row])
-    start = jnp.where(span > 0.0, start, float(cache_rows))
-    put_ranges(sort_start, sort_span, far_bounds, start, span)
+    put_ranges(far_start, far_span, far_bounds, start, span, slot_rows)
 
 
 def qkv_kernel(piece_count, home_count, slot_rows, hop_count, *refs):
@@ -230,10 +227,9 @@
     token_far[...] = dot(one_hot(part, middle[...] - count // 2), raw[...]).astype(BF)
 
 
-def attend_all(bounds, packed, starts, spans, kv_ref, result, heads, outs):
+def attend_all(bounds, packed, starts, spans, kv_ref, result, heads, outs, tile_rows):
     width = heads * HD
-    rows = Q_TILE
-    tiles = packed.shape[0] // rows
+    tiles = row_tiles(packed.shape[0], tile_rows)
     lane_head = lax.broadcasted_iota(jnp.int32, (packed.shape[0], width), 1) // HD
     masks = [lane_head == h for h in range(heads)]
     stack = lambda parts: jnp.concatenate(parts, axis=0)
@@ -243,13 +239,13 @@
     single = [jnp.where(m, query, jnp.zeros_like(query)) for m in masks]
     value = packed[:, 2 * width :].astype(F32)
     tops, totals = [], []
-    for tile in range(tiles):
-        cut = slice(tile * rows, (tile + 1) * rows)
+    for tile, cut in enumerate(tiles):
+        rows = cut.stop - cut.start
         own = stack([part[cut] for part in owns])
         stacked = stack([part[cut] for part in single])
         start, span = starts[cut, :], spans[cut, :]
 
-        def advance(step, carry):
+        def advance(step, carry, rows=rows, start=start, span=span, stacked=stacked):
             top, total, out = carry
             first = pl.multiple_of(step * P_TILE, P_TILE)
             keys = kv_ref[0, pl.ds(first, P_TILE), :]
@@ -268,7 +264,7 @@
         top, total, out = lax.fori_loop(bounds[0, tile], bounds[1, tile], advance, first_carry)
         tops.append(top)
         totals.append(total)
-        outs[tile * heads * rows : (tile + 1) * heads * rows, :] = out
+        outs[cut.start * heads : cut.stop * heads, :] = out
     total = stack(totals)
     log_sum = stack(tops) + jnp.log(total)
     scaled = outs[...] * (1.0 / total)
@@ -277,16 +273,18 @@
     for part in range(3):
         pieces.append(rest.astype(BF).astype(F32))
         rest = rest - pieces[-1]
-    lane = lax.broadcasted_iota(jnp.int32, (rows, LANES), 1)
-    for tile in range(tiles):
+    for tile in tiles:
+        rows = tile.stop - tile.start
+        lane = lax.broadcasted_iota(jnp.int32, (rows, LANES), 1)
         attended = jnp.zeros((rows, width), F32)
         extra = jnp.zeros((rows, LANES), F32)
         for h in range(heads):
-            cut = slice((tile * heads + h) * rows, (tile * heads + h + 1) * rows)
+            first = tile.start * heads + h * rows
+            cut = slice(first, first + rows)
             attended = jnp.where(masks[h][:rows], scaled[cut], attended)
             for part in range(3):
                 extra = jnp.where(lane == part * heads + h, pieces[part][cut], extra)
-        result[tile * rows : (tile + 1) * rows, :] = jnp.concatenate(
+        result[tile, :] = jnp.concatenate(
             [attended.astype(BF), extra.astype(BF)], axis=1
         )
 
@@ -304,29 +302,18 @@
 def home_kernel(
     heads, bounds, packed, starts, spans, kv_ref, weights, result, keep_ref, send_ref, partial, outs
 ):
-    attend_all(bounds, packed[...], starts, spans, kv_ref, result, heads, outs)
+    attend_all(bounds, packed[...], starts, spans, kv_ref, result, heads, outs, Q_TILE)
     send_middle(result[:, : heads * HD], weights, keep_ref, send_ref, partial)
 
 
-def far_kernel(heads, hop_count, sorted_count, bounds, *refs):
+def far_kernel(heads, hop_count, bounds, *refs):
     arrived = jnp.concatenate([ref[...] for ref in refs[:hop_count]], axis=0)
-    order, starts, spans, kv_ref, _ = refs[hop_count : hop_count + 5]
-    outs = refs[hop_count + 5 : 2 * hop_count + 5]
-    scratch, state = refs[-2:]
-    mover = one_hot(sorted_count, order[...])
-    in_order = dot(mover, arrived).astype(BF)
-    attend_all(bounds, in_order, starts, spans, kv_ref, scratch, heads, state)
-    back = dot_tn(mover, scratch[...]).astype(BF)
-    slot_rows = arrived.shape[0] // hop_count
+    starts, spans, kv_ref, _ = refs[hop_count : hop_count + 4]
+    *outs, result, state = refs[hop_count + 4 :]
+    rows = arrived.shape[0] // hop_count
+    attend_all(bounds, arrived, starts, spans, kv_ref, result, heads, state, rows)
     for k in range(hop_count):
-        outs[k][...] = back[k * slot_rows : (k + 1) * slot_rows]
-
-
-def put_chunks(keep_ref, send_ref, partial, rows):
-    me = lax.axis_index("tensor")
-    for k in range(partial.shape[0] // rows):
-        ref = keep_ref if k % 2 == 0 else send_ref
-        ref[k // 2] = partial[pl.ds(pl.multiple_of((me ^ k) * rows, rows), rows), :]
+        outs[k][...] = result[k * rows : (k + 1) * rows, :]
 
 
 def far_out_kernel(heads, hop_count, slots, far_pick, home, *refs):
@@ -353,27 +340,30 @@
     inner_ref[...] = (gate / (1.0 + jnp.exp(-gate)) * upward).astype(BF)
 
 
-def down_first_kernel(rows, home, far, middle, down, inner_ref, keep_ref, send_ref, partial):
-    half = keep_ref.shape[2]
+def send_rows(partial, rows, keep_ref, send_ref):
+    for k in range(partial.shape[0] // rows):
+        ref = keep_ref if k % 2 == 0 else send_ref
+        ref[k // 2] = partial[k * rows : (k + 1) * rows]
+
+
+def down_first_kernel(rows, home, far, order, down, rest_ref, keep_ref, send_ref):
     both = jnp.concatenate([home[...], far[...]], axis=0)
-    inner = dot_tn(one_hot(both.shape[0], middle[...]), both).astype(BF)
-    inner_ref[...] = inner
-    partial[...] = dot(inner, down[:, :half]).astype(BF)
-    put_chunks(keep_ref, send_ref, partial, rows)
-
-
-def down_second_kernel(rows, inner, down, keep_ref, send_ref, partial):
-    half = keep_ref.shape[2]
-    partial[...] = dot(inner[...], down[:, half:]).astype(BF)
-    put_chunks(keep_ref, send_ref, partial, rows)
-
-
-def own_rows_kernel(own_middle, *refs):
+    inner = dot_tn(one_hot(both.shape[0], order[...]), both).astype(BF)
+    half = rest_ref.shape[0]
+    rest_ref[...] = inner[:half]
+    send_rows(dot(inner[half:], down[...]).astype(BF), rows, keep_ref, send_ref)
+
+
+def down_second_kernel(rows, inner, down, keep_ref, send_ref):
+    send_rows(dot(inner[...], down[...]).astype(BF), rows, keep_ref, send_ref)
+
+
+def own_rows_kernel(order, *refs):
     pieces = refs[:-1]
     values = jnp.concatenate([piece[...] for piece in pieces], axis=0)
-    shape = (own_middle.shape[0], values.shape[0])
-    selector = jnp.where(lax.broadcasted_iota(jnp.int32, shape, 1) == own_middle[...], 1.0, 0.0)
-    refs[-1][...] = dot(selector.astype(BF), values).astype(BF)
+    rows = refs[-1].shape[0]
+    chosen = dot_tn(one_hot(values.shape[0], order[...]), values)
+    refs[-1][...] = chosen[:rows].astype(BF)
 
 
 def update_kernel(hop_count, width, home_rows, far_rows, home, *refs):
@@ -421,7 +411,6 @@
     capacity = (request_count // 2 + groups - 2) // (groups - 1)
     slot_rows = round_up(capacity, 16)
     far_count = hops * slot_rows
-    sorted_count = round_up(min(hops * capacity, far_count), Q_TILE)
     shape = jax.ShapeDtypeStruct
     smem = pl.BlockSpec(memory_space=pltpu.SMEM)
     anywhere = pl.BlockSpec(memory_space=pl.ANY)
@@ -439,12 +428,12 @@
     plan = lambda: pl.pallas_call(
         functools.partial(
             plan_kernel,
-            (groups, request_count, home_count, slot_rows, sorted_count, cache_rows, rows),
+            (groups, request_count, home_count, slot_rows, cache_rows, rows),
         ),
         out_shape=[
             ints(1, request_count),
             ints(1, request_count),
-            ints(rows, 1),
+            ints(1, request_count),
             ints(1, far_count),
             shape((request_count, LANES), F32),
             shape((request_count, LANES), F32),
@@ -452,14 +441,13 @@
             ints(home_count, 1),
             ints(1, home_count),
             ints(2, home_count // Q_TILE),
+            ints(far_count, 1),
+            ints(far_count, 1),
             ints(1, far_count),
-            ints(sorted_count, 1),
-            ints(sorted_count, 1),
-            ints(1, far_count),
-            ints(2, sorted_count // Q_TILE),
+            ints(2, hops),
         ],
         in_specs=vmem(4),
-        out_specs=vmem(9) + [smem] + vmem(4) + [smem],
+        out_specs=vmem(9) + [smem] + vmem(3) + [smem],
         compiler_params=params(16),
         cost_estimate=cost(4 * 10**9, 10**6, 10**5),
         name="plan",
@@ -468,7 +456,7 @@
     (
         slots,
         middle,
-        own_middle,
+        own_order,
         far_pick,
         cosine,
         sine,
@@ -476,9 +464,8 @@
         home_span,
         home_write,
         home_bounds,
-        far_order,
-        sort_start,
-        sort_span,
+        far_start,
+        far_span,
         far_write,
         far_bounds,
     ) = planned
@@ -494,7 +481,7 @@
         in_specs=vmem(tensor_count + 6),
         out_specs=vmem(3 + hops),
         scratch_shapes=[pltpu.VMEM((request_count, model_width), BF)] * 2,
-        compiler_params=params(24),
+        compiler_params=params(16),
         name="qkv",
     )(*pieces, attn_gain[None, :], project_in, cosine, sine, slots, middle)
     home_packed = packed_outs[0]
@@ -515,20 +502,20 @@
         name="home_attention",
     )(home_bounds, home_packed, home_start, home_span, kv_cache, project_out)
     (keep, send), arrived = lax.optimization_barrier(((keep, send), arrived))
-    home_sums = reduce_tensor(keep, send)
+    home_sums = reduce_chips(keep, send, 0)
     far_outs = pl.pallas_call(
-        functools.partial(far_kernel, heads, hops, sorted_count),
+        functools.partial(far_kernel, heads, hops),
         out_shape=[shape((slot_rows, out_width), BF)] * hops,
-        in_specs=[smem] + vmem(hops + 4) + [anywhere],
+        in_specs=[smem] + vmem(hops + 3) + [anywhere],
         out_specs=vmem(hops),
         scratch_shapes=[
-            pltpu.VMEM((sorted_count, out_width), BF),
-            pltpu.VMEM((sorted_count * heads, width), F32),
+            pltpu.VMEM((far_count, out_width), BF),
+            pltpu.VMEM((far_count * heads, width), F32),
         ],
         compiler_params=params(16),
         cost_estimate=cost(2 * 10**9, 4 * 2**20, 10**6),
         name="far_attention",
-    )(far_bounds, *arrived, far_order, sort_start, sort_span, kv_cache, home_att)
+    )(far_bounds, *arrived, far_start, far_span, kv_cache, home_att)
     backs = [swap(far_outs[k - 1], "dp", k) for k in range(1, groups)]
 
     block = 512
@@ -556,12 +543,12 @@
         out_shape=shape((middle_count, hidden), BF),
         in_specs=vmem(tensor_count + 2),
         out_specs=vmem(1)[0],
-        compiler_params=params(24),
+        compiler_params=params(16),
         cost_estimate=cost(2 * 10**9, 8 * 2**20),
         name=name,
     )(*pieces, mlp_gain[None, :], gate_up)
-    home_pieces = gather_tensor(add_up(token_home, home_sums))
-    home_inner = gate(home_pieces, "gate_up_home")
+    backs, home_sums = lax.optimization_barrier((backs, home_sums))
+    home_far_chips = gather_chips(add_up(token_home, home_sums))
 
     log_sum, keep, send = pl.pallas_call(
         functools.partial(far_out_kernel, heads, hops),
@@ -573,32 +560,35 @@
         name="project_out_far",
     )(slots, far_pick, home_att, *backs, project_out)
     log_sum_exp = log_sum[:, :heads]
-    far_pieces = gather_tensor(add_up(token_far, reduce_tensor(keep, send)))
+    far_sums, home_far_chips = lax.optimization_barrier(
+        (reduce_chips(keep, send, 0), home_far_chips)
+    )
+    home_pieces = gather_cores(home_far_chips)
+    far_pieces, home_inner = gather_tensor(
+        add_up(token_far, far_sums), lambda: gate(home_pieces, "gate_up_home")
+    )
     far_inner = gate(far_pieces, "gate_up_far")
 
-    half = model_width // 2
-    halves = [shape((half_count, rows, half), BF)] * 2
-    row_scratch = [pltpu.VMEM((request_count, half), BF)]
-    inner, keep, send = pl.pallas_call(
+    near = half_count // 2
+    quarters = [shape((near, rows, model_width), BF)] * 2
+    rest, keep, send = pl.pallas_call(
         functools.partial(down_first_kernel, rows),
-        out_shape=[shape((request_count, hidden), BF)] + halves,
+        out_shape=[shape((middle_count, hidden), BF)] + quarters,
         in_specs=vmem(4),
         out_specs=vmem(3),
-        scratch_shapes=row_scratch,
         compiler_params=params(16),
         name="down_first",
-    )(home_inner, far_inner, middle, project_down)
-    sums_first = reduce_tensor(keep, send)
+    )(home_inner, far_inner, own_order, project_down)
+    down_sums = reduce_chips(keep, send, near)
     keep, send = pl.pallas_call(
         functools.partial(down_second_kernel, rows),
-        out_shape=halves,
+        out_shape=quarters,
         in_specs=vmem(2),
         out_specs=vmem(2),
-        scratch_shapes=row_scratch,
         compiler_params=params(16),
         name="down_second",
-    )(inner, project_down)
-    sums_second = reduce_tensor(keep, send)
+    )(rest, project_down)
+    down_sums += reduce_chips(keep, send, 0)
     resid = pl.pallas_call(
         own_rows_kernel,
         out_shape=shape(tokens.shape, BF),
@@ -606,10 +596,8 @@
         out_specs=vmem(1)[0],
         compiler_params=params(16),
         name="own_rows",
-    )(own_middle, *home_pieces, *far_pieces)
-    hidden_states = jnp.concatenate(
-        [add_up(resid[:, :half], sums_first), add_up(resid[:, half:], sums_second)], axis=1
-    )
+    )(own_order, *home_pieces, *far_pieces)
+    hidden_states = add_up(resid, down_sums)
     return (hidden_states, log_sum_exp, kv_updated)
 
 

time: 94.6 us -> 91.8 us (0.970); the launches traced: 94.9 us -> 90.2 us
  starting transfers between devices: 43.5 us -> 38.8 us
  waiting for transfers between devices: 20.7 us -> 22.4 us
  Pallas kernels: 25.2 us -> 24.2 us
    ppermute x43 -> x40, starting transfers between devices: 43.5 us -> 38.8 us  [swap(): lax.ppermute(values, axis_name, [(i, i ^ offset) for i in range(count)])]
    ppermute x43 -> x40, waiting for transfers between devices: 20.7 us -> 22.4 us  [swap(): lax.ppermute(values, axis_name, [(i, i ^ offset) for i in range(count)])]
    pallas_call x2, Pallas kernels: 6.07 us -> 5.11 us  [the longest x1 4.38 us: on_device(): pl.pallas_call(functools.partial(far_kernel, heads, hops), out_shape=[sha...]
  transfers between devices with their start and end apart: 43 -> 40, of which waited for: 16 -> 20; matrix products, arithmetic and copies ran while one was open for 1% -> 1% of each run, Pallas kernels for 22% -> 21%
where the time goes in v4:
time: 91.8 us; the launch traced here: 90.2 us
  starting transfers between devices  38.8 us (42%)
  Pallas kernels  24.2 us (26%)
  waiting for transfers between devices  22.4 us (24%)
  local copies, waits for them, and re-layouts  2.78 us (3%)
  other arithmetic  1.1 us (1%)
    ppermute x40, starting transfers between devices, swap(): lax.ppermute(values, axis_name, [(i, i ^ offset) for i in range(count)])  38.8 us
    ppermute x40, waiting for transfers between devices, swap(): lax.ppermute(values, axis_name, [(i, i ^ offset) for i in range(count)])  22.4 us
    pallas_call x1, Pallas kernels, on_device(): pl.pallas_call(functools.partial(update_kernel, hops, width), grid=(cache...  5.56 us
    pallas_call x1, Pallas kernels, on_device(): pl.pallas_call(functools.partial(far_kernel, heads, hops), out_shape=[sha...  4.38 us
    pallas_call x1, Pallas kernels, on_device(): pl.pallas_call(functools.partial(home_kernel, heads), out_shape=[shape((h...  4.35 us
    pallas_call x2, Pallas kernels, on_device(): pl.pallas_call(functools.partial(gate_kernel, tensor_count), out_shape=sh...  2.9 us
    unnamed x25, local copies, waits for them, and re-layouts  2.77 us
    pallas_call x1, Pallas kernels, on_device(): pl.pallas_call(functools.partial(qkv_kernel, tensor_count, home_count, sl...  2.31 us
  transfers between devices with their start and end apart: 40, of which 20 were waited for; matrix products, arithmetic and copies ran while one was open for 1% of the time, Pallas kernels for 21%

profile of v4, /device:TPU:0, one launch (start us, length us, event | category | flops | bytes accessed | tf_op | source)
XLA Modules:
  0.0 90.2 jit_solution(684975807725051045)
XLA Ops:
  0.6 4.1 %collective-permute-start.1 = (bf16[32,2048]{1,0:T(8,128)(2,1)}, bf16[32,2048]{1,0:T(8,128)(2,1)S(1)}, u32[]{:S(2)}, u32[]{:S(2)}) collective-permute-start(bf16[32,2048]{1,0:T(8,128)(2,1)} %refs_0_), channel_id=1, source_target_pairs={{0,4},{1,5},{2,6},{3,7},{4,0},{5,1},{6,2},{7,3},{8,12},{9,13},{10,... | collective-permute-start | bytes 393224 | tf_op jit(solution)/shard_map/ppermute | solution.py:49
  4.7 1.6 %collective-permute-start = (bf16[32,2048]{1,0:T(8,128)(2,1)}, bf16[32,2048]{1,0:T(8,128)(2,1)S(1)}, u32[]{:S(2)}, u32[]{:S(2)}) collective-permute-start(bf16[32,2048]{1,0:T(8,128)(2,1)} %refs_0_), channel_id=1, source_target_pairs={{0,2},{1,3},{2,0},{3,1},{4,6},{5,7},{6,4},{7,5},{8,10},{9,11},{10,... | collective-permute-start | bytes 393224 | tf_op jit(solution)/shard_map/ppermute | solution.py:49
  6.3 0.7 copy-done.5
  7.0 0.7 copy-done.6
  7.7 0.7 copy-done.7
  8.4 2.1 %plan.1 = (s32[1,256]{1,0:T(1,128)S(1)}, s32[1,256]{1,0:T(1,128)S(1)}, s32[1,256]{1,0:T(1,128)S(1)}, s32[1,144]{1,0:T(1,128)S(1)}, f32[256,128]{1,0:T(8,128)S(1)...) custom-call(s32[1,1024]{1,0:T(1,128)S(1)} %bitcast.34, ...), custom_call_target="tpu_custom_call" | custom-call | flops 4000000000 | bytes 1000000 | tf_op jit(solution)/shard_map/plan/pallas_call | solution.py:428
  10.5 2.4 %collective-permute-done.1.refs_4_ = bf16[32,2048]{1,0:T(8,128)(2,1)S(1)} collective-permute-done((bf16[32,2048]{1,0:T(8,128)(2,1)}, bf16[32,2048]{1,0:T(8,128)(2,1)S(1)}, u32[]{:S(2)}, u32[]{:S(2)}) %collective-permute-start.1) | collective-permute-done | bytes 131104 | tf_op jit(solution)/shard_map/ppermute | solution.py:49
  12.9 2.4 %collective-permute-done.2.refs_6_ = bf16[32,2048]{1,0:T(8,128)(2,1)S(1)} collective-permute-done((bf16[32,2048]{1,0:T(8,128)(2,1)}, bf16[32,2048]{1,0:T(8,128)(2,1)S(1)}, u32[]{:S(2)}, u32[]{:S(2)}) %collective-permute-start.2) | collective-permute-done | bytes 131104 | tf_op jit(solution)/shard_map/ppermute | solution.py:49
  15.3 0.5 collective-permute-start.4
  15.8 0.5 collective-permute-start.6
  16.3 0.3 collective-permute-done.3.refs_1_
  16.6 0.2 collective-permute-done.4.refs_3_
  16.8 0.3 collective-permute-done.5.refs_5_
  17.1 0.2 collective-permute-done.6.refs_7_
  17.3 2.3 %qkv.1 = (bf16[128,768]{1,0:T(8,128)(2,1)S(1)}, bf16[48,768]{1,0:T(8,128)(2,1)S(1)}, bf16[48,768]{1,0:T(8,128)(2,1)S(1)}, bf16[48,768]{1,0:T(8,128)(2,1)S(1)}, b...) custom-call(bf16[32,2048]{1,0:T(8,128)(2,1)S(1)} %copy-done.4, ...), custom_call_target="tpu_custom_call" | custom-call | tf_op jit(solution)/shard_map/qkv/pallas_call | solution.py:476
  19.6 1.5 %collective-permute-start.7 = (bf16[48,768]{1,0:T(8,128)(2,1)S(1)}, bf16[48,768]{1,0:T(8,128)(2,1)S(1)}, u32[]{:S(2)}, u32[]{:S(2)}) collective-permute-start(bf16[48,768]{1,0:T(8,128)(2,1)S(1)} %get-tuple-element.112), channel_id=1, source_target_pairs={{0,8},{8,0},{16,24},{24,16},{1,9},{9,1},{17,25},{25,17},{2,10},{10... | collective-permute-start | bytes 221192 | tf_op jit(solution)/shard_map/ppermute | solution.py:49
  21.1 1.5 %collective-permute-start.8 = (bf16[48,768]{1,0:T(8,128)(2,1)S(1)}, bf16[48,768]{1,0:T(8,128)(2,1)S(1)}, u32[]{:S(2)}, u32[]{:S(2)}) collective-permute-start(bf16[48,768]{1,0:T(8,128)(2,1)S(1)} %get-tuple-element.113), channel_id=1, source_target_pairs={{0,16},{8,24},{16,0},{24,8},{1,17},{9,25},{17,1},{25,9},{2,18},{10... | collective-permute-start | bytes 221192 | tf_op jit(solution)/shard_map/ppermute | solution.py:49
  22.7 0.5 collective-permute-start.9
  23.1 4.3 %home_attention.1 = (bf16[128,384]{1,0:T(8,128)(2,1)S(1)}, bf16[4,16,2048]{2,1,0:T(8,128)(2,1)S(1)}, bf16[4,16,2048]{2,1,0:T(8,128)(2,1)S(1)}) custom-call(s32[2,2]{1,0:T(2,128)S(1)} %get-tuple-element.97.bounds, bf16[128,768]{1,0:T(8,128)(2,1)S(1)} %get-tuple-element.105.packed.home, s32[128,1]{1,0:T(8,128)S(1)} %get-tuple-element.106.starts, ...), custom_call_target="tpu_custom_call" | custom-call | flops 2000000000 | bytes 4194304 | tf_op jit(solution)/shard_map/home_attention/pallas_call | solution.py:494
  27.5 0.4 collective-permute-done.9.refs_2_
  27.9 4.4 %far_attention.1 = (bf16[48,384]{1,0:T(8,128)(2,1)S(1)}, bf16[48,384]{1,0:T(8,128)(2,1)S(1)}, bf16[48,384]{1,0:T(8,128)(2,1)S(1)}) custom-call(s32[2,3]{1,0:T(2,128)S(1)} %get-tuple-element.109.bounds, bf16[48,768]{1,0:T(8,128)(2,1)S(1)} %collective-permute-done.7.refs_0_, bf16[48,768]{1,0:T(8,128)(2,1)S(1)} %collective-permute-done.8.refs_1_, ...), custom_call_target="tpu_custom_call" | custom-call | flops 2000000000 | bytes 4194304 | tf_op jit(solution)/shard_map/far_attention/pallas_call | solution.py:506
  32.5 2.5 %collective-permute-start.16 = (bf16[16,2048]{1,0:T(8,128)(2,1)S(1)}, bf16[16,2048]{1,0:T(8,128)(2,1)S(1)}, u32[]{:S(2)}, u32[]{:S(2)}) collective-permute-start(bf16[16,2048]{1,0:T(8,128)(2,1)S(1)} %get-tuple-element.166), channel_id=1, source_target_pairs={{0,6},{1,7},{2,4},{3,5},{4,2},{5,3},{6,0},{7,1},{8,14},{9,15},{10,... | collective-permute-start | bytes 196616 | tf_op jit(solution)/shard_map/ppermute | solution.py:49
  35.0 1.9 %collective-permute-start.15 = (bf16[16,2048]{1,0:T(8,128)(2,1)S(1)}, bf16[16,2048]{1,0:T(8,128)(2,1)S(1)}, u32[]{:S(2)}, u32[]{:S(2)}) collective-permute-start(bf16[16,2048]{1,0:T(8,128)(2,1)S(1)} %get-tuple-element.167), channel_id=1, source_target_pairs={{0,4},{1,5},{2,6},{3,7},{4,0},{5,1},{6,2},{7,3},{8,12},{9,13},{10,... | collective-permute-start | bytes 196616 | tf_op jit(solution)/shard_map/ppermute | solution.py:49
  36.9 0.5 collective-permute-start.14
  37.3 1.3 %collective-permute-start.11 = (bf16[48,384]{1,0:T(8,128)(2,1)S(1)}, bf16[48,384]{1,0:T(8,128)(2,1)S(1)}, u32[]{:S(2)}, u32[]{:S(2)}) collective-permute-start(bf16[48,384]{1,0:T(8,128)(2,1)S(1)} %get-tuple-element.121), channel_id=1, source_target_pairs={{0,16},{8,24},{16,0},{24,8},{1,17},{9,25},{17,1},{25,9},{2,18},{10... | collective-permute-start | bytes 110600 | tf_op jit(solution)/shard_map/ppermute | solution.py:49
  38.7 2.1 %collective-permute-start.12 = (bf16[48,384]{1,0:T(8,128)(2,1)S(1)}, bf16[48,384]{1,0:T(8,128)(2,1)S(1)}, u32[]{:S(2)}, u32[]{:S(2)}) collective-permute-start(bf16[48,384]{1,0:T(8,128)(2,1)S(1)} %get-tuple-element.122), channel_id=1, source_target_pairs={{0,24},{8,16},{16,8},{24,0},{1,25},{9,17},{17,9},{25,1},{2,26},{10... | collective-permute-start | bytes 110600 | tf_op jit(solution)/shard_map/ppermute | solution.py:49
  40.8 0.5 collective-permute-done.11.refs_1_
  41.3 2.2 %collective-permute-done.12.refs_2_ = bf16[48,384]{1,0:T(8,128)(2,1)S(1)} collective-permute-done((bf16[48,384]{1,0:T(8,128)(2,1)S(1)}, bf16[48,384]{1,0:T(8,128)(2,1)S(1)}, u32[]{:S(2)}, u32[]{:S(2)}) %collective-permute-start.12) | collective-permute-done | bytes 36896 | tf_op jit(solution)/shard_map/ppermute | solution.py:49
  43.6 0.6 project_out_far.1
  44.3 2.4 %collective-permute-start.23 = (bf16[16,2048]{1,0:T(8,128)(2,1)S(1)}, bf16[16,2048]{1,0:T(8,128)(2,1)S(1)}, u32[]{:S(2)}, u32[]{:S(2)}) collective-permute-start(bf16[16,2048]{1,0:T(8,128)(2,1)S(1)} %add_convert_fusion.5.refs_0_), channel_id=1, source_target_pairs={{0,6},{1,7},{2,4},{3,5},{4,2},{5,3},{6,0},{7,1},{8,14},{9,15},{10,... | collective-permute-start | bytes 196616 | tf_op jit(solution)/shard_map/ppermute | solution.py:49
  46.7 0.6 collective-permute-start.22
  47.3 1.4 %collective-permute-start.21 = (bf16[16,2048]{1,0:T(8,128)(2,1)S(1)}, bf16[16,2048]{1,0:T(8,128)(2,1)S(1)}, u32[]{:S(2)}, u32[]{:S(2)}) collective-permute-start(bf16[16,2048]{1,0:T(8,128)(2,1)S(1)} %add_convert_fusion.5.refs_0_), channel_id=1, source_target_pairs={{0,2},{1,3},{2,0},{3,1},{4,6},{5,7},{6,4},{7,5},{8,10},{9,11},{10,... | collective-permute-start | bytes 196616 | tf_op jit(solution)/shard_map/ppermute | solution.py:49
  48.8 2.4 %collective-permute-start.20 = (bf16[16,2048]{1,0:T(8,128)(2,1)S(1)}, bf16[16,2048]{1,0:T(8,128)(2,1)S(1)}, u32[]{:S(2)}, u32[]{:S(2)}) collective-permute-start(bf16[16,2048]{1,0:T(8,128)(2,1)S(1)} %get-tuple-element.162), channel_id=1, source_target_pairs={{0,6},{1,7},{2,4},{3,5},{4,2},{5,3},{6,0},{7,1},{8,14},{9,15},{10,... | collective-permute-start | bytes 196616 | tf_op jit(solution)/shard_map/ppermute | solution.py:49
  51.2 2.4 %collective-permute-start.18 = (bf16[16,2048]{1,0:T(8,128)(2,1)S(1)}, bf16[16,2048]{1,0:T(8,128)(2,1)S(1)}, u32[]{:S(2)}, u32[]{:S(2)}) collective-permute-start(bf16[16,2048]{1,0:T(8,128)(2,1)S(1)} %get-tuple-element.164), channel_id=1, source_target_pairs={{0,2},{1,3},{2,0},{3,1},{4,6},{5,7},{6,4},{7,5},{8,10},{9,11},{10,... | collective-permute-start | bytes 196616 | tf_op jit(solution)/shard_map/ppermute | solution.py:49
  53.7 3.6 %collective-permute-done.22.refs_4_ = bf16[16,2048]{1,0:T(8,128)(2,1)S(1)} collective-permute-done((bf16[16,2048]{1,0:T(8,128)(2,1)S(1)}, bf16[16,2048]{1,0:T(8,128)(2,1)S(1)}, u32[]{:S(2)}, u32[]{:S(2)}) %collective-permute-start.22) | collective-permute-done | bytes 65568 | tf_op jit(solution)/shard_map/ppermute | solution.py:49
  57.3 2.5 %collective-permute-done.19 = bf16[16,2048]{1,0:T(8,128)(2,1)S(1)} collective-permute-done((bf16[16,2048]{1,0:T(8,128)(2,1)S(1)}, bf16[16,2048]{1,0:T(8,128)(2,1)S(1)}, u32[]{:S(2)}, u32[]{:S(2)}) %collective-permute-start.19) | collective-permute-done | bytes 65568 | tf_op jit(solution)/shard_map/ppermute | solution.py:49
  59.8 0.5 collective-permute-start.25
  60.4 0.5 collective-permute-start.27
  60.9 2.7 %collective-permute-start.30 = (bf16[16,2048]{1,0:T(8,128)(2,1)S(1)}, bf16[16,2048]{1,0:T(8,128)(2,1)S(1)}, u32[]{:S(2)}, u32[]{:S(2)}) collective-permute-start(bf16[16,2048]{1,0:T(8,128)(2,1)S(1)} %add_convert_fusion.4.refs_8_.refs_0_), channel_id=1, source_target_pairs={{0,6},{1,7},{2,4},{3,5},{4,2},{5,3},{6,0},{7,1},{8,14},{9,15},{10,... | collective-permute-start | bytes 196616 | tf_op jit(solution)/shard_map/ppermute | solution.py:49
  63.6 1.7 %collective-permute-start.28 = (bf16[16,2048]{1,0:T(8,128)(2,1)S(1)}, bf16[16,2048]{1,0:T(8,128)(2,1)S(1)}, u32[]{:S(2)}, u32[]{:S(2)}) collective-permute-start(bf16[16,2048]{1,0:T(8,128)(2,1)S(1)} %add_convert_fusion.4.refs_8_.refs_0_), channel_id=1, source_target_pairs={{0,2},{1,3},{2,0},{3,1},{4,6},{5,7},{6,4},{7,5},{8,10},{9,11},{10,... | collective-permute-start | bytes 196616 | tf_op jit(solution)/shard_map/ppermute | solution.py:49
  65.4 1.5 %gate_up_home.1.home = bf16[128,1024]{1,0:T(8,128)(2,1)S(1)} custom-call(bf16[16,2048]{1,0:T(8,128)(2,1)S(1)} %add_convert_fusion.5.refs_0_, bf16[16,2048]{1,0:T(8,128)(2,1)S(1)} %collective-permute-done.24.refs_1_, bf16[16,2048]{1,0:T(8,128)(2,1)S(1)} %collective-permute-done.21.refs_2_, bf16[16,2048]{1,0:T(8,128)(2,1)S(1)} %collective-permute-done.25.refs_3_, ...), custom_call_target="tpu_custom_call" | custom-call | flops 2000000000 | bytes 8388608 | tf_op jit(solution)/shard_map/gate_up_home/pallas_call | solution.py:541
  66.9 0.7 collective-permute-done.30.refs_14_.refs_6_
  67.6 2.0 %collective-permute-done.29.refs_12_.refs_4_ = bf16[16,2048]{1,0:T(8,128)(2,1)S(1)} collective-permute-done((bf16[16,2048]{1,0:T(8,128)(2,1)S(1)}, bf16[16,2048]{1,0:T(8,128)(2,1)S(1)}, u32[]{:S(2)}, u32[]{:S(2)}) %collective-permute-start.29) | collective-permute-done | bytes 65568 | tf_op jit(solution)/shard_map/ppermute | solution.py:49
  69.6 0.5 collective-permute-start.32
  70.1 0.5 collective-permute-start.34
  70.6 0.2 collective-permute-done.31.refs_9_.refs_1_
  70.9 0.2 collective-permute-done.32.refs_11_.refs_3_
  71.0 0.4 collective-permute-done.33.refs_13_.refs_5_
  71.4 0.2 collective-permute-done.34.refs_15_.refs_7_
  71.5 1.4 %gate_up_far.1.far = bf16[128,1024]{1,0:T(8,128)(2,1)S(1)} custom-call(bf16[16,2048]{1,0:T(8,128)(2,1)S(1)} %add_convert_fusion.4.refs_8_.refs_0_, bf16[16,2048]{1,0:T(8,128)(2,1)S(1)} %collective-permute-done.31.refs_9_.refs_1_, bf16[16,2048]{1,0:T(8,128)(2,1)S(1)} %collective-permute-done.28.refs_10_.refs_2_, ...), custom_call_target="tpu_custom_call" | custom-call | flops 2000000000 | bytes 8388608 | tf_op jit(solution)/shard_map/gate_up_far/pallas_call | solution.py:541
  73.0 0.9 %down_first.1 = (bf16[128,1024]{1,0:T(8,128)(2,1)S(1)}, bf16[2,32,2048]{2,1,0:T(8,128)(2,1)S(1)}, bf16[2,32,2048]{2,1,0:T(8,128)(2,1)S(1)}) custom-call(bf16[128,1024]{1,0:T(8,128)(2,1)S(1)} %gate_up_home.1.home, bf16[128,1024]{1,0:T(8,128)(2,1)S(1)} %gate_up_far.1.far, s32[1,256]{1,0:T(1,128)S(1)} %get-tuple-element.94.order, bf16[1024,2048]{1,0:T(8,128)(2,1)S(1)} %copy-done), custom_call_target="tpu_custom_call" | custom-call | tf_op jit(solution)/shard_map/down_first/pallas_call | solution.py:574
  73.9 0.4 collective-permute-start.35
  74.3 0.7 down_second.1
  75.1 0.2 collective-permute-start.38
  75.3 0.2 collective-permute-done.35
  75.6 1.3 %collective-permute-start.36 = (bf16[32,2048]{1,0:T(8,128)(2,1)S(1)}, bf16[32,2048]{1,0:T(8,128)(2,1)S(1)}, u32[]{:S(2)}, u32[]{:S(2)}) collective-permute-start(bf16[32,2048]{1,0:T(8,128)(2,1)S(1)} %get-tuple-element.160), channel_id=1, source_target_pairs={{0,4},{1,5},{2,6},{3,7},{4,0},{5,1},{6,2},{7,3},{8,12},{9,13},{10,... | collective-permute-start | bytes 393224 | tf_op jit(solution)/shard_map/ppermute | solution.py:49
  76.9 2.0 %collective-permute-start.37 = (bf16[32,2048]{1,0:T(8,128)(2,1)S(1)}, bf16[32,2048]{1,0:T(8,128)(2,1)S(1)}, u32[]{:S(2)}, u32[]{:S(2)}) collective-permute-start(bf16[32,2048]{1,0:T(8,128)(2,1)S(1)} %get-tuple-element.161), channel_id=1, source_target_pairs={{0,6},{1,7},{2,4},{3,5},{4,2},{5,3},{6,0},{7,1},{8,14},{9,15},{10,... | collective-permute-start | bytes 393224 | tf_op jit(solution)/shard_map/ppermute | solution.py:49
  78.9 0.3 collective-permute-start.39
  79.2 5.6 %cache_update.1 = bf16[2,4096,256]{2,1,0:T(8,128)(2,1)} custom-call(s32[1,128]{1,0:T(1,128)S(1)} %get-tuple-element.155.home_rows, s32[1,144]{1,0:T(1,128)S(1)} %get-tuple-element.156.far_rows, bf16[128,768]{1,0:T(8,128)(2,1)S(1)} %get-tuple-element.105.packed.home, bf16[48,768]{1,0:T(8,128)(2,1)S(1)} %collective-permute-done.7.refs_0_, ...), custom_call_target="tpu_custom_call" | custom-call | flops 2000000000 | bytes 8388608 | tf_op jit(solution)/shard_map/cache_update/pallas_call | solution.py:524
  84.8 0.7 copy.14
  85.5 0.5 own_rows.1
  85.9 2.4 %collective-permute-done.36 = bf16[32,2048]{1,0:T(8,128)(2,1)S(1)} collective-permute-done((bf16[32,2048]{1,0:T(8,128)(2,1)S(1)}, bf16[32,2048]{1,0:T(8,128)(2,1)S(1)}, u32[]{:S(2)}, u32[]{:S(2)}) %collective-permute-start.36) | collective-permute-done | bytes 131104 | tf_op jit(solution)/shard_map/ppermute | solution.py:49
  88.3 1.1 %collective-permute-done.39 = bf16[32,2048]{1,0:T(8,128)(2,1)S(1)} collective-permute-done((bf16[32,2048]{1,0:T(8,128)(2,1)S(1)}, bf16[32,2048]{1,0:T(8,128)(2,1)S(1)}, u32[]{:S(2)}, u32[]{:S(2)}) %collective-permute-start.39) | collective-permute-done | bytes 131104 | tf_op jit(solution)/shard_map/ppermute | solution.py:49
  89.4 0.8 fusion.2
  (63 shorter events, 0.7 us)
Async XLA Ops:
  0.6 12.3 %collective-permute-start.1 = (bf16[32,2048]{1,0:T(8,128)(2,1)}, bf16[32,2048]{1,0:T(8,128)(2,1)S(1)}, u32[]{:S(2)}, u32[]{:S(2)}) collective-permute-start(bf16[32,2048]{1,0:T(8,128)(2,1)} %refs_0_), channel_id=1, source_target_pairs={{0,4},{1,5},{2,6},{3,7},{4,0},{5,1},{6,2},{7,3},{8,12},{9,13},{10,... | collective-permute-start | bytes 393224 | tf_op jit(solution)/shard_map/ppermute | solution.py:49
  4.7 8.2 %collective-permute-start = (bf16[32,2048]{1,0:T(8,128)(2,1)}, bf16[32,2048]{1,0:T(8,128)(2,1)S(1)}, u32[]{:S(2)}, u32[]{:S(2)}) collective-permute-start(bf16[32,2048]{1,0:T(8,128)(2,1)} %refs_0_), channel_id=1, source_target_pairs={{0,2},{1,3},{2,0},{3,1},{4,6},{5,7},{6,4},{7,5},{8,10},{9,11},{10,... | collective-permute-start | bytes 393224 | tf_op jit(solution)/shard_map/ppermute | solution.py:49
  6.3 9.0 %collective-permute-start.2 = (bf16[32,2048]{1,0:T(8,128)(2,1)}, bf16[32,2048]{1,0:T(8,128)(2,1)S(1)}, u32[]{:S(2)}, u32[]{:S(2)}) collective-permute-start(bf16[32,2048]{1,0:T(8,128)(2,1)} %refs_0_), channel_id=1, source_target_pairs={{0,6},{1,7},{2,4},{3,5},{4,2},{5,3},{6,0},{7,1},{8,14},{9,15},{10,... | collective-permute-start | bytes 393224 | tf_op jit(solution)/shard_map/ppermute | solution.py:49
  6.3 0.7 copy-start.5
  7.0 0.7 copy-start.6
  7.7 0.7 copy-start.7
  8.4 6.9 %copy-start.4 = (bf16[32,2048]{1,0:T(8,128)(2,1)S(1)}, bf16[32,2048]{1,0:T(8,128)(2,1)}, u32[]{:S(2)}) copy-start(bf16[32,2048]{1,0:T(8,128)(2,1)} %refs_0_) | copy-start | bytes 393220
  8.4 7.9 %copy-start.8 = (bf16[2048]{0:T(1024)(128)(2,1)S(1)}, bf16[2048]{0:T(1024)(128)(2,1)}, u32[]{:S(2)}) copy-start(bf16[2048]{0:T(1024)(128)(2,1)} %param.12) | copy-start | bytes 12292
  8.4 8.9 %copy-start.2 = (bf16[3,2048,256]{2,1,0:T(8,128)(2,1)S(1)}, bf16[3,2048,256]{2,1,0:T(8,128)(2,1)}, u32[]{:S(2)}) copy-start(bf16[3,2048,256]{2,1,0:T(8,128)(2,1)} %refs_9_.3) | copy-start | bytes 9437188
  8.4 14.8 %copy-start.3 = (bf16[256,2048]{1,0:T(8,128)(2,1)S(1)}, bf16[256,2048]{1,0:T(8,128)(2,1)}, u32[]{:S(2)}) copy-start(bf16[256,2048]{1,0:T(8,128)(2,1)} %refs_3_.2) | copy-start | bytes 3145732
  10.5 12.7 %copy-start.1 = (bf16[2,4096,256]{2,1,0:T(8,128)(2,1)S(1)}, bf16[2,4096,256]{2,1,0:T(8,128)(2,1)}, u32[]{:S(2)}) copy-start(bf16[2,4096,256]{2,1,0:T(8,128)(2,1)} %refs_3_.3) | copy-start | bytes 12582916
  15.3 1.3 %collective-permute-start.3 = (bf16[32,2048]{1,0:T(8,128)(2,1)S(1)}, bf16[32,2048]{1,0:T(8,128)(2,1)S(1)}, u32[]{:S(2)}, u32[]{:S(2)}) collective-permute-start(bf16[32,2048]{1,0:T(8,128)(2,1)S(1)} %copy-done.4), channel_id=1, source_target_pairs={{0,1},{1,0},{2,3},{3,2},{4,5},{5,4},{6,7},{7,6},{8,9},{9,8},{10,11... | collective-permute-start | bytes 393224 | tf_op jit(solution)/shard_map/ppermute | solution.py:49
  15.3 1.5 %collective-permute-start.4 = (bf16[32,2048]{1,0:T(8,128)(2,1)S(1)}, bf16[32,2048]{1,0:T(8,128)(2,1)S(1)}, u32[]{:S(2)}, u32[]{:S(2)}) collective-permute-start(bf16[32,2048]{1,0:T(8,128)(2,1)S(1)} %collective-permute-done.refs_2_), channel_id=1, source_target_pairs={{0,1},{1,0},{2,3},{3,2},{4,5},{5,4},{6,7},{7,6},{8,9},{9,8},{10,11... | collective-permute-start | bytes 393224 | tf_op jit(solution)/shard_map/ppermute | solution.py:49
  15.8 1.3 %collective-permute-start.5 = (bf16[32,2048]{1,0:T(8,128)(2,1)S(1)}, bf16[32,2048]{1,0:T(8,128)(2,1)S(1)}, u32[]{:S(2)}, u32[]{:S(2)}) collective-permute-start(bf16[32,2048]{1,0:T(8,128)(2,1)S(1)} %collective-permute-done.1.refs_4_), channel_id=1, source_target_pairs={{0,1},{1,0},{2,3},{3,2},{4,5},{5,4},{6,7},{7,6},{8,9},{9,8},{10,11... | collective-permute-start | bytes 393224 | tf_op jit(solution)/shard_map/ppermute | solution.py:49
  15.8 1.5 %collective-permute-start.6 = (bf16[32,2048]{1,0:T(8,128)(2,1)S(1)}, bf16[32,2048]{1,0:T(8,128)(2,1)S(1)}, u32[]{:S(2)}, u32[]{:S(2)}) collective-permute-start(bf16[32,2048]{1,0:T(8,128)(2,1)S(1)} %collective-permute-done.2.refs_6_), channel_id=1, source_target_pairs={{0,1},{1,0},{2,3},{3,2},{4,5},{5,4},{6,7},{7,6},{8,9},{9,8},{10,11... | collective-permute-start | bytes 393224 | tf_op jit(solution)/shard_map/ppermute | solution.py:49
  19.6 7.9 %collective-permute-start.7 = (bf16[48,768]{1,0:T(8,128)(2,1)S(1)}, bf16[48,768]{1,0:T(8,128)(2,1)S(1)}, u32[]{:S(2)}, u32[]{:S(2)}) collective-permute-start(bf16[48,768]{1,0:T(8,128)(2,1)S(1)} %get-tuple-element.112), channel_id=1, source_target_pairs={{0,8},{8,0},{16,24},{24,16},{1,9},{9,1},{17,25},{25,17},{2,10},{10... | collective-permute-start | bytes 221192 | tf_op jit(solution)/shard_map/ppermute | solution.py:49
  21.1 6.4 %collective-permute-start.8 = (bf16[48,768]{1,0:T(8,128)(2,1)S(1)}, bf16[48,768]{1,0:T(8,128)(2,1)S(1)}, u32[]{:S(2)}, u32[]{:S(2)}) collective-permute-start(bf16[48,768]{1,0:T(8,128)(2,1)S(1)} %get-tuple-element.113), channel_id=1, source_target_pairs={{0,16},{8,24},{16,0},{24,8},{1,17},{9,25},{17,1},{25,9},{2,18},{10... | collective-permute-start | bytes 221192 | tf_op jit(solution)/shard_map/ppermute | solution.py:49
  22.7 5.3 %collective-permute-start.9 = (bf16[48,768]{1,0:T(8,128)(2,1)S(1)}, bf16[48,768]{1,0:T(8,128)(2,1)S(1)}, u32[]{:S(2)}, u32[]{:S(2)}) collective-permute-start(bf16[48,768]{1,0:T(8,128)(2,1)S(1)} %get-tuple-element.114), channel_id=1, source_target_pairs={{0,24},{8,16},{16,8},{24,0},{1,25},{9,17},{17,9},{25,1},{2,26},{10... | collective-permute-start | bytes 221192 | tf_op jit(solution)/shard_map/ppermute | solution.py:49
  23.1 42.2 %slice-start = ((s8[8388608]{0:T(1024)(128)(4,1)}), s8[4194304]{0:T(1024)(128)(4,1)S(1)}, s32[]{:S(2)}) async-start(s8[8388608]{0:T(1024)(128)(4,1)} %bitcast.31), calls=%async_computation | async-start | bytes 8388608
  27.9 4.5 %collective-permute-start.13 = (bf16[4,16,2048]{2,1,0:T(8,128)(2,1)S(1)}, bf16[4,16,2048]{2,1,0:T(8,128)(2,1)S(1)}, u32[]{:S(2)}, u32[]{:S(2)}) collective-permute-start(bf16[4,16,2048]{2,1,0:T(8,128)(2,1)S(1)} %get-tuple-element.124), channel_id=1, source_target_pairs={{0,1},{1,0},{2,3},{3,2},{4,5},{5,4},{6,7},{7,6},{8,9},{9,8},{10,11... | collective-permute-start | bytes 786440 | tf_op jit(solution)/shard_map/ppermute | solution.py:49
  27.9 25.8 %copy-start.9 = (bf16[2048]{0:T(1024)(128)(2,1)S(1)}, bf16[2048]{0:T(1024)(128)(2,1)}, u32[]{:S(2)}) copy-start(bf16[2048]{0:T(1024)(128)(2,1)} %param.13) | copy-start | bytes 12292
  27.9 37.5 %slice-start.1 = ((s8[8388608]{0:T(1024)(128)(4,1)}), s8[4194304]{0:T(1024)(128)(4,1)S(1)}, s32[]{:S(2)}) async-start(s8[8388608]{0:T(1024)(128)(4,1)} %bitcast.31), calls=%async_computation.1 | async-start | bytes 8388608
  32.3 6.4 %collective-permute-start.10 = (bf16[48,384]{1,0:T(8,128)(2,1)S(1)}, bf16[48,384]{1,0:T(8,128)(2,1)S(1)}, u32[]{:S(2)}, u32[]{:S(2)}) collective-permute-start(bf16[48,384]{1,0:T(8,128)(2,1)S(1)} %get-tuple-element.120), channel_id=1, source_target_pairs={{0,8},{8,0},{16,24},{24,16},{1,9},{9,1},{17,25},{25,17},{2,10},{10... | collective-permute-start | bytes 110600 | tf_op jit(solution)/shard_map/ppermute | solution.py:49
  32.5 11.1 %collective-permute-start.16 = (bf16[16,2048]{1,0:T(8,128)(2,1)S(1)}, bf16[16,2048]{1,0:T(8,128)(2,1)S(1)}, u32[]{:S(2)}, u32[]{:S(2)}) collective-permute-start(bf16[16,2048]{1,0:T(8,128)(2,1)S(1)} %get-tuple-element.166), channel_id=1, source_target_pairs={{0,6},{1,7},{2,4},{3,5},{4,2},{5,3},{6,0},{7,1},{8,14},{9,15},{10,... | collective-permute-start | bytes 196616 | tf_op jit(solution)/shard_map/ppermute | solution.py:49
  35.0 8.6 %collective-permute-start.15 = (bf16[16,2048]{1,0:T(8,128)(2,1)S(1)}, bf16[16,2048]{1,0:T(8,128)(2,1)S(1)}, u32[]{:S(2)}, u32[]{:S(2)}) collective-permute-start(bf16[16,2048]{1,0:T(8,128)(2,1)S(1)} %get-tuple-element.167), channel_id=1, source_target_pairs={{0,4},{1,5},{2,6},{3,7},{4,0},{5,1},{6,2},{7,3},{8,12},{9,13},{10,... | collective-permute-start | bytes 196616 | tf_op jit(solution)/shard_map/ppermute | solution.py:49
  36.9 6.7 %collective-permute-start.14 = (bf16[16,2048]{1,0:T(8,128)(2,1)S(1)}, bf16[16,2048]{1,0:T(8,128)(2,1)S(1)}, u32[]{:S(2)}, u32[]{:S(2)}) collective-permute-start(bf16[16,2048]{1,0:T(8,128)(2,1)S(1)} %get-tuple-element.168), channel_id=1, source_target_pairs={{0,2},{1,3},{2,0},{3,1},{4,6},{5,7},{6,4},{7,5},{8,10},{9,11},{10,... | collective-permute-start | bytes 196616 | tf_op jit(solution)/shard_map/ppermute | solution.py:49
  37.3 4.0 %collective-permute-start.11 = (bf16[48,384]{1,0:T(8,128)(2,1)S(1)}, bf16[48,384]{1,0:T(8,128)(2,1)S(1)}, u32[]{:S(2)}, u32[]{:S(2)}) collective-permute-start(bf16[48,384]{1,0:T(8,128)(2,1)S(1)} %get-tuple-element.121), channel_id=1, source_target_pairs={{0,16},{8,24},{16,0},{24,8},{1,17},{9,25},{17,1},{25,9},{2,18},{10... | collective-permute-start | bytes 110600 | tf_op jit(solution)/shard_map/ppermute | solution.py:49
  38.7 4.9 %collective-permute-start.12 = (bf16[48,384]{1,0:T(8,128)(2,1)S(1)}, bf16[48,384]{1,0:T(8,128)(2,1)S(1)}, u32[]{:S(2)}, u32[]{:S(2)}) collective-permute-start(bf16[48,384]{1,0:T(8,128)(2,1)S(1)} %get-tuple-element.122), channel_id=1, source_target_pairs={{0,24},{8,16},{16,8},{24,0},{1,25},{9,17},{17,9},{25,1},{2,26},{10... | collective-permute-start | bytes 110600 | tf_op jit(solution)/shard_map/ppermute | solution.py:49
  44.1 4.6 %collective-permute-start.17 = (bf16[4,16,2048]{2,1,0:T(8,128)(2,1)S(1)}, bf16[4,16,2048]{2,1,0:T(8,128)(2,1)S(1)}, u32[]{:S(2)}, u32[]{:S(2)}) collective-permute-start(bf16[4,16,2048]{2,1,0:T(8,128)(2,1)S(1)} %get-tuple-element.129), channel_id=1, source_target_pairs={{0,1},{1,0},{2,3},{3,2},{4,5},{5,4},{6,7},{7,6},{8,9},{9,8},{10,11... | collective-permute-start | bytes 786440 | tf_op jit(solution)/shard_map/ppermute | solution.py:49
  44.3 7.0 %collective-permute-start.23 = (bf16[16,2048]{1,0:T(8,128)(2,1)S(1)}, bf16[16,2048]{1,0:T(8,128)(2,1)S(1)}, u32[]{:S(2)}, u32[]{:S(2)}) collective-permute-start(bf16[16,2048]{1,0:T(8,128)(2,1)S(1)} %add_convert_fusion.5.refs_0_), channel_id=1, source_target_pairs={{0,6},{1,7},{2,4},{3,5},{4,2},{5,3},{6,0},{7,1},{8,14},{9,15},{10,... | collective-permute-start | bytes 196616 | tf_op jit(solution)/shard_map/ppermute | solution.py:49
  46.7 10.6 %collective-permute-start.22 = (bf16[16,2048]{1,0:T(8,128)(2,1)S(1)}, bf16[16,2048]{1,0:T(8,128)(2,1)S(1)}, u32[]{:S(2)}, u32[]{:S(2)}) collective-permute-start(bf16[16,2048]{1,0:T(8,128)(2,1)S(1)} %add_convert_fusion.5.refs_0_), channel_id=1, source_target_pairs={{0,4},{1,5},{2,6},{3,7},{4,0},{5,1},{6,2},{7,3},{8,12},{9,13},{10,... | collective-permute-start | bytes 196616 | tf_op jit(solution)/shard_map/ppermute | solution.py:49
  47.3 10.0 %collective-permute-start.21 = (bf16[16,2048]{1,0:T(8,128)(2,1)S(1)}, bf16[16,2048]{1,0:T(8,128)(2,1)S(1)}, u32[]{:S(2)}, u32[]{:S(2)}) collective-permute-start(bf16[16,2048]{1,0:T(8,128)(2,1)S(1)} %add_convert_fusion.5.refs_0_), channel_id=1, source_target_pairs={{0,2},{1,3},{2,0},{3,1},{4,6},{5,7},{6,4},{7,5},{8,10},{9,11},{10,... | collective-permute-start | bytes 196616 | tf_op jit(solution)/shard_map/ppermute | solution.py:49
  48.8 8.5 %collective-permute-start.20 = (bf16[16,2048]{1,0:T(8,128)(2,1)S(1)}, bf16[16,2048]{1,0:T(8,128)(2,1)S(1)}, u32[]{:S(2)}, u32[]{:S(2)}) collective-permute-start(bf16[16,2048]{1,0:T(8,128)(2,1)S(1)} %get-tuple-element.162), channel_id=1, source_target_pairs={{0,6},{1,7},{2,4},{3,5},{4,2},{5,3},{6,0},{7,1},{8,14},{9,15},{10,... | collective-permute-start | bytes 196616 | tf_op jit(solution)/shard_map/ppermute | solution.py:49
  51.2 8.6 %collective-permute-start.19 = (bf16[16,2048]{1,0:T(8,128)(2,1)S(1)}, bf16[16,2048]{1,0:T(8,128)(2,1)S(1)}, u32[]{:S(2)}, u32[]{:S(2)}) collective-permute-start(bf16[16,2048]{1,0:T(8,128)(2,1)S(1)} %get-tuple-element.163), channel_id=1, source_target_pairs={{0,4},{1,5},{2,6},{3,7},{4,0},{5,1},{6,2},{7,3},{8,12},{9,13},{10,... | collective-permute-start | bytes 196616 | tf_op jit(solution)/shard_map/ppermute | solution.py:49
  51.2 8.6 %collective-permute-start.18 = (bf16[16,2048]{1,0:T(8,128)(2,1)S(1)}, bf16[16,2048]{1,0:T(8,128)(2,1)S(1)}, u32[]{:S(2)}, u32[]{:S(2)}) collective-permute-start(bf16[16,2048]{1,0:T(8,128)(2,1)S(1)} %get-tuple-element.164), channel_id=1, source_target_pairs={{0,2},{1,3},{2,0},{3,1},{4,6},{5,7},{6,4},{7,5},{8,10},{9,11},{10,... | collective-permute-start | bytes 196616 | tf_op jit(solution)/shard_map/ppermute | solution.py:49
  59.8 3.8 %collective-permute-start.24 = (bf16[16,2048]{1,0:T(8,128)(2,1)S(1)}, bf16[16,2048]{1,0:T(8,128)(2,1)S(1)}, u32[]{:S(2)}, u32[]{:S(2)}) collective-permute-start(bf16[16,2048]{1,0:T(8,128)(2,1)S(1)} %add_convert_fusion.5.refs_0_), channel_id=1, source_target_pairs={{0,1},{1,0},{2,3},{3,2},{4,5},{5,4},{6,7},{7,6},{8,9},{9,8},{10,11... | collective-permute-start | bytes 196616 | tf_op jit(solution)/shard_map/ppermute | solution.py:49
  59.8 3.8 %collective-permute-start.25 = (bf16[16,2048]{1,0:T(8,128)(2,1)S(1)}, bf16[16,2048]{1,0:T(8,128)(2,1)S(1)}, u32[]{:S(2)}, u32[]{:S(2)}) collective-permute-start(bf16[16,2048]{1,0:T(8,128)(2,1)S(1)} %collective-permute-done.21.refs_2_), channel_id=1, source_target_pairs={{0,1},{1,0},{2,3},{3,2},{4,5},{5,4},{6,7},{7,6},{8,9},{9,8},{10,11... | collective-permute-start | bytes 196616 | tf_op jit(solution)/shard_map/ppermute | solution.py:49
  60.4 5.0 %collective-permute-start.26 = (bf16[16,2048]{1,0:T(8,128)(2,1)S(1)}, bf16[16,2048]{1,0:T(8,128)(2,1)S(1)}, u32[]{:S(2)}, u32[]{:S(2)}) collective-permute-start(bf16[16,2048]{1,0:T(8,128)(2,1)S(1)} %collective-permute-done.22.refs_4_), channel_id=1, source_target_pairs={{0,1},{1,0},{2,3},{3,2},{4,5},{5,4},{6,7},{7,6},{8,9},{9,8},{10,11... | collective-permute-start | bytes 196616 | tf_op jit(solution)/shard_map/ppermute | solution.py:49
  60.4 5.0 %collective-permute-start.27 = (bf16[16,2048]{1,0:T(8,128)(2,1)S(1)}, bf16[16,2048]{1,0:T(8,128)(2,1)S(1)}, u32[]{:S(2)}, u32[]{:S(2)}) collective-permute-start(bf16[16,2048]{1,0:T(8,128)(2,1)S(1)} %collective-permute-done.23.refs_6_), channel_id=1, source_target_pairs={{0,1},{1,0},{2,3},{3,2},{4,5},{5,4},{6,7},{7,6},{8,9},{9,8},{10,11... | collective-permute-start | bytes 196616 | tf_op jit(solution)/shard_map/ppermute | solution.py:49
  60.9 6.7 %collective-permute-start.30 = (bf16[16,2048]{1,0:T(8,128)(2,1)S(1)}, bf16[16,2048]{1,0:T(8,128)(2,1)S(1)}, u32[]{:S(2)}, u32[]{:S(2)}) collective-permute-start(bf16[16,2048]{1,0:T(8,128)(2,1)S(1)} %add_convert_fusion.4.refs_8_.refs_0_), channel_id=1, source_target_pairs={{0,6},{1,7},{2,4},{3,5},{4,2},{5,3},{6,0},{7,1},{8,14},{9,15},{10,... | collective-permute-start | bytes 196616 | tf_op jit(solution)/shard_map/ppermute | solution.py:49
  63.6 6.0 %collective-permute-start.29 = (bf16[16,2048]{1,0:T(8,128)(2,1)S(1)}, bf16[16,2048]{1,0:T(8,128)(2,1)S(1)}, u32[]{:S(2)}, u32[]{:S(2)}) collective-permute-start(bf16[16,2048]{1,0:T(8,128)(2,1)S(1)} %add_convert_fusion.4.refs_8_.refs_0_), channel_id=1, source_target_pairs={{0,4},{1,5},{2,6},{3,7},{4,0},{5,1},{6,2},{7,3},{8,12},{9,13},{10,... | collective-permute-start | bytes 196616 | tf_op jit(solution)/shard_map/ppermute | solution.py:49
  63.6 6.0 %collective-permute-start.28 = (bf16[16,2048]{1,0:T(8,128)(2,1)S(1)}, bf16[16,2048]{1,0:T(8,128)(2,1)S(1)}, u32[]{:S(2)}, u32[]{:S(2)}) collective-permute-start(bf16[16,2048]{1,0:T(8,128)(2,1)S(1)} %add_convert_fusion.4.refs_8_.refs_0_), channel_id=1, source_target_pairs={{0,2},{1,3},{2,0},{3,1},{4,6},{5,7},{6,4},{7,5},{8,10},{9,11},{10,... | collective-permute-start | bytes 196616 | tf_op jit(solution)/shard_map/ppermute | solution.py:49
  66.9 6.1 %copy-start = (bf16[1024,2048]{1,0:T(8,128)(2,1)S(1)}, bf16[1024,2048]{1,0:T(8,128)(2,1)}, u32[]{:S(2)}) copy-start(bf16[1024,2048]{1,0:T(8,128)(2,1)} %down.3) | copy-start | bytes 12582916
  69.6 1.3 %collective-permute-start.31 = (bf16[16,2048]{1,0:T(8,128)(2,1)S(1)}, bf16[16,2048]{1,0:T(8,128)(2,1)S(1)}, u32[]{:S(2)}, u32[]{:S(2)}) collective-permute-start(bf16[16,2048]{1,0:T(8,128)(2,1)S(1)} %add_convert_fusion.4.refs_8_.refs_0_), channel_id=1, source_target_pairs={{0,1},{1,0},{2,3},{3,2},{4,5},{5,4},{6,7},{7,6},{8,9},{9,8},{10,11... | collective-permute-start | bytes 196616 | tf_op jit(solution)/shard_map/ppermute | solution.py:49
  69.6 1.4 %collective-permute-start.32 = (bf16[16,2048]{1,0:T(8,128)(2,1)S(1)}, bf16[16,2048]{1,0:T(8,128)(2,1)S(1)}, u32[]{:S(2)}, u32[]{:S(2)}) collective-permute-start(bf16[16,2048]{1,0:T(8,128)(2,1)S(1)} %collective-permute-done.28.refs_10_.refs_2_), channel_id=1, source_target_pairs={{0,1},{1,0},{2,3},{3,2},{4,5},{5,4},{6,7},{7,6},{8,9},{9,8},{10,11... | collective-permute-start | bytes 196616 | tf_op jit(solution)/shard_map/ppermute | solution.py:49
  70.1 1.3 %collective-permute-start.33 = (bf16[16,2048]{1,0:T(8,128)(2,1)S(1)}, bf16[16,2048]{1,0:T(8,128)(2,1)S(1)}, u32[]{:S(2)}, u32[]{:S(2)}) collective-permute-start(bf16[16,2048]{1,0:T(8,128)(2,1)S(1)} %collective-permute-done.29.refs_12_.refs_4_), channel_id=1, source_target_pairs={{0,1},{1,0},{2,3},{3,2},{4,5},{5,4},{6,7},{7,6},{8,9},{9,8},{10,11... | collective-permute-start | bytes 196616 | tf_op jit(solution)/shard_map/ppermute | solution.py:49
  70.1 1.4 %collective-permute-start.34 = (bf16[16,2048]{1,0:T(8,128)(2,1)S(1)}, bf16[16,2048]{1,0:T(8,128)(2,1)S(1)}, u32[]{:S(2)}, u32[]{:S(2)}) collective-permute-start(bf16[16,2048]{1,0:T(8,128)(2,1)S(1)} %collective-permute-done.30.refs_14_.refs_6_), channel_id=1, source_target_pairs={{0,1},{1,0},{2,3},{3,2},{4,5},{5,4},{6,7},{7,6},{8,9},{9,8},{10,11... | collective-permute-start | bytes 196616 | tf_op jit(solution)/shard_map/ppermute | solution.py:49
  73.9 1.6 %collective-permute-start.35 = (bf16[2,32,2048]{2,1,0:T(8,128)(2,1)S(1)}, bf16[2,32,2048]{2,1,0:T(8,128)(2,1)S(1)}, u32[]{:S(2)}, u32[]{:S(2)}) collective-permute-start(bf16[2,32,2048]{2,1,0:T(8,128)(2,1)S(1)} %get-tuple-element.150), channel_id=1, source_target_pairs={{0,1},{1,0},{2,3},{3,2},{4,5},{5,4},{6,7},{7,6},{8,9},{9,8},{10,11... | collective-permute-start | bytes 786440 | tf_op jit(solution)/shard_map/ppermute | solution.py:49
  75.1 3.8 %collective-permute-start.38 = (bf16[2,32,2048]{2,1,0:T(8,128)(2,1)S(1)}, bf16[2,32,2048]{2,1,0:T(8,128)(2,1)S(1)}, u32[]{:S(2)}, u32[]{:S(2)}) collective-permute-start(bf16[2,32,2048]{2,1,0:T(8,128)(2,1)S(1)} %get-tuple-element.153), channel_id=1, source_target_pairs={{0,1},{1,0},{2,3},{3,2},{4,5},{5,4},{6,7},{7,6},{8,9},{9,8},{10,11... | collective-permute-start | bytes 786440 | tf_op jit(solution)/shard_map/ppermute | solution.py:49
  75.6 12.7 %collective-permute-start.36 = (bf16[32,2048]{1,0:T(8,128)(2,1)S(1)}, bf16[32,2048]{1,0:T(8,128)(2,1)S(1)}, u32[]{:S(2)}, u32[]{:S(2)}) collective-permute-start(bf16[32,2048]{1,0:T(8,128)(2,1)S(1)} %get-tuple-element.160), channel_id=1, source_target_pairs={{0,4},{1,5},{2,6},{3,7},{4,0},{5,1},{6,2},{7,3},{8,12},{9,13},{10,... | collective-permute-start | bytes 393224 | tf_op jit(solution)/shard_map/ppermute | solution.py:49
  76.9 11.4 %collective-permute-start.37 = (bf16[32,2048]{1,0:T(8,128)(2,1)S(1)}, bf16[32,2048]{1,0:T(8,128)(2,1)S(1)}, u32[]{:S(2)}, u32[]{:S(2)}) collective-permute-start(bf16[32,2048]{1,0:T(8,128)(2,1)S(1)} %get-tuple-element.161), channel_id=1, source_target_pairs={{0,6},{1,7},{2,4},{3,5},{4,2},{5,3},{6,0},{7,1},{8,14},{9,15},{10,... | collective-permute-start | bytes 393224 | tf_op jit(solution)/shard_map/ppermute | solution.py:49
  78.9 10.5 %collective-permute-start.39 = (bf16[32,2048]{1,0:T(8,128)(2,1)S(1)}, bf16[32,2048]{1,0:T(8,128)(2,1)S(1)}, u32[]{:S(2)}, u32[]{:S(2)}) collective-permute-start(bf16[32,2048]{1,0:T(8,128)(2,1)S(1)} %fusion.6), channel_id=1, source_target_pairs={{0,2},{1,3},{2,0},{3,1},{4,6},{5,7},{6,4},{7,5},{8,10},{9,11},{10,... | collective-permute-start | bytes 393224 | tf_op jit(solution)/shard_map/ppermute | solution.py:49

commit v5 on v4

--- a/solution.py
+++ b/solution.py
@@ -560,9 +560,7 @@
         name="project_out_far",
     )(slots, far_pick, home_att, *backs, project_out)
     log_sum_exp = log_sum[:, :heads]
-    far_sums, home_far_chips = lax.optimization_barrier(
-        (reduce_chips(keep, send, 0), home_far_chips)
-    )
+    far_sums = reduce_chips(keep, send, 0)
     home_pieces = gather_cores(home_far_chips)
     far_pieces, home_inner = gather_tensor(
         add_up(token_far, far_sums), lambda: gate(home_pieces, "gate_up_home")

time: 91.8 us -> 90.2 us (0.983); the launches traced: 90.2 us -> 91 us
  starting transfers between devices: 38.8 us -> 42.2 us
  waiting for transfers between devices: 22.4 us -> 21 us
  Pallas kernels: 24.2 us -> 23 us
    ppermute x40, starting transfers between devices: 38.8 us -> 42.2 us  [swap(): lax.ppermute(values, axis_name, [(i, i ^ offset) for i in range(count)])]
    ppermute x40, waiting for transfers between devices: 22.4 us -> 21 us  [swap(): lax.ppermute(values, axis_name, [(i, i ^ offset) for i in range(count)])]
    pallas_call x1, Pallas kernels: 4.38 us -> 3.15 us  [on_device(): pl.pallas_call(functools.partial(far_kernel, heads, hops), out_shape=[sha...]
  transfers between devices with their start and end apart: 40 -> 40, of which waited for: 20 -> 20; matrix products, arithmetic and copies ran while one was open for 1% -> 1% of each run, Pallas kernels for 21% -> 19%
where the time goes in v5:
time: 90.2 us; the launch traced here: 91 us
  starting transfers between devices  42.2 us (47%)
  Pallas kernels  23 us (25%)
  waiting for transfers between devices  21 us (23%)
  local copies, waits for them, and re-layouts  2.78 us (3%)
  other arithmetic  1.1 us (1%)
    ppermute x40, starting transfers between devices, swap(): lax.ppermute(values, axis_name, [(i, i ^ offset) for i in range(count)])  42.2 us
    ppermute x40, waiting for transfers between devices, swap(): lax.ppermute(values, axis_name, [(i, i ^ offset) for i in range(count)])  21 us
    pallas_call x1, Pallas kernels, on_device(): pl.pallas_call(functools.partial(update_kernel, hops, width), grid=(cache...  5.54 us
    pallas_call x1, Pallas kernels, on_device(): pl.pallas_call(functools.partial(home_kernel, heads), out_shape=[shape((h...  4.35 us
    pallas_call x1, Pallas kernels, on_device(): pl.pallas_call(functools.partial(far_kernel, heads, hops), out_shape=[sha...  3.15 us
    pallas_call x2, Pallas kernels, on_device(): pl.pallas_call(functools.partial(gate_kernel, tensor_count), out_shape=sh...  2.91 us
    unnamed x25, local copies, waits for them, and re-layouts  2.77 us
    pallas_call x1, Pallas kernels, on_device(): pl.pallas_call(functools.partial(qkv_kernel, tensor_count, home_count, sl...  2.31 us
  transfers between devices with their start and end apart: 40, of which 20 were waited for; matrix products, arithmetic and copies ran while one was open for 1% of the time, Pallas kernels for 19%

profile of v5, /device:TPU:0, one launch (start us, length us, event | category | flops | bytes accessed | tf_op | source)
XLA Modules:
  0.0 91.0 jit_solution(9171751110077366715)
XLA Ops:
  0.6 4.1 %collective-permute-start.1 = (bf16[32,2048]{1,0:T(8,128)(2,1)}, bf16[32,2048]{1,0:T(8,128)(2,1)S(1)}, u32[]{:S(2)}, u32[]{:S(2)}) collective-permute-start(bf16[32,2048]{1,0:T(8,128)(2,1)} %refs_0_), channel_id=1, source_target_pairs={{0,4},{1,5},{2,6},{3,7},{4,0},{5,1},{6,2},{7,3},{8,12},{9,13},{10,... | collective-permute-start | bytes 393224 | tf_op jit(solution)/shard_map/ppermute | solution.py:49
  4.7 1.6 %collective-permute-start = (bf16[32,2048]{1,0:T(8,128)(2,1)}, bf16[32,2048]{1,0:T(8,128)(2,1)S(1)}, u32[]{:S(2)}, u32[]{:S(2)}) collective-permute-start(bf16[32,2048]{1,0:T(8,128)(2,1)} %refs_0_), channel_id=1, source_target_pairs={{0,2},{1,3},{2,0},{3,1},{4,6},{5,7},{6,4},{7,5},{8,10},{9,11},{10,... | collective-permute-start | bytes 393224 | tf_op jit(solution)/shard_map/ppermute | solution.py:49
  6.3 0.7 copy-done.5
  7.0 0.7 copy-done.6
  7.7 0.7 copy-done.7
  8.4 2.1 %plan.1 = (s32[1,256]{1,0:T(1,128)S(1)}, s32[1,256]{1,0:T(1,128)S(1)}, s32[1,256]{1,0:T(1,128)S(1)}, s32[1,144]{1,0:T(1,128)S(1)}, f32[256,128]{1,0:T(8,128)S(1)...) custom-call(s32[1,1024]{1,0:T(1,128)S(1)} %bitcast.37, ...), custom_call_target="tpu_custom_call" | custom-call | flops 4000000000 | bytes 1000000 | tf_op jit(solution)/shard_map/plan/pallas_call | solution.py:428
  10.5 2.4 %collective-permute-done.1.refs_4_ = bf16[32,2048]{1,0:T(8,128)(2,1)S(1)} collective-permute-done((bf16[32,2048]{1,0:T(8,128)(2,1)}, bf16[32,2048]{1,0:T(8,128)(2,1)S(1)}, u32[]{:S(2)}, u32[]{:S(2)}) %collective-permute-start.1) | collective-permute-done | bytes 131104 | tf_op jit(solution)/shard_map/ppermute | solution.py:49
  12.9 2.4 %collective-permute-done.2.refs_6_ = bf16[32,2048]{1,0:T(8,128)(2,1)S(1)} collective-permute-done((bf16[32,2048]{1,0:T(8,128)(2,1)}, bf16[32,2048]{1,0:T(8,128)(2,1)S(1)}, u32[]{:S(2)}, u32[]{:S(2)}) %collective-permute-start.2) | collective-permute-done | bytes 131104 | tf_op jit(solution)/shard_map/ppermute | solution.py:49
  15.3 0.5 collective-permute-start.4
  15.8 0.5 collective-permute-start.6
  16.3 0.3 collective-permute-done.3.refs_1_
  16.6 0.2 collective-permute-done.4.refs_3_
  16.8 0.3 collective-permute-done.5.refs_5_
  17.1 0.2 collective-permute-done.6.refs_7_
  17.3 2.3 %qkv.1 = (bf16[128,768]{1,0:T(8,128)(2,1)S(1)}, bf16[48,768]{1,0:T(8,128)(2,1)S(1)}, bf16[48,768]{1,0:T(8,128)(2,1)S(1)}, bf16[48,768]{1,0:T(8,128)(2,1)S(1)}, b...) custom-call(bf16[32,2048]{1,0:T(8,128)(2,1)S(1)} %copy-done.4, ...), custom_call_target="tpu_custom_call" | custom-call | tf_op jit(solution)/shard_map/qkv/pallas_call | solution.py:476
  19.6 1.5 %collective-permute-start.7 = (bf16[48,768]{1,0:T(8,128)(2,1)S(1)}, bf16[48,768]{1,0:T(8,128)(2,1)S(1)}, u32[]{:S(2)}, u32[]{:S(2)}) collective-permute-start(bf16[48,768]{1,0:T(8,128)(2,1)S(1)} %get-tuple-element.103), channel_id=1, source_target_pairs={{0,8},{8,0},{16,24},{24,16},{1,9},{9,1},{17,25},{25,17},{2,10},{10... | collective-permute-start | bytes 221192 | tf_op jit(solution)/shard_map/ppermute | solution.py:49
  21.1 1.5 %collective-permute-start.8 = (bf16[48,768]{1,0:T(8,128)(2,1)S(1)}, bf16[48,768]{1,0:T(8,128)(2,1)S(1)}, u32[]{:S(2)}, u32[]{:S(2)}) collective-permute-start(bf16[48,768]{1,0:T(8,128)(2,1)S(1)} %get-tuple-element.104), channel_id=1, source_target_pairs={{0,16},{8,24},{16,0},{24,8},{1,17},{9,25},{17,1},{25,9},{2,18},{10... | collective-permute-start | bytes 221192 | tf_op jit(solution)/shard_map/ppermute | solution.py:49
  22.7 0.5 collective-permute-start.9
  23.1 4.4 %home_attention.1 = (bf16[128,384]{1,0:T(8,128)(2,1)S(1)}, bf16[4,16,2048]{2,1,0:T(8,128)(2,1)S(1)}, bf16[4,16,2048]{2,1,0:T(8,128)(2,1)S(1)}) custom-call(s32[2,2]{1,0:T(2,128)S(1)} %get-tuple-element.97.bounds, bf16[128,768]{1,0:T(8,128)(2,1)S(1)} %get-tuple-element.98.packed.home, s32[128,1]{1,0:T(8,128)S(1)} %get-tuple-element.99.starts, ...), custom_call_target="tpu_custom_call" | custom-call | flops 2000000000 | bytes 4194304 | tf_op jit(solution)/shard_map/home_attention/pallas_call | solution.py:494
  27.5 0.4 collective-permute-done.9.refs_2_
  27.9 3.2 %far_attention.1 = (bf16[48,384]{1,0:T(8,128)(2,1)S(1)}, bf16[48,384]{1,0:T(8,128)(2,1)S(1)}, bf16[48,384]{1,0:T(8,128)(2,1)S(1)}) custom-call(s32[2,3]{1,0:T(2,128)S(1)} %get-tuple-element.96.bounds, bf16[48,768]{1,0:T(8,128)(2,1)S(1)} %collective-permute-done.7.refs_0_, bf16[48,768]{1,0:T(8,128)(2,1)S(1)} %collective-permute-done.8.refs_1_, ...), custom_call_target="tpu_custom_call" | custom-call | flops 2000000000 | bytes 4194304 | tf_op jit(solution)/shard_map/far_attention/pallas_call | solution.py:506
  31.1 2.5 %collective-permute-start.10 = (bf16[48,384]{1,0:T(8,128)(2,1)S(1)}, bf16[48,384]{1,0:T(8,128)(2,1)S(1)}, u32[]{:S(2)}, u32[]{:S(2)}) collective-permute-start(bf16[48,384]{1,0:T(8,128)(2,1)S(1)} %get-tuple-element.112), channel_id=1, source_target_pairs={{0,8},{8,0},{16,24},{24,16},{1,9},{9,1},{17,25},{25,17},{2,10},{10... | collective-permute-start | bytes 110600 | tf_op jit(solution)/shard_map/ppermute | solution.py:49
  33.7 2.5 %collective-permute-start.16 = (bf16[16,2048]{1,0:T(8,128)(2,1)S(1)}, bf16[16,2048]{1,0:T(8,128)(2,1)S(1)}, u32[]{:S(2)}, u32[]{:S(2)}) collective-permute-start(bf16[16,2048]{1,0:T(8,128)(2,1)S(1)} %get-tuple-element.149), channel_id=1, source_target_pairs={{0,6},{1,7},{2,4},{3,5},{4,2},{5,3},{6,0},{7,1},{8,14},{9,15},{10,... | collective-permute-start | bytes 196616 | tf_op jit(solution)/shard_map/ppermute | solution.py:49
  36.2 1.9 %collective-permute-start.15 = (bf16[16,2048]{1,0:T(8,128)(2,1)S(1)}, bf16[16,2048]{1,0:T(8,128)(2,1)S(1)}, u32[]{:S(2)}, u32[]{:S(2)}) collective-permute-start(bf16[16,2048]{1,0:T(8,128)(2,1)S(1)} %get-tuple-element.150), channel_id=1, source_target_pairs={{0,4},{1,5},{2,6},{3,7},{4,0},{5,1},{6,2},{7,3},{8,12},{9,13},{10,... | collective-permute-start | bytes 196616 | tf_op jit(solution)/shard_map/ppermute | solution.py:49
  38.0 0.5 collective-permute-start.14
  38.5 2.2 %collective-permute-start.11 = (bf16[48,384]{1,0:T(8,128)(2,1)S(1)}, bf16[48,384]{1,0:T(8,128)(2,1)S(1)}, u32[]{:S(2)}, u32[]{:S(2)}) collective-permute-start(bf16[48,384]{1,0:T(8,128)(2,1)S(1)} %get-tuple-element.113), channel_id=1, source_target_pairs={{0,16},{8,24},{16,0},{24,8},{1,17},{9,25},{17,1},{25,9},{2,18},{10... | collective-permute-start | bytes 110600 | tf_op jit(solution)/shard_map/ppermute | solution.py:49
  40.7 1.4 %collective-permute-start.12 = (bf16[48,384]{1,0:T(8,128)(2,1)S(1)}, bf16[48,384]{1,0:T(8,128)(2,1)S(1)}, u32[]{:S(2)}, u32[]{:S(2)}) collective-permute-start(bf16[48,384]{1,0:T(8,128)(2,1)S(1)} %get-tuple-element.114), channel_id=1, source_target_pairs={{0,24},{8,16},{16,8},{24,0},{1,25},{9,17},{17,9},{25,1},{2,26},{10... | collective-permute-start | bytes 110600 | tf_op jit(solution)/shard_map/ppermute | solution.py:49
  42.1 0.5 collective-permute-done.11.refs_1_
  42.6 2.9 %collective-permute-done.12.refs_2_ = bf16[48,384]{1,0:T(8,128)(2,1)S(1)} collective-permute-done((bf16[48,384]{1,0:T(8,128)(2,1)S(1)}, bf16[48,384]{1,0:T(8,128)(2,1)S(1)}, u32[]{:S(2)}, u32[]{:S(2)}) %collective-permute-start.12) | collective-permute-done | bytes 36896 | tf_op jit(solution)/shard_map/ppermute | solution.py:49
  45.6 0.6 project_out_far.1
  46.3 2.4 %collective-permute-start.22 = (bf16[16,2048]{1,0:T(8,128)(2,1)S(1)}, bf16[16,2048]{1,0:T(8,128)(2,1)S(1)}, u32[]{:S(2)}, u32[]{:S(2)}) collective-permute-start(bf16[16,2048]{1,0:T(8,128)(2,1)S(1)} %add_convert_fusion.8.refs_0_), channel_id=1, source_target_pairs={{0,6},{1,7},{2,4},{3,5},{4,2},{5,3},{6,0},{7,1},{8,14},{9,15},{10,... | collective-permute-start | bytes 196616 | tf_op jit(solution)/shard_map/ppermute | solution.py:49
  48.7 0.6 collective-permute-start.20
  49.4 1.4 %collective-permute-start.18 = (bf16[16,2048]{1,0:T(8,128)(2,1)S(1)}, bf16[16,2048]{1,0:T(8,128)(2,1)S(1)}, u32[]{:S(2)}, u32[]{:S(2)}) collective-permute-start(bf16[16,2048]{1,0:T(8,128)(2,1)S(1)} %add_convert_fusion.8.refs_0_), channel_id=1, source_target_pairs={{0,2},{1,3},{2,0},{3,1},{4,6},{5,7},{6,4},{7,5},{8,10},{9,11},{10,... | collective-permute-start | bytes 196616 | tf_op jit(solution)/shard_map/ppermute | solution.py:49
  50.8 0.7 collective-permute-start.25
  51.5 2.8 %collective-permute-start.27 = (bf16[16,2048]{1,0:T(8,128)(2,1)S(1)}, bf16[16,2048]{1,0:T(8,128)(2,1)S(1)}, u32[]{:S(2)}, u32[]{:S(2)}) collective-permute-start(bf16[16,2048]{1,0:T(8,128)(2,1)S(1)} %get-tuple-element.147), channel_id=1, source_target_pairs={{0,6},{1,7},{2,4},{3,5},{4,2},{5,3},{6,0},{7,1},{8,14},{9,15},{10,... | collective-permute-start | bytes 196616 | tf_op jit(solution)/shard_map/ppermute | solution.py:49
  54.4 2.6 %collective-permute-start.26 = (bf16[16,2048]{1,0:T(8,128)(2,1)S(1)}, bf16[16,2048]{1,0:T(8,128)(2,1)S(1)}, u32[]{:S(2)}, u32[]{:S(2)}) collective-permute-start(bf16[16,2048]{1,0:T(8,128)(2,1)S(1)} %get-tuple-element.148), channel_id=1, source_target_pairs={{0,4},{1,5},{2,6},{3,7},{4,0},{5,1},{6,2},{7,3},{8,12},{9,13},{10,... | collective-permute-start | bytes 196616 | tf_op jit(solution)/shard_map/ppermute | solution.py:49
  57.0 0.5 collective-permute-start.23
  57.6 1.8 %collective-permute-done.27 = bf16[16,2048]{1,0:T(8,128)(2,1)S(1)} collective-permute-done((bf16[16,2048]{1,0:T(8,128)(2,1)S(1)}, bf16[16,2048]{1,0:T(8,128)(2,1)S(1)}, u32[]{:S(2)}, u32[]{:S(2)}) %collective-permute-start.27) | collective-permute-done | bytes 65568 | tf_op jit(solution)/shard_map/ppermute | solution.py:49
  59.4 2.4 %collective-permute-done.26 = bf16[16,2048]{1,0:T(8,128)(2,1)S(1)} collective-permute-done((bf16[16,2048]{1,0:T(8,128)(2,1)S(1)}, bf16[16,2048]{1,0:T(8,128)(2,1)S(1)}, u32[]{:S(2)}, u32[]{:S(2)}) %collective-permute-start.26) | collective-permute-done | bytes 65568 | tf_op jit(solution)/shard_map/ppermute | solution.py:49
  61.9 2.7 %collective-permute-start.30 = (bf16[16,2048]{1,0:T(8,128)(2,1)S(1)}, bf16[16,2048]{1,0:T(8,128)(2,1)S(1)}, u32[]{:S(2)}, u32[]{:S(2)}) collective-permute-start(bf16[16,2048]{1,0:T(8,128)(2,1)S(1)} %fusion.10.refs_8_.refs_0_), channel_id=1, source_target_pairs={{0,6},{1,7},{2,4},{3,5},{4,2},{5,3},{6,0},{7,1},{8,14},{9,15},{10,... | collective-permute-start | bytes 196616 | tf_op jit(solution)/shard_map/ppermute | solution.py:49
  64.6 1.7 %collective-permute-start.28 = (bf16[16,2048]{1,0:T(8,128)(2,1)S(1)}, bf16[16,2048]{1,0:T(8,128)(2,1)S(1)}, u32[]{:S(2)}, u32[]{:S(2)}) collective-permute-start(bf16[16,2048]{1,0:T(8,128)(2,1)S(1)} %fusion.10.refs_8_.refs_0_), channel_id=1, source_target_pairs={{0,2},{1,3},{2,0},{3,1},{4,6},{5,7},{6,4},{7,5},{8,10},{9,11},{10,... | collective-permute-start | bytes 196616 | tf_op jit(solution)/shard_map/ppermute | solution.py:49
  66.4 1.5 %gate_up_home.1.home = bf16[128,1024]{1,0:T(8,128)(2,1)S(1)} custom-call(bf16[16,2048]{1,0:T(8,128)(2,1)S(1)} %add_convert_fusion.8.refs_0_, bf16[16,2048]{1,0:T(8,128)(2,1)S(1)} %collective-permute-done.17.refs_1_, bf16[16,2048]{1,0:T(8,128)(2,1)S(1)} %collective-permute-done.18.refs_2_, bf16[16,2048]{1,0:T(8,128)(2,1)S(1)} %collective-permute-done.19.refs_3_, ...), custom_call_target="tpu_custom_call" | custom-call | flops 2000000000 | bytes 8388608 | tf_op jit(solution)/shard_map/gate_up_home/pallas_call | solution.py:541
  67.9 0.5 collective-permute-done.30.refs_14_.refs_6_
  68.4 2.0 %collective-permute-done.29.refs_12_.refs_4_ = bf16[16,2048]{1,0:T(8,128)(2,1)S(1)} collective-permute-done((bf16[16,2048]{1,0:T(8,128)(2,1)S(1)}, bf16[16,2048]{1,0:T(8,128)(2,1)S(1)}, u32[]{:S(2)}, u32[]{:S(2)}) %collective-permute-start.29) | collective-permute-done | bytes 65568 | tf_op jit(solution)/shard_map/ppermute | solution.py:49
  70.4 0.5 collective-permute-start.32
  71.0 0.5 collective-permute-start.34
  71.5 0.2 collective-permute-done.31.refs_9_.refs_1_
  71.7 0.2 collective-permute-done.32.refs_11_.refs_3_
  71.9 0.4 collective-permute-done.33.refs_13_.refs_5_
  72.4 1.5 %gate_up_far.1.far = bf16[128,1024]{1,0:T(8,128)(2,1)S(1)} custom-call(bf16[16,2048]{1,0:T(8,128)(2,1)S(1)} %fusion.10.refs_8_.refs_0_, bf16[16,2048]{1,0:T(8,128)(2,1)S(1)} %collective-permute-done.31.refs_9_.refs_1_, bf16[16,2048]{1,0:T(8,128)(2,1)S(1)} %collective-permute-done.28.refs_10_.refs_2_, ...), custom_call_target="tpu_custom_call" | custom-call | flops 2000000000 | bytes 8388608 | tf_op jit(solution)/shard_map/gate_up_far/pallas_call | solution.py:541
  73.8 0.9 %down_first.1 = (bf16[128,1024]{1,0:T(8,128)(2,1)S(1)}, bf16[2,32,2048]{2,1,0:T(8,128)(2,1)S(1)}, bf16[2,32,2048]{2,1,0:T(8,128)(2,1)S(1)}) custom-call(bf16[128,1024]{1,0:T(8,128)(2,1)S(1)} %gate_up_home.1.home, bf16[128,1024]{1,0:T(8,128)(2,1)S(1)} %gate_up_far.1.far, s32[1,256]{1,0:T(1,128)S(1)} %get-tuple-element.86.order, bf16[1024,2048]{1,0:T(8,128)(2,1)S(1)} %copy-done), custom_call_target="tpu_custom_call" | custom-call | tf_op jit(solution)/shard_map/down_first/pallas_call | solution.py:572
  74.8 0.4 collective-permute-start.35
  75.2 0.7 down_second.1
  75.9 0.2 collective-permute-start.38
  76.1 0.2 collective-permute-done.35
  76.4 1.4 %collective-permute-start.36 = (bf16[32,2048]{1,0:T(8,128)(2,1)S(1)}, bf16[32,2048]{1,0:T(8,128)(2,1)S(1)}, u32[]{:S(2)}, u32[]{:S(2)}) collective-permute-start(bf16[32,2048]{1,0:T(8,128)(2,1)S(1)} %get-tuple-element.144), channel_id=1, source_target_pairs={{0,4},{1,5},{2,6},{3,7},{4,0},{5,1},{6,2},{7,3},{8,12},{9,13},{10,... | collective-permute-start | bytes 393224 | tf_op jit(solution)/shard_map/ppermute | solution.py:49
  77.9 1.7 %collective-permute-start.37 = (bf16[32,2048]{1,0:T(8,128)(2,1)S(1)}, bf16[32,2048]{1,0:T(8,128)(2,1)S(1)}, u32[]{:S(2)}, u32[]{:S(2)}) collective-permute-start(bf16[32,2048]{1,0:T(8,128)(2,1)S(1)} %get-tuple-element.145), channel_id=1, source_target_pairs={{0,6},{1,7},{2,4},{3,5},{4,2},{5,3},{6,0},{7,1},{8,14},{9,15},{10,... | collective-permute-start | bytes 393224 | tf_op jit(solution)/shard_map/ppermute | solution.py:49
  79.6 0.4 collective-permute-start.39
  80.1 5.5 %cache_update.1 = bf16[2,4096,256]{2,1,0:T(8,128)(2,1)} custom-call(s32[1,128]{1,0:T(1,128)S(1)} %get-tuple-element.139.home_rows, s32[1,144]{1,0:T(1,128)S(1)} %get-tuple-element.140.far_rows, bf16[128,768]{1,0:T(8,128)(2,1)S(1)} %get-tuple-element.98.packed.home, bf16[48,768]{1,0:T(8,128)(2,1)S(1)} %collective-permute-done.7.refs_0_, ...), custom_call_target="tpu_custom_call" | custom-call | flops 2000000000 | bytes 8388608 | tf_op jit(solution)/shard_map/cache_update/pallas_call | solution.py:524
  85.6 0.7 copy.14
  86.3 0.5 own_rows.1
  86.8 2.3 %collective-permute-done.36 = bf16[32,2048]{1,0:T(8,128)(2,1)S(1)} collective-permute-done((bf16[32,2048]{1,0:T(8,128)(2,1)S(1)}, bf16[32,2048]{1,0:T(8,128)(2,1)S(1)}, u32[]{:S(2)}, u32[]{:S(2)}) %collective-permute-start.36) | collective-permute-done | bytes 131104 | tf_op jit(solution)/shard_map/ppermute | solution.py:49
  89.1 1.1 %collective-permute-done.39 = bf16[32,2048]{1,0:T(8,128)(2,1)S(1)} collective-permute-done((bf16[32,2048]{1,0:T(8,128)(2,1)S(1)}, bf16[32,2048]{1,0:T(8,128)(2,1)S(1)}, u32[]{:S(2)}, u32[]{:S(2)}) %collective-permute-start.39) | collective-permute-done | bytes 131104 | tf_op jit(solution)/shard_map/ppermute | solution.py:49
  90.2 0.8 fusion.2
  (63 shorter events, 0.9 us)
Async XLA Ops:
  0.6 12.3 %collective-permute-start.1 = (bf16[32,2048]{1,0:T(8,128)(2,1)}, bf16[32,2048]{1,0:T(8,128)(2,1)S(1)}, u32[]{:S(2)}, u32[]{:S(2)}) collective-permute-start(bf16[32,2048]{1,0:T(8,128)(2,1)} %refs_0_), channel_id=1, source_target_pairs={{0,4},{1,5},{2,6},{3,7},{4,0},{5,1},{6,2},{7,3},{8,12},{9,13},{10,... | collective-permute-start | bytes 393224 | tf_op jit(solution)/shard_map/ppermute | solution.py:49
  4.7 8.2 %collective-permute-start = (bf16[32,2048]{1,0:T(8,128)(2,1)}, bf16[32,2048]{1,0:T(8,128)(2,1)S(1)}, u32[]{:S(2)}, u32[]{:S(2)}) collective-permute-start(bf16[32,2048]{1,0:T(8,128)(2,1)} %refs_0_), channel_id=1, source_target_pairs={{0,2},{1,3},{2,0},{3,1},{4,6},{5,7},{6,4},{7,5},{8,10},{9,11},{10,... | collective-permute-start | bytes 393224 | tf_op jit(solution)/shard_map/ppermute | solution.py:49
  6.3 9.0 %collective-permute-start.2 = (bf16[32,2048]{1,0:T(8,128)(2,1)}, bf16[32,2048]{1,0:T(8,128)(2,1)S(1)}, u32[]{:S(2)}, u32[]{:S(2)}) collective-permute-start(bf16[32,2048]{1,0:T(8,128)(2,1)} %refs_0_), channel_id=1, source_target_pairs={{0,6},{1,7},{2,4},{3,5},{4,2},{5,3},{6,0},{7,1},{8,14},{9,15},{10,... | collective-permute-start | bytes 393224 | tf_op jit(solution)/shard_map/ppermute | solution.py:49
  6.3 0.7 copy-start.5
  7.0 0.7 copy-start.6
  7.7 0.7 copy-start.7
  8.4 6.9 %copy-start.4 = (bf16[32,2048]{1,0:T(8,128)(2,1)S(1)}, bf16[32,2048]{1,0:T(8,128)(2,1)}, u32[]{:S(2)}) copy-start(bf16[32,2048]{1,0:T(8,128)(2,1)} %refs_0_) | copy-start | bytes 393220
  8.4 7.9 %copy-start.8 = (bf16[2048]{0:T(1024)(128)(2,1)S(1)}, bf16[2048]{0:T(1024)(128)(2,1)}, u32[]{:S(2)}) copy-start(bf16[2048]{0:T(1024)(128)(2,1)} %param.12) | copy-start | bytes 12292
  8.4 8.9 %copy-start.2 = (bf16[3,2048,256]{2,1,0:T(8,128)(2,1)S(1)}, bf16[3,2048,256]{2,1,0:T(8,128)(2,1)}, u32[]{:S(2)}) copy-start(bf16[3,2048,256]{2,1,0:T(8,128)(2,1)} %refs_9_.3) | copy-start | bytes 9437188
  8.4 14.8 %copy-start.3 = (bf16[256,2048]{1,0:T(8,128)(2,1)S(1)}, bf16[256,2048]{1,0:T(8,128)(2,1)}, u32[]{:S(2)}) copy-start(bf16[256,2048]{1,0:T(8,128)(2,1)} %refs_3_.2) | copy-start | bytes 3145732
  10.5 12.7 %copy-start.1 = (bf16[2,4096,256]{2,1,0:T(8,128)(2,1)S(1)}, bf16[2,4096,256]{2,1,0:T(8,128)(2,1)}, u32[]{:S(2)}) copy-start(bf16[2,4096,256]{2,1,0:T(8,128)(2,1)} %refs_3_.3) | copy-start | bytes 12582916
  15.3 1.3 %collective-permute-start.3 = (bf16[32,2048]{1,0:T(8,128)(2,1)S(1)}, bf16[32,2048]{1,0:T(8,128)(2,1)S(1)}, u32[]{:S(2)}, u32[]{:S(2)}) collective-permute-start(bf16[32,2048]{1,0:T(8,128)(2,1)S(1)} %copy-done.4), channel_id=1, source_target_pairs={{0,1},{1,0},{2,3},{3,2},{4,5},{5,4},{6,7},{7,6},{8,9},{9,8},{10,11... | collective-permute-start | bytes 393224 | tf_op jit(solution)/shard_map/ppermute | solution.py:49
  15.3 1.5 %collective-permute-start.4 = (bf16[32,2048]{1,0:T(8,128)(2,1)S(1)}, bf16[32,2048]{1,0:T(8,128)(2,1)S(1)}, u32[]{:S(2)}, u32[]{:S(2)}) collective-permute-start(bf16[32,2048]{1,0:T(8,128)(2,1)S(1)} %collective-permute-done.refs_2_), channel_id=1, source_target_pairs={{0,1},{1,0},{2,3},{3,2},{4,5},{5,4},{6,7},{7,6},{8,9},{9,8},{10,11... | collective-permute-start | bytes 393224 | tf_op jit(solution)/shard_map/ppermute | solution.py:49
  15.8 1.3 %collective-permute-start.5 = (bf16[32,2048]{1,0:T(8,128)(2,1)S(1)}, bf16[32,2048]{1,0:T(8,128)(2,1)S(1)}, u32[]{:S(2)}, u32[]{:S(2)}) collective-permute-start(bf16[32,2048]{1,0:T(8,128)(2,1)S(1)} %collective-permute-done.1.refs_4_), channel_id=1, source_target_pairs={{0,1},{1,0},{2,3},{3,2},{4,5},{5,4},{6,7},{7,6},{8,9},{9,8},{10,11... | collective-permute-start | bytes 393224 | tf_op jit(solution)/shard_map/ppermute | solution.py:49
  15.8 1.5 %collective-permute-start.6 = (bf16[32,2048]{1,0:T(8,128)(2,1)S(1)}, bf16[32,2048]{1,0:T(8,128)(2,1)S(1)}, u32[]{:S(2)}, u32[]{:S(2)}) collective-permute-start(bf16[32,2048]{1,0:T(8,128)(2,1)S(1)} %collective-permute-done.2.refs_6_), channel_id=1, source_target_pairs={{0,1},{1,0},{2,3},{3,2},{4,5},{5,4},{6,7},{7,6},{8,9},{9,8},{10,11... | collective-permute-start | bytes 393224 | tf_op jit(solution)/shard_map/ppermute | solution.py:49
  19.6 7.9 %collective-permute-start.7 = (bf16[48,768]{1,0:T(8,128)(2,1)S(1)}, bf16[48,768]{1,0:T(8,128)(2,1)S(1)}, u32[]{:S(2)}, u32[]{:S(2)}) collective-permute-start(bf16[48,768]{1,0:T(8,128)(2,1)S(1)} %get-tuple-element.103), channel_id=1, source_target_pairs={{0,8},{8,0},{16,24},{24,16},{1,9},{9,1},{17,25},{25,17},{2,10},{10... | collective-permute-start | bytes 221192 | tf_op jit(solution)/shard_map/ppermute | solution.py:49
  21.1 6.4 %collective-permute-start.8 = (bf16[48,768]{1,0:T(8,128)(2,1)S(1)}, bf16[48,768]{1,0:T(8,128)(2,1)S(1)}, u32[]{:S(2)}, u32[]{:S(2)}) collective-permute-start(bf16[48,768]{1,0:T(8,128)(2,1)S(1)} %get-tuple-element.104), channel_id=1, source_target_pairs={{0,16},{8,24},{16,0},{24,8},{1,17},{9,25},{17,1},{25,9},{2,18},{10... | collective-permute-start | bytes 221192 | tf_op jit(solution)/shard_map/ppermute | solution.py:49
  22.7 5.3 %collective-permute-start.9 = (bf16[48,768]{1,0:T(8,128)(2,1)S(1)}, bf16[48,768]{1,0:T(8,128)(2,1)S(1)}, u32[]{:S(2)}, u32[]{:S(2)}) collective-permute-start(bf16[48,768]{1,0:T(8,128)(2,1)S(1)} %get-tuple-element.105), channel_id=1, source_target_pairs={{0,24},{8,16},{16,8},{24,0},{1,25},{9,17},{17,9},{25,1},{2,26},{10... | collective-permute-start | bytes 221192 | tf_op jit(solution)/shard_map/ppermute | solution.py:49
  23.1 43.2 %slice-start = ((s8[8388608]{0:T(1024)(128)(4,1)}), s8[4194304]{0:T(1024)(128)(4,1)S(1)}, s32[]{:S(2)}) async-start(s8[8388608]{0:T(1024)(128)(4,1)} %bitcast.34), calls=%async_computation | async-start | bytes 8388608
  27.9 5.7 %collective-permute-start.13 = (bf16[4,16,2048]{2,1,0:T(8,128)(2,1)S(1)}, bf16[4,16,2048]{2,1,0:T(8,128)(2,1)S(1)}, u32[]{:S(2)}, u32[]{:S(2)}) collective-permute-start(bf16[4,16,2048]{2,1,0:T(8,128)(2,1)S(1)} %get-tuple-element.116), channel_id=1, source_target_pairs={{0,1},{1,0},{2,3},{3,2},{4,5},{5,4},{6,7},{7,6},{8,9},{9,8},{10,11... | collective-permute-start | bytes 786440 | tf_op jit(solution)/shard_map/ppermute | solution.py:49
  27.9 29.0 %copy-start.9 = (bf16[2048]{0:T(1024)(128)(2,1)S(1)}, bf16[2048]{0:T(1024)(128)(2,1)}, u32[]{:S(2)}) copy-start(bf16[2048]{0:T(1024)(128)(2,1)} %param.13) | copy-start | bytes 12292
  27.9 38.5 %slice-start.1 = ((s8[8388608]{0:T(1024)(128)(4,1)}), s8[4194304]{0:T(1024)(128)(4,1)S(1)}, s32[]{:S(2)}) async-start(s8[8388608]{0:T(1024)(128)(4,1)} %bitcast.34), calls=%async_computation.1 | async-start | bytes 8388608
  31.1 9.6 %collective-permute-start.10 = (bf16[48,384]{1,0:T(8,128)(2,1)S(1)}, bf16[48,384]{1,0:T(8,128)(2,1)S(1)}, u32[]{:S(2)}, u32[]{:S(2)}) collective-permute-start(bf16[48,384]{1,0:T(8,128)(2,1)S(1)} %get-tuple-element.112), channel_id=1, source_target_pairs={{0,8},{8,0},{16,24},{24,16},{1,9},{9,1},{17,25},{25,17},{2,10},{10... | collective-permute-start | bytes 110600 | tf_op jit(solution)/shard_map/ppermute | solution.py:49
  33.7 11.9 %collective-permute-start.16 = (bf16[16,2048]{1,0:T(8,128)(2,1)S(1)}, bf16[16,2048]{1,0:T(8,128)(2,1)S(1)}, u32[]{:S(2)}, u32[]{:S(2)}) collective-permute-start(bf16[16,2048]{1,0:T(8,128)(2,1)S(1)} %get-tuple-element.149), channel_id=1, source_target_pairs={{0,6},{1,7},{2,4},{3,5},{4,2},{5,3},{6,0},{7,1},{8,14},{9,15},{10,... | collective-permute-start | bytes 196616 | tf_op jit(solution)/shard_map/ppermute | solution.py:49
  36.2 9.4 %collective-permute-start.15 = (bf16[16,2048]{1,0:T(8,128)(2,1)S(1)}, bf16[16,2048]{1,0:T(8,128)(2,1)S(1)}, u32[]{:S(2)}, u32[]{:S(2)}) collective-permute-start(bf16[16,2048]{1,0:T(8,128)(2,1)S(1)} %get-tuple-element.150), channel_id=1, source_target_pairs={{0,4},{1,5},{2,6},{3,7},{4,0},{5,1},{6,2},{7,3},{8,12},{9,13},{10,... | collective-permute-start | bytes 196616 | tf_op jit(solution)/shard_map/ppermute | solution.py:49
  38.0 7.5 %collective-permute-start.14 = (bf16[16,2048]{1,0:T(8,128)(2,1)S(1)}, bf16[16,2048]{1,0:T(8,128)(2,1)S(1)}, u32[]{:S(2)}, u32[]{:S(2)}) collective-permute-start(bf16[16,2048]{1,0:T(8,128)(2,1)S(1)} %get-tuple-element.151), channel_id=1, source_target_pairs={{0,2},{1,3},{2,0},{3,1},{4,6},{5,7},{6,4},{7,5},{8,10},{9,11},{10,... | collective-permute-start | bytes 196616 | tf_op jit(solution)/shard_map/ppermute | solution.py:49
  38.5 4.1 %collective-permute-start.11 = (bf16[48,384]{1,0:T(8,128)(2,1)S(1)}, bf16[48,384]{1,0:T(8,128)(2,1)S(1)}, u32[]{:S(2)}, u32[]{:S(2)}) collective-permute-start(bf16[48,384]{1,0:T(8,128)(2,1)S(1)} %get-tuple-element.113), channel_id=1, source_target_pairs={{0,16},{8,24},{16,0},{24,8},{1,17},{9,25},{17,1},{25,9},{2,18},{10... | collective-permute-start | bytes 110600 | tf_op jit(solution)/shard_map/ppermute | solution.py:49
  40.7 4.9 %collective-permute-start.12 = (bf16[48,384]{1,0:T(8,128)(2,1)S(1)}, bf16[48,384]{1,0:T(8,128)(2,1)S(1)}, u32[]{:S(2)}, u32[]{:S(2)}) collective-permute-start(bf16[48,384]{1,0:T(8,128)(2,1)S(1)} %get-tuple-element.114), channel_id=1, source_target_pairs={{0,24},{8,16},{16,8},{24,0},{1,25},{9,17},{17,9},{25,1},{2,26},{10... | collective-permute-start | bytes 110600 | tf_op jit(solution)/shard_map/ppermute | solution.py:49
  46.2 4.6 %collective-permute-start.24 = (bf16[4,16,2048]{2,1,0:T(8,128)(2,1)S(1)}, bf16[4,16,2048]{2,1,0:T(8,128)(2,1)S(1)}, u32[]{:S(2)}, u32[]{:S(2)}) collective-permute-start(bf16[4,16,2048]{2,1,0:T(8,128)(2,1)S(1)} %get-tuple-element.127), channel_id=1, source_target_pairs={{0,1},{1,0},{2,3},{3,2},{4,5},{5,4},{6,7},{7,6},{8,9},{9,8},{10,11... | collective-permute-start | bytes 786440 | tf_op jit(solution)/shard_map/ppermute | solution.py:49
  46.3 8.1 %collective-permute-start.22 = (bf16[16,2048]{1,0:T(8,128)(2,1)S(1)}, bf16[16,2048]{1,0:T(8,128)(2,1)S(1)}, u32[]{:S(2)}, u32[]{:S(2)}) collective-permute-start(bf16[16,2048]{1,0:T(8,128)(2,1)S(1)} %add_convert_fusion.8.refs_0_), channel_id=1, source_target_pairs={{0,6},{1,7},{2,4},{3,5},{4,2},{5,3},{6,0},{7,1},{8,14},{9,15},{10,... | collective-permute-start | bytes 196616 | tf_op jit(solution)/shard_map/ppermute | solution.py:49
  48.7 8.2 %collective-permute-start.20 = (bf16[16,2048]{1,0:T(8,128)(2,1)S(1)}, bf16[16,2048]{1,0:T(8,128)(2,1)S(1)}, u32[]{:S(2)}, u32[]{:S(2)}) collective-permute-start(bf16[16,2048]{1,0:T(8,128)(2,1)S(1)} %add_convert_fusion.8.refs_0_), channel_id=1, source_target_pairs={{0,4},{1,5},{2,6},{3,7},{4,0},{5,1},{6,2},{7,3},{8,12},{9,13},{10,... | collective-permute-start | bytes 196616 | tf_op jit(solution)/shard_map/ppermute | solution.py:49
  49.4 7.7 %collective-permute-start.18 = (bf16[16,2048]{1,0:T(8,128)(2,1)S(1)}, bf16[16,2048]{1,0:T(8,128)(2,1)S(1)}, u32[]{:S(2)}, u32[]{:S(2)}) collective-permute-start(bf16[16,2048]{1,0:T(8,128)(2,1)S(1)} %add_convert_fusion.8.refs_0_), channel_id=1, source_target_pairs={{0,2},{1,3},{2,0},{3,1},{4,6},{5,7},{6,4},{7,5},{8,10},{9,11},{10,... | collective-permute-start | bytes 196616 | tf_op jit(solution)/shard_map/ppermute | solution.py:49
  50.8 6.7 %collective-permute-start.25 = (bf16[16,2048]{1,0:T(8,128)(2,1)S(1)}, bf16[16,2048]{1,0:T(8,128)(2,1)S(1)}, u32[]{:S(2)}, u32[]{:S(2)}) collective-permute-start(bf16[16,2048]{1,0:T(8,128)(2,1)S(1)} %get-tuple-element.146), channel_id=1, source_target_pairs={{0,2},{1,3},{2,0},{3,1},{4,6},{5,7},{6,4},{7,5},{8,10},{9,11},{10,... | collective-permute-start | bytes 196616 | tf_op jit(solution)/shard_map/ppermute | solution.py:49
  51.5 7.9 %collective-permute-start.27 = (bf16[16,2048]{1,0:T(8,128)(2,1)S(1)}, bf16[16,2048]{1,0:T(8,128)(2,1)S(1)}, u32[]{:S(2)}, u32[]{:S(2)}) collective-permute-start(bf16[16,2048]{1,0:T(8,128)(2,1)S(1)} %get-tuple-element.147), channel_id=1, source_target_pairs={{0,6},{1,7},{2,4},{3,5},{4,2},{5,3},{6,0},{7,1},{8,14},{9,15},{10,... | collective-permute-start | bytes 196616 | tf_op jit(solution)/shard_map/ppermute | solution.py:49
  54.4 7.5 %collective-permute-start.26 = (bf16[16,2048]{1,0:T(8,128)(2,1)S(1)}, bf16[16,2048]{1,0:T(8,128)(2,1)S(1)}, u32[]{:S(2)}, u32[]{:S(2)}) collective-permute-start(bf16[16,2048]{1,0:T(8,128)(2,1)S(1)} %get-tuple-element.148), channel_id=1, source_target_pairs={{0,4},{1,5},{2,6},{3,7},{4,0},{5,1},{6,2},{7,3},{8,12},{9,13},{10,... | collective-permute-start | bytes 196616 | tf_op jit(solution)/shard_map/ppermute | solution.py:49
  57.0 7.7 %collective-permute-start.17 = (bf16[16,2048]{1,0:T(8,128)(2,1)S(1)}, bf16[16,2048]{1,0:T(8,128)(2,1)S(1)}, u32[]{:S(2)}, u32[]{:S(2)}) collective-permute-start(bf16[16,2048]{1,0:T(8,128)(2,1)S(1)} %add_convert_fusion.8.refs_0_), channel_id=1, source_target_pairs={{0,1},{1,0},{2,3},{3,2},{4,5},{5,4},{6,7},{7,6},{8,9},{9,8},{10,11... | collective-permute-start | bytes 196616 | tf_op jit(solution)/shard_map/ppermute | solution.py:49
  57.0 7.6 %collective-permute-start.23 = (bf16[16,2048]{1,0:T(8,128)(2,1)S(1)}, bf16[16,2048]{1,0:T(8,128)(2,1)S(1)}, u32[]{:S(2)}, u32[]{:S(2)}) collective-permute-start(bf16[16,2048]{1,0:T(8,128)(2,1)S(1)} %collective-permute-done.22.refs_6_), channel_id=1, source_target_pairs={{0,1},{1,0},{2,3},{3,2},{4,5},{5,4},{6,7},{7,6},{8,9},{9,8},{10,11... | collective-permute-start | bytes 196616 | tf_op jit(solution)/shard_map/ppermute | solution.py:49
  57.5 8.8 %collective-permute-start.21 = (bf16[16,2048]{1,0:T(8,128)(2,1)S(1)}, bf16[16,2048]{1,0:T(8,128)(2,1)S(1)}, u32[]{:S(2)}, u32[]{:S(2)}) collective-permute-start(bf16[16,2048]{1,0:T(8,128)(2,1)S(1)} %collective-permute-done.20.refs_4_), channel_id=1, source_target_pairs={{0,1},{1,0},{2,3},{3,2},{4,5},{5,4},{6,7},{7,6},{8,9},{9,8},{10,11... | collective-permute-start | bytes 196616 | tf_op jit(solution)/shard_map/ppermute | solution.py:49
  59.4 7.0 %collective-permute-start.19 = (bf16[16,2048]{1,0:T(8,128)(2,1)S(1)}, bf16[16,2048]{1,0:T(8,128)(2,1)S(1)}, u32[]{:S(2)}, u32[]{:S(2)}) collective-permute-start(bf16[16,2048]{1,0:T(8,128)(2,1)S(1)} %collective-permute-done.18.refs_2_), channel_id=1, source_target_pairs={{0,1},{1,0},{2,3},{3,2},{4,5},{5,4},{6,7},{7,6},{8,9},{9,8},{10,11... | collective-permute-start | bytes 196616 | tf_op jit(solution)/shard_map/ppermute | solution.py:49
  61.9 6.5 %collective-permute-start.30 = (bf16[16,2048]{1,0:T(8,128)(2,1)S(1)}, bf16[16,2048]{1,0:T(8,128)(2,1)S(1)}, u32[]{:S(2)}, u32[]{:S(2)}) collective-permute-start(bf16[16,2048]{1,0:T(8,128)(2,1)S(1)} %fusion.10.refs_8_.refs_0_), channel_id=1, source_target_pairs={{0,6},{1,7},{2,4},{3,5},{4,2},{5,3},{6,0},{7,1},{8,14},{9,15},{10,... | collective-permute-start | bytes 196616 | tf_op jit(solution)/shard_map/ppermute | solution.py:49
  64.6 5.8 %collective-permute-start.29 = (bf16[16,2048]{1,0:T(8,128)(2,1)S(1)}, bf16[16,2048]{1,0:T(8,128)(2,1)S(1)}, u32[]{:S(2)}, u32[]{:S(2)}) collective-permute-start(bf16[16,2048]{1,0:T(8,128)(2,1)S(1)} %fusion.10.refs_8_.refs_0_), channel_id=1, source_target_pairs={{0,4},{1,5},{2,6},{3,7},{4,0},{5,1},{6,2},{7,3},{8,12},{9,13},{10,... | collective-permute-start | bytes 196616 | tf_op jit(solution)/shard_map/ppermute | solution.py:49
  64.6 5.8 %collective-permute-start.28 = (bf16[16,2048]{1,0:T(8,128)(2,1)S(1)}, bf16[16,2048]{1,0:T(8,128)(2,1)S(1)}, u32[]{:S(2)}, u32[]{:S(2)}) collective-permute-start(bf16[16,2048]{1,0:T(8,128)(2,1)S(1)} %fusion.10.refs_8_.refs_0_), channel_id=1, source_target_pairs={{0,2},{1,3},{2,0},{3,1},{4,6},{5,7},{6,4},{7,5},{8,10},{9,11},{10,... | collective-permute-start | bytes 196616 | tf_op jit(solution)/shard_map/ppermute | solution.py:49
  67.9 6.0 %copy-start = (bf16[1024,2048]{1,0:T(8,128)(2,1)S(1)}, bf16[1024,2048]{1,0:T(8,128)(2,1)}, u32[]{:S(2)}) copy-start(bf16[1024,2048]{1,0:T(8,128)(2,1)} %down.3) | copy-start | bytes 12582916
  70.4 1.3 %collective-permute-start.31 = (bf16[16,2048]{1,0:T(8,128)(2,1)S(1)}, bf16[16,2048]{1,0:T(8,128)(2,1)S(1)}, u32[]{:S(2)}, u32[]{:S(2)}) collective-permute-start(bf16[16,2048]{1,0:T(8,128)(2,1)S(1)} %fusion.10.refs_8_.refs_0_), channel_id=1, source_target_pairs={{0,1},{1,0},{2,3},{3,2},{4,5},{5,4},{6,7},{7,6},{8,9},{9,8},{10,11... | collective-permute-start | bytes 196616 | tf_op jit(solution)/shard_map/ppermute | solution.py:49
  70.4 1.4 %collective-permute-start.32 = (bf16[16,2048]{1,0:T(8,128)(2,1)S(1)}, bf16[16,2048]{1,0:T(8,128)(2,1)S(1)}, u32[]{:S(2)}, u32[]{:S(2)}) collective-permute-start(bf16[16,2048]{1,0:T(8,128)(2,1)S(1)} %collective-permute-done.28.refs_10_.refs_2_), channel_id=1, source_target_pairs={{0,1},{1,0},{2,3},{3,2},{4,5},{5,4},{6,7},{7,6},{8,9},{9,8},{10,11... | collective-permute-start | bytes 196616 | tf_op jit(solution)/shard_map/ppermute | solution.py:49
  71.0 1.3 %collective-permute-start.33 = (bf16[16,2048]{1,0:T(8,128)(2,1)S(1)}, bf16[16,2048]{1,0:T(8,128)(2,1)S(1)}, u32[]{:S(2)}, u32[]{:S(2)}) collective-permute-start(bf16[16,2048]{1,0:T(8,128)(2,1)S(1)} %collective-permute-done.29.refs_12_.refs_4_), channel_id=1, source_target_pairs={{0,1},{1,0},{2,3},{3,2},{4,5},{5,4},{6,7},{7,6},{8,9},{9,8},{10,11... | collective-permute-start | bytes 196616 | tf_op jit(solution)/shard_map/ppermute | solution.py:49
  71.0 1.4 %collective-permute-start.34 = (bf16[16,2048]{1,0:T(8,128)(2,1)S(1)}, bf16[16,2048]{1,0:T(8,128)(2,1)S(1)}, u32[]{:S(2)}, u32[]{:S(2)}) collective-permute-start(bf16[16,2048]{1,0:T(8,128)(2,1)S(1)} %collective-permute-done.30.refs_14_.refs_6_), channel_id=1, source_target_pairs={{0,1},{1,0},{2,3},{3,2},{4,5},{5,4},{6,7},{7,6},{8,9},{9,8},{10,11... | collective-permute-start | bytes 196616 | tf_op jit(solution)/shard_map/ppermute | solution.py:49
  74.8 1.6 %collective-permute-start.35 = (bf16[2,32,2048]{2,1,0:T(8,128)(2,1)S(1)}, bf16[2,32,2048]{2,1,0:T(8,128)(2,1)S(1)}, u32[]{:S(2)}, u32[]{:S(2)}) collective-permute-start(bf16[2,32,2048]{2,1,0:T(8,128)(2,1)S(1)} %get-tuple-element.134), channel_id=1, source_target_pairs={{0,1},{1,0},{2,3},{3,2},{4,5},{5,4},{6,7},{7,6},{8,9},{9,8},{10,11... | collective-permute-start | bytes 786440 | tf_op jit(solution)/shard_map/ppermute | solution.py:49
  75.9 3.7 %collective-permute-start.38 = (bf16[2,32,2048]{2,1,0:T(8,128)(2,1)S(1)}, bf16[2,32,2048]{2,1,0:T(8,128)(2,1)S(1)}, u32[]{:S(2)}, u32[]{:S(2)}) collective-permute-start(bf16[2,32,2048]{2,1,0:T(8,128)(2,1)S(1)} %get-tuple-element.137), channel_id=1, source_target_pairs={{0,1},{1,0},{2,3},{3,2},{4,5},{5,4},{6,7},{7,6},{8,9},{9,8},{10,11... | collective-permute-start | bytes 786440 | tf_op jit(solution)/shard_map/ppermute | solution.py:49
  76.4 12.6 %collective-permute-start.36 = (bf16[32,2048]{1,0:T(8,128)(2,1)S(1)}, bf16[32,2048]{1,0:T(8,128)(2,1)S(1)}, u32[]{:S(2)}, u32[]{:S(2)}) collective-permute-start(bf16[32,2048]{1,0:T(8,128)(2,1)S(1)} %get-tuple-element.144), channel_id=1, source_target_pairs={{0,4},{1,5},{2,6},{3,7},{4,0},{5,1},{6,2},{7,3},{8,12},{9,13},{10,... | collective-permute-start | bytes 393224 | tf_op jit(solution)/shard_map/ppermute | solution.py:49
  77.9 11.2 %collective-permute-start.37 = (bf16[32,2048]{1,0:T(8,128)(2,1)S(1)}, bf16[32,2048]{1,0:T(8,128)(2,1)S(1)}, u32[]{:S(2)}, u32[]{:S(2)}) collective-permute-start(bf16[32,2048]{1,0:T(8,128)(2,1)S(1)} %get-tuple-element.145), channel_id=1, source_target_pairs={{0,6},{1,7},{2,4},{3,5},{4,2},{5,3},{6,0},{7,1},{8,14},{9,15},{10,... | collective-permute-start | bytes 393224 | tf_op jit(solution)/shard_map/ppermute | solution.py:49
  79.6 10.6 %collective-permute-start.39 = (bf16[32,2048]{1,0:T(8,128)(2,1)S(1)}, bf16[32,2048]{1,0:T(8,128)(2,1)S(1)}, u32[]{:S(2)}, u32[]{:S(2)}) collective-permute-start(bf16[32,2048]{1,0:T(8,128)(2,1)S(1)} %fusion.6), channel_id=1, source_target_pairs={{0,2},{1,3},{2,0},{3,1},{4,6},{5,7},{6,4},{7,5},{8,10},{9,11},{10,... | collective-permute-start | bytes 393224 | tf_op jit(solution)/shard_map/ppermute | solution.py:49
